TPU v7x, 256 devices: a whole 4x4x8 slice. The times are simulated.
256 devices in a mesh: wide: 64 (over y, z, core), narrow: 4 (over x).
Axes of the slice: x: 4, y: 4, z: 8, core: 2. Of those that a mesh axis runs over, the one named last changes fastest.
Arguments:
- items: bfloat16 [131072, 256], P(('wide', 'narrow')), may hold values from -6 to 6
- tile1_values: bfloat16 [24576, 128, 128], P(('wide', 'narrow')), may hold values from -0.109375 to 0.109375
- tile1_source: int32 [24576], P(('wide', 'narrow')), may hold values from 0 to 3
- tile1_owner: int32 [24576, 1], P(('wide', 'narrow')), may hold values from 0 to 63; in each aligned block of 96 rows (0 to 95, 96 to 191, ...) at most 2 rows name the same one
- tile1_slot: int32 [24576], P(('wide', 'narrow')), may hold values from 0 to 3
- tile2_values: bfloat16 [24576, 128, 128], P(('wide', 'narrow')), may hold values from -0.109375 to 0.109375
- tile2_source: int32 [24576], P(('wide', 'narrow')), may hold values from 0 to 3
- tile2_owner: int32 [24576, 1], P(('wide', 'narrow')), may hold values from 0 to 63; in each aligned block of 96 rows (0 to 95, 96 to 191, ...) at most 2 rows name the same one
- tile2_slot: int32 [24576], P(('wide', 'narrow')), may hold values from 0 to 15
- weight: bfloat16 [256, 256], replicated, may hold values from -0.375 to 0.375
- bundle_degree: int32 [131072], P(('wide', 'narrow')), may hold values from 1 to 4
- user_degree: int32 [131072], P('wide'), may hold values from 1 to 4
- cotangent: bfloat16 [131072, 256], P('wide'), may hold values from -6 to 6
Outputs:
- user_out: bfloat16 [131072, 256], P('wide')
- grad_weight: float32 [256, 256], replicated
- grad_bundle: bfloat16 [131072, 256], P(('wide', 'narrow'))
Inputs may be any that keep to these rules, and one draw needn't show every extreme that they name: `tile1_owner`: among the 96 tiles of one device, at most 2 name the same owner, a bound that some block reaches. `tile2_owner`: among the 96 tiles of one device, at most 2 name the same owner, a bound that some block reaches.
All inputs are finite; a program needn't handle non-finite values.
Results may differ from a plain program's by a relative error of at most 0.0073.
Values may be sent and summed in bfloat16 or wider, within the bound.
No kernel may reach another device: no remote copies, remote signals or barrier semaphores. Data moves between devices by JAX's collectives and lax.ppermute only.
A program may use at most 128 MiB of HBM per device.

v0:
```python
import jax
import jax.numpy as jnp
from jax import lax
from jax.sharding import PartitionSpec as P

F = 256
TILE = 128
CAP = 2


def placing(owner_col, width):
    owner = owner_col[:, 0]
    table = (owner[:, None] == jnp.arange(width, dtype=jnp.int32)[None, :]).astype(jnp.int32)
    rank = jnp.sum(jnp.cumsum(table, axis=0) * table, axis=1) - 1
    return owner * CAP + rank


def bucketed(terms, slots, where, width):
    buffer = jnp.zeros((width * CAP, TILE, F), jnp.bfloat16).at[where].set(terms)
    labels = jnp.full((width * CAP,), -1, jnp.int32).at[where].set(slots)
    return (buffer.reshape(width, CAP, TILE, F), labels.reshape(width, CAP))


def collect(received, labels, count):
    flat = received.reshape(-1, TILE * F)
    table = (labels.reshape(-1)[None, :] == jnp.arange(count, dtype=jnp.int32)[:, None]).astype(
        jnp.bfloat16
    )
    return jnp.dot(table, flat, preferred_element_type=jnp.float32).reshape(count * TILE, F)


def local(
    items,
    tile1_values,
    tile1_source,
    tile1_owner,
    tile1_slot,
    tile2_values,
    tile2_source,
    tile2_owner,
    tile2_slot,
    weight,
    bundle_degree,
    user_degree,
    cotangent,
):
    width = lax.axis_size("wide")
    bb_count = bundle_degree.shape[0] // TILE
    group = user_degree.shape[0] // TILE
    item_blocks = items.reshape(-1, TILE, F)
    term1 = jnp.einsum(
        "tij,tjf->tif", tile1_values, item_blocks[tile1_source], preferred_element_type=jnp.float32
    ).astype(jnp.bfloat16)
    where1 = placing(tile1_owner, width)
    buffer1, labels1 = bucketed(term1, tile1_slot, where1, width)
    got1, got_labels1 = (
        lax.all_to_all(buffer1, "wide", split_axis=0, concat_axis=0, tiled=True),
        lax.all_to_all(labels1, "wide", split_axis=0, concat_axis=0, tiled=True),
    )
    summed = collect(got1, got_labels1, bb_count)
    bundle_emb = (summed / bundle_degree[:, None].astype(jnp.float32)).astype(jnp.bfloat16)
    mixed = jnp.dot(bundle_emb, weight, preferred_element_type=jnp.float32)
    activated = jax.nn.silu(mixed).astype(jnp.bfloat16)
    bundle_blocks = activated.reshape(-1, TILE, F)
    term2 = jnp.einsum(
        "tij,tjf->tif",
        tile2_values,
        bundle_blocks[tile2_source],
        preferred_element_type=jnp.float32,
    ).astype(jnp.bfloat16)
    where2 = placing(tile2_owner, width)
    buffer2, labels2 = bucketed(term2, tile2_slot, where2, width)
    got2, got_labels2 = (
        lax.all_to_all(buffer2, "wide", split_axis=0, concat_axis=0, tiled=True),
        lax.all_to_all(labels2, "wide", split_axis=0, concat_axis=0, tiled=True),
    )
    partial_value = collect(got2, got_labels2, group)
    degrees = user_degree[:, None].astype(jnp.float32)
    gathered = lax.psum(partial_value, "narrow")
    user_out = (gathered / degrees).astype(jnp.bfloat16)
    scaled_grad = (cotangent.astype(jnp.float32) / degrees).astype(jnp.bfloat16)
    grad_blocks = scaled_grad.reshape(-1, TILE, F)
    wanted = lax.all_to_all(labels2, "wide", split_axis=0, concat_axis=0, tiled=True)
    present = (wanted >= 0).astype(jnp.bfloat16)
    reply = grad_blocks[jnp.maximum(wanted, 0)] * present[:, :, None, None]
    back = lax.all_to_all(reply, "wide", split_axis=0, concat_axis=0, tiled=True)
    needed = back.reshape(width * CAP, TILE, F)[where2]
    term3 = jnp.einsum(
        "tji,tjf->tif", tile2_values, needed, preferred_element_type=jnp.float32
    ).astype(jnp.bfloat16)
    table = (tile2_source[None, :] == jnp.arange(bb_count, dtype=jnp.int32)[:, None]).astype(
        jnp.bfloat16
    )
    grad_act = jnp.dot(
        table, term3.reshape(-1, TILE * F), preferred_element_type=jnp.float32
    ).reshape(bb_count * TILE, F)
    sigma = jax.nn.sigmoid(mixed)
    grad_mixed = (grad_act * sigma * (1.0 + mixed * (1.0 - sigma))).astype(jnp.bfloat16)
    local_grad = lax.dot_general(
        bundle_emb, grad_mixed, (((0,), (0,)), ((), ())), preferred_element_type=jnp.float32
    )
    grad_weight = lax.psum(local_grad, ("wide", "narrow"))
    grad_bundle = lax.dot_general(
        grad_mixed, weight, (((1,), (1,)), ((), ())), preferred_element_type=jnp.float32
    ).astype(jnp.bfloat16)
    return (user_out, grad_weight, grad_bundle)


def solution(mesh):
    in_specs = (
        P(("wide", "narrow"), None),
        P(("wide", "narrow"), None, None),
        P(("wide", "narrow")),
        P(("wide", "narrow"), None),
        P(("wide", "narrow")),
        P(("wide", "narrow"), None, None),
        P(("wide", "narrow")),
        P(("wide", "narrow"), None),
        P(("wide", "narrow")),
        P(),
        P(("wide", "narrow")),
        P("wide"),
        P("wide", None),
    )
    out_specs = (P("wide", None), P(), P(("wide", "narrow"), None))
    return jax.shard_map(local, mesh=mesh, in_specs=in_specs, out_specs=out_specs, check_vma=False)
```

profile of v0, /device:TPU:1, one launch (start us, length us, event | category | flops | bytes accessed | tf_op | source)
XLA Modules:
  0.0 1090.7 jit_solution(18026438690920707844)
XLA Ops:
  11.5 13.2 %all-to-all-start.1 = ((s32[64,1,2]{2,1,0:T(1,128)}), s32[64,1,2]{2,1,0:T(1,128)S(1)}, u32[]{:S(2)}, u32[]{:S(2)}) async-start(s32[64,1,2]{2,1,0:T(1,128)} %bitcast.7), calls=%async_computation.1 | async-start | bytes 65536 | tf_op jit(solution)/shard_map/all_to_all | solution.py:58
  29.5 6.9 gather_fusion
  36.3 10.3 all-to-all-start
  46.7 8.2 convert_bitcast_fusion.2
  54.9 8.7 copy.41
  67.8 17.7 %scatter_fusion = bf16[128,128,256]{2,1,0:T(8,128)(2,1)} fusion(bf16[128,128,256]{2,1,0:T(8,128)(2,1)} %broadcast.83.clone, s32[96]{0:T(128)S(1)} %fusion.10, bf16[96,128,256]{2,1,0:T(8,128)(2,1)} %copy.41), kind=kCustom, calls=%fused_computation.6 | custom fusion | bytes 18874752 | tf_op jit(solution)/shard_map/scatter | solution.py:19
  85.5 11.2 %all-to-all-start.2 = ((bf16[64,2,128,256]{3,2,1,0:T(8,128)(2,1)}), bf16[64,2,128,256]{3,2,1,0:T(8,128)(2,1)}, u32[]{:S(2)}, u32[]{:S(2)}) async-start(bf16[64,2,128,256]{3,2,1,0:T(8,128)(2,1)} %bitcast.65), calls=%async_computation.2 | async-start | bytes 16777216 | tf_op jit(solution)/shard_map/all_to_all | solution.py:57
  99.8 7.8 gather_fusion.2
  107.6 7.3 broadcast_multiply_fusion
  114.9 167.5 %all-to-all-done.2 = bf16[64,2,128,256]{3,2,1,0:T(8,128)(2,1)} async-done(((bf16[64,2,128,256]{3,2,1,0:T(8,128)(2,1)}), bf16[64,2,128,256]{3,2,1,0:T(8,128)(2,1)}, u32[]{:S(2)}, u32[]{:S(2)}) %all-to-all-start.2) | async-done | bytes 8388640 | tf_op jit(solution)/shard_map/all_to_all | solution.py:57
  282.4 6.1 all-to-all-start.4
  289.9 12.3 %copy.53 = bf16[16,8,128,256]{3,1,2,0:T(8,128)(2,1)} copy(bf16[16,8,128,256]{3,2,1,0:T(8,128)(2,1)} %bitcast.20) | data formatting | bytes 16777216
  311.7 162.5 %all-to-all-done.4 = bf16[64,2,128,256]{3,2,1,0:T(8,128)(2,1)} async-done(((bf16[64,2,128,256]{3,2,1,0:T(8,128)(2,1)}), bf16[64,2,128,256]{3,2,1,0:T(8,128)(2,1)}, u32[]{:S(2)}, u32[]{:S(2)}) %all-to-all-start.4) | async-done | bytes 8388640 | tf_op jit(solution)/shard_map/all_to_all | solution.py:86
  474.2 9.4 gather_fusion.3
  483.6 7.3 convert_bitcast_fusion
  490.9 9.2 copy.55
  515.0 7.3 convert_bitcast_fusion.1
  522.3 8.7 copy.43
  535.3 17.8 %scatter_fusion.1 = bf16[128,128,256]{2,1,0:T(8,128)(2,1)} fusion(bf16[128,128,256]{2,1,0:T(8,128)(2,1)} %broadcast.83, s32[96]{0:T(128)S(1)} %fusion.9, bf16[96,128,256]{2,1,0:T(8,128)(2,1)} %copy.43), kind=kCustom, calls=%fused_computation.7 | custom fusion | bytes 18874752 | tf_op jit(solution)/shard_map/scatter | solution.py:19
  553.1 6.0 all-to-all-start.3
  560.2 184.6 %all-to-all-done.3 = bf16[64,2,128,256]{3,2,1,0:T(8,128)(2,1)} async-done(((bf16[64,2,128,256]{3,2,1,0:T(8,128)(2,1)}), bf16[64,2,128,256]{3,2,1,0:T(8,128)(2,1)}, u32[]{:S(2)}, u32[]{:S(2)}) %all-to-all-start.3) | async-done | bytes 8388640 | tf_op jit(solution)/shard_map/all_to_all | solution.py:74
  744.9 12.3 %copy.54 = bf16[16,8,128,256]{3,1,2,0:T(8,128)(2,1)} copy(bf16[16,8,128,256]{3,2,1,0:T(8,128)(2,1)} %bitcast.23) | data formatting | bytes 16777216
  769.8 56.6 %all-reduce.3.cloned.1.call-done = f32[2048,256]{1,0:T(8,128)} async-done(((f32[2048,256]{1,0:T(8,128)}), f32[2048,256]{1,0:T(8,128)}) %all-reduce.3.cloned.1.call-update) | async-done | bytes 2097168 | tf_op jit(solution)/shard_map/psum | solution.py:79
  829.3 252.6 %all-reduce.5.cloned.1.call-done = f32[256,256]{1,0:T(8,128)} async-done(((f32[256,256]{1,0:T(8,128)}), f32[256,256]{1,0:T(8,128)}) %all-reduce.5.cloned.1.call-update) | async-done | bytes 262160 | tf_op jit(solution)/shard_map/psum | solution.py:102
  (65 shorter events, 64.6 us)
Async XLA Ops:
  7.2 476.5 %copy-start = (bf16[96,128,128]{2,1,0:T(8,128)(2,1)S(1)}, bf16[96,128,128]{2,1,0:T(8,128)(2,1)}, u32[]{:S(2)}) copy-start(bf16[96,128,128]{2,1,0:T(8,128)(2,1)} %param.18) | copy-start | bytes 9437188
  11.5 24.9 %all-to-all-start.1 = ((s32[64,1,2]{2,1,0:T(1,128)}), s32[64,1,2]{2,1,0:T(1,128)S(1)}, u32[]{:S(2)}, u32[]{:S(2)}) async-start(s32[64,1,2]{2,1,0:T(1,128)} %bitcast.7), calls=%async_computation.1 | async-start | bytes 65536 | tf_op jit(solution)/shard_map/all_to_all | solution.py:58
  36.3 49.2 %all-to-all-start = ((s32[64,1,2]{2,1,0:T(1,128)}), s32[64,1,2]{2,1,0:T(1,128)S(1)}, u32[]{:S(2)}, u32[]{:S(2)}) async-start(s32[64,1,2]{2,1,0:T(1,128)} %bitcast.3), calls=%async_computation | async-start | bytes 65536 | tf_op jit(solution)/shard_map/all_to_all | solution.py:75
  85.5 11.3 %copy-start.3 = (s32[2048]{0:T(1024)S(1)}, s32[2048]{0:T(1024)}, u32[]{:S(2)}) copy-start(s32[2048]{0:T(1024)} %param.24) | copy-start | bytes 24580
  85.5 196.8 %all-to-all-start.2 = ((bf16[64,2,128,256]{3,2,1,0:T(8,128)(2,1)}), bf16[64,2,128,256]{3,2,1,0:T(8,128)(2,1)}, u32[]{:S(2)}, u32[]{:S(2)}) async-start(bf16[64,2,128,256]{3,2,1,0:T(8,128)(2,1)} %bitcast.65), calls=%async_computation.2 | async-start | bytes 16777216 | tf_op jit(solution)/shard_map/all_to_all | solution.py:57
  114.9 173.6 %copy-start.4 = (s32[512]{0:T(512)S(1)}, s32[512]{0:T(512)}, u32[]{:S(2)}) copy-start(s32[512]{0:T(512)} %param.23) | copy-start | bytes 6148
  114.9 173.6 %copy-start.5 = (s32[96]{0:T(128)S(1)}, s32[96]{0:T(128)}, u32[]{:S(2)}) copy-start(s32[96]{0:T(128)} %param.19) | copy-start | bytes 1156
  282.4 191.9 %all-to-all-start.4 = ((bf16[64,2,128,256]{3,2,1,0:T(8,128)(2,1)}), bf16[64,2,128,256]{3,2,1,0:T(8,128)(2,1)}, u32[]{:S(2)}, u32[]{:S(2)}) async-start(bf16[64,2,128,256]{3,2,1,0:T(8,128)(2,1)} %broadcast_multiply_fusion), calls=%async_computation.4 | async-start | bytes 16777216 | tf_op jit(solution)/shard_map/all_to_all | solution.py:86
  553.1 191.8 %all-to-all-start.3 = ((bf16[64,2,128,256]{3,2,1,0:T(8,128)(2,1)}), bf16[64,2,128,256]{3,2,1,0:T(8,128)(2,1)}, u32[]{:S(2)}, u32[]{:S(2)}) async-start(bf16[64,2,128,256]{3,2,1,0:T(8,128)(2,1)} %bitcast.64), calls=%async_computation.3 | async-start | bytes 16777216 | tf_op jit(solution)/shard_map/all_to_all | solution.py:74
  559.1 267.4 %all-reduce.3.cloned.1.call-start = ((), (), s32[]{:S(2)}) async-start(), calls=%async_computation.5 | async-start | bytes 4194304 | tf_op jit(solution)/shard_map/psum | solution.py:79
  757.2 8.7 copy-start.2
  757.2 10.7 copy-start.1
  765.9 316.1 %all-reduce.5.cloned.1.call-start = ((), (), s32[]{:S(2)}) async-start(), calls=%async_computation.6 | async-start | bytes 524288 | tf_op jit(solution)/shard_map/psum | solution.py:102
Sparse Core Ops, SparseCore 0:
  766.0 60.3 all-reduce.2
  833.4 248.5 all-reduce.4
where the time goes:
time: 1100 us; the launch traced here: 1090 us
  waiting for transfers between devices  824 us (75%)
  local copies, waits for them, and re-layouts  139 us (13%)
  starting transfers between devices  47.1 us (4%)
  matrix products  44.7 us (4%)
  other arithmetic  21.6 us (2%)
  between operations  14.5 us (1%)
    psum x1, waiting for transfers between devices, local(): grad_weight = lax.psum(local_grad, ('wide', 'narrow'))  253 us
    all_to_all x1, waiting for transfers between devices, local(): lax.all_to_all(buffer2, 'wide', split_axis=0, concat_axis=0, tiled=True)  185 us
    all_to_all x1, waiting for transfers between devices, local(): lax.all_to_all(buffer1, 'wide', split_axis=0, concat_axis=0, tiled=True)  167 us
    all_to_all x1, waiting for transfers between devices, local(): lax.all_to_all(reply, 'wide', split_axis=0, concat_axis=0, tiled=True)  163 us
    psum x1, waiting for transfers between devices, local(): gathered = lax.psum(partial_value, 'narrow')  56.6 us
    unnamed x16, local copies, waits for them, and re-layouts  35.5 us
    scatter x2, local copies, waits for them, and re-layouts, bucketed(): jnp.zeros((width * CAP, TILE, F), jnp.bfloat16).at[where].set(terms)  35.5 us
  transfers between devices with their start and end apart: 7, of which 5 were waited for; matrix products, arithmetic and copies ran while one was open for 9% of the time, Pallas kernels for 0%

commit v1 on v0

v1 whole, which is shorter than its diff:
```python
import jax
import jax.numpy as jnp
from jax import lax
from jax.experimental import pallas as pl
from jax.experimental.pallas import tpu as pltpu
from jax.sharding import Mesh, PartitionSpec as P

F = 256
TILE = 128
TILES = 96
BLK = 4
UGRP = 16
NY, NZ, NC, NX = 4, 8, 2, 4
WIDE = ("y", "z", "c")
ALL = ("y", "z", "c", "x")
LAB = 16
BF16 = jnp.bfloat16
F32 = jnp.float32
VMEM_LIMIT = 48 * 1024 * 1024

SMEM_SPEC = pl.BlockSpec(memory_space=pltpu.SMEM)
VMEM_SPEC = pl.BlockSpec(memory_space=pltpu.VMEM)
ANY_SPEC = pl.BlockSpec(memory_space=pl.ANY)


def pack(me, first, second):
    parts = (first, second)
    shapes = [(p["groups"], p["cap"] * TILE + LAB, TILE) for p in parts]

    def kernel(me_ref, *rest):
        refs = (rest[0:4], rest[4:8])
        groups1 = shapes[0][0]
        outs1, out2 = rest[8 : 8 + groups1], rest[8 + groups1]
        tiles1, tiles2, room1, room2, count, labels, in_sems, sems1, sem2 = rest[9 + groups1 :]
        loads = [
            pltpu.make_async_copy(refs[1][3], tiles2, in_sems.at[1]),
            pltpu.make_async_copy(refs[0][3], tiles1, in_sems.at[0]),
        ]
        for load in loads:
            load.start()
        lane = lax.broadcasted_iota(jnp.int32, (1, TILE), 1)

        def lay(part, part_refs, tiles_ref, room):
            source_ref, owner_ref, slot_ref = part_refs[:3]
            groups, rows, _ = room.shape
            for g in range(groups):
                count[g] = 0
            labels[...] = jnp.full(labels.shape, float(BLK * part["dummy"]), F32)

            def step(t, carry):
                own = owner_ref[t]
                g = part["group_of"](own, me_ref)
                rank = count[g]
                count[g] = rank + 1
                row = pl.multiple_of(rank * TILE, TILE)
                room[g, pl.ds(row, TILE), :] = tiles_ref[t]
                label = (BLK * part["block_of"](own, slot_ref[t]) + source_ref[t]).astype(F32)
                old = labels[pl.ds(g, 1), :]
                labels[pl.ds(g, 1), :] = jnp.where(lane == rank, label, old)
                return carry

            lax.fori_loop(0, TILES, step, 0)
            room[:, rows - LAB : rows, :] = jnp.broadcast_to(
                labels[0:groups][:, None, :], (groups, LAB, TILE)
            ).astype(BF16)

        loads[0].wait()
        lay(second, refs[1], tiles2, room2)
        copies = [pltpu.make_async_copy(room2, out2, sem2)]
        copies[0].start()
        loads[1].wait()
        lay(first, refs[0], tiles1, room1)
        for g in range(groups1):
            copies.append(pltpu.make_async_copy(room1.at[g], outs1[g], sems1.at[g]))
            copies[-1].start()
        for copy in copies:
            copy.wait()

    out_shape = [jax.ShapeDtypeStruct(shapes[0][1:], BF16)] * shapes[0][0]
    out_shape.append(jax.ShapeDtypeStruct(shapes[1], BF16))
    most = max(shapes[0][0], shapes[1][0])
    outs = pl.pallas_call(
        kernel,
        out_shape=out_shape,
        in_specs=[SMEM_SPEC] + [SMEM_SPEC, SMEM_SPEC, SMEM_SPEC, ANY_SPEC] * 2,
        out_specs=[ANY_SPEC] * len(out_shape),
        scratch_shapes=[
            pltpu.VMEM((TILES, TILE, TILE), BF16),
            pltpu.VMEM((TILES, TILE, TILE), BF16),
            pltpu.VMEM(shapes[0], BF16),
            pltpu.VMEM(shapes[1], BF16),
            pltpu.SMEM((most,), jnp.int32),
            pltpu.VMEM((most, TILE), F32),
            pltpu.SemaphoreType.DMA((2,)),
            pltpu.SemaphoreType.DMA((shapes[0][0],)),
            pltpu.SemaphoreType.DMA,
        ],
        compiler_params=pltpu.CompilerParams(vmem_limit_bytes=VMEM_LIMIT),
        cost_estimate=pl.CostEstimate(flops=0, bytes_accessed=16 * 1024 * 1024, transcendentals=0),
        name="pack",
    )(me, *first["args"], *second["args"])
    return outs[:-1], outs[-1]


def labels_of(received, cap):
    return received[..., cap * TILE, :cap].astype(jnp.int32)


def products(labels, bases, received, blocks, cap, count, split_out, flip):
    groups = len(received) if isinstance(received, (list, tuple)) else received.shape[0]
    many = isinstance(received, (list, tuple))
    tiles_in = list(received) if many else [received]
    n_out = (split_out > 0) + (split_out < count)

    def kernel(lab_ref, base_ref, *rest):
        tile_refs, blocks_ref = rest[: len(tiles_in)], rest[len(tiles_in)]
        outs, acc = rest[len(tiles_in) + 1 : -1], rest[-1]
        acc[...] = jnp.zeros_like(acc)

        def one(i, g, tile):
            lab = lab_ref[i]
            near = base_ref[g] + lax.rem(lab, BLK)
            far = lax.div(lab, BLK)
            if flip:
                empty = far >= blocks.shape[0]
                into = jnp.where(empty, count, near)
                block = blocks_ref[jnp.where(empty, 0, far)]
                term = lax.dot_general(tile, block, (((0,), (0,)), ((), ())), preferred_element_type=F32)
            else:
                into = far
                term = jnp.dot(tile, blocks_ref[near], preferred_element_type=F32)
            acc[into] = acc[into] + term

        if many:
            for g, ref in enumerate(tile_refs):

                def step(k, carry, g=g, ref=ref):
                    row = pl.multiple_of(k * TILE, TILE)
                    one(g * cap + k, g, ref[pl.ds(row, TILE), :])
                    return carry

                lax.fori_loop(0, cap, step, 0, unroll=4)
        else:

            def step(i, carry):
                row = pl.multiple_of((i % cap) * TILE, TILE)
                one(i, i // cap, tile_refs[0][i // cap, pl.ds(row, TILE), :])
                return carry

            lax.fori_loop(0, groups * cap, step, 0, unroll=4)
        at = 0
        if split_out > 0:
            outs[at][...] = acc[0:split_out]
            at += 1
        if split_out < count:
            outs[at][...] = acc[split_out:count].astype(BF16)

    out_shape = []
    if split_out > 0:
        out_shape.append(jax.ShapeDtypeStruct((split_out, TILE, F), F32))
    if split_out < count:
        out_shape.append(jax.ShapeDtypeStruct((count - split_out, TILE, F), BF16))
    return pl.pallas_call(
        kernel,
        out_shape=out_shape,
        in_specs=[SMEM_SPEC, SMEM_SPEC] + [VMEM_SPEC] * (len(tiles_in) + 1),
        out_specs=[VMEM_SPEC] * n_out,
        scratch_shapes=[pltpu.VMEM((count + 1, TILE, F), F32)],
        compiler_params=pltpu.CompilerParams(vmem_limit_bytes=VMEM_LIMIT),
        cost_estimate=pl.CostEstimate(
            flops=2 * groups * cap * TILE * TILE * F, bytes_accessed=12 * 1024 * 1024, transcendentals=0
        ),
        name="back_products" if flip else "products",
    )(labels, bases, *tiles_in, blocks)


def all_to_all(value, axes):
    return lax.all_to_all(value, axes, split_axis=0, concat_axis=0, tiled=True)


def local(
    items,
    tile1_values,
    tile1_source,
    tile1_owner,
    tile1_slot,
    tile2_values,
    tile2_source,
    tile2_owner,
    tile2_slot,
    weight,
    bundle_degree,
    user_degree,
    cotangent,
):
    y, z, c, x = (lax.axis_index(a) for a in ALL)
    me = jnp.stack([y, c]).astype(jnp.int32)
    near1, near2 = NY * NC, NZ * NC
    cap1, cap2 = TILE // near1, TILE // near2

    def group1(own, me_ref):
        dest_y, dest_c = own // (NZ * NC), own % NC
        return ((dest_y - me_ref[0] + NY) % NY) * NC + (dest_c - me_ref[1] + NC) % NC

    send1, send2 = pack(
        me,
        dict(
            args=(tile1_source, tile1_owner[:, 0], tile1_slot, tile1_values),
            groups=near1, cap=cap1, group_of=group1, dummy=NZ * BLK,
            block_of=lambda own, slot: ((own // NC) % NZ) * BLK + slot,
        ),
        dict(
            args=(tile2_source, tile2_owner[:, 0], tile2_slot, tile2_values),
            groups=near2, cap=cap2, group_of=lambda own, me_ref: own % (NZ * NC), dummy=NY * UGRP,
            block_of=lambda own, slot: (own // (NZ * NC)) * UGRP + slot,
        ),
    )
    senders = jnp.arange(near1, dtype=jnp.int32)
    got1 = [send1[0]]
    for offset in range(1, near1):
        pairs = [
            (a * NC + b, ((a + offset // NC) % NY) * NC + (b + offset) % NC)
            for a in range(NY) for b in range(NC)
        ]
        got1.append(lax.ppermute(send1[offset], ("y", "c"), pairs))
    labels1 = jnp.concatenate([labels_of(part, cap1) for part in got1])
    bases1 = (((y - senders // NC + NY) % NY) * NC + (c + senders) % NC) * BLK
    got2 = all_to_all(send2, ("z", "c"))
    near_items = lax.all_gather(items, ("y", "c"), axis=0, tiled=True)

    rows = user_degree.shape[0] // NX
    degree = lax.dynamic_slice_in_dim(user_degree, x * rows, rows)[:, None].astype(F32)
    cot = lax.dynamic_slice_in_dim(cotangent, x * rows, rows)
    scaled_grad = (cot.astype(F32) / degree).astype(BF16)
    got2, scaled_grad = lax.optimization_barrier((got2, scaled_grad))
    near_grad = all_to_all(jnp.broadcast_to(scaled_grad, (NY * NX, rows, F)), ("y", "x"))

    part1 = products(
        labels1, bases1, got1, near_items.reshape(-1, TILE, F), cap1, NZ * BLK, NZ * BLK, False
    )[0]
    got2, part1 = lax.optimization_barrier((got2, part1))
    summed = lax.psum_scatter(part1.reshape(-1, F), "z", scatter_dimension=0, tiled=True)
    summed, near_grad = lax.optimization_barrier((summed, near_grad))
    bundle_emb = (summed / bundle_degree[:, None].astype(F32)).astype(BF16)
    mixed = jnp.dot(bundle_emb, weight, preferred_element_type=F32)
    activated = jax.nn.silu(mixed).astype(BF16)
    near_act = lax.all_gather(activated, ("z", "c"), axis=0, tiled=True)

    labels2 = labels_of(got2, cap2).reshape(-1)
    senders = jnp.arange(near2, dtype=jnp.int32)
    halves = ((senders + c) % NC) * (NZ * BLK) + (senders // NC) * BLK
    mine, other = products(
        labels2, halves, got2, near_grad.reshape(-1, TILE, F), cap2, NC * NZ * BLK, NZ * BLK, True
    )
    other = lax.ppermute(other, "c", [(0, 1), (1, 0)])
    both = (mine + other.astype(F32)).reshape(-1, F)
    near_act, both = lax.optimization_barrier((near_act, both))
    grad_act = lax.psum_scatter(both, "z", scatter_dimension=0, tiled=True)
    sigma = jax.nn.sigmoid(mixed)
    grad_mixed = (grad_act * sigma * (1.0 + mixed * (1.0 - sigma))).astype(BF16)
    local_grad = lax.dot_general(
        bundle_emb, grad_mixed, (((0,), (0,)), ((), ())), preferred_element_type=F32
    )
    grad_bundle = lax.dot_general(
        grad_mixed, weight, (((1,), (1,)), ((), ())), preferred_element_type=F32
    ).astype(BF16)

    part2 = products(
        labels2, senders * BLK, got2, near_act.reshape(-1, TILE, F), cap2, NY * UGRP, 0, False
    )[0]
    got_part = all_to_all(part2.reshape(NY * NX, rows, F), ("y", "x"))
    gathered = jnp.sum(got_part.astype(F32), axis=0)
    user_part = (gathered / degree).astype(BF16)
    user_out = lax.all_gather(user_part, "x", axis=0, tiled=True)

    piece = jnp.sum(all_to_all(local_grad.reshape(near2, -1, F), ("z", "c")), axis=0)
    piece = jnp.sum(all_to_all(jnp.broadcast_to(piece, (NY * NX,) + piece.shape), ("y", "x")), axis=0)
    grad_weight = all_to_all(jnp.broadcast_to(piece, (near2,) + piece.shape), ("z", "c")).reshape(F, F)
    return (user_out, grad_weight, grad_bundle)


def solution(mesh):
    axes = Mesh(mesh.devices.reshape(NY, NZ, NC, NX), ALL)
    in_specs = (
        P(ALL, None),
        P(ALL, None, None),
        P(ALL),
        P(ALL, None),
        P(ALL),
        P(ALL, None, None),
        P(ALL),
        P(ALL, None),
        P(ALL),
        P(),
        P(ALL),
        P(WIDE),
        P(WIDE, None),
    )
    out_specs = (P(WIDE, None), P(), P(ALL, None))
    return jax.shard_map(local, mesh=axes, in_specs=in_specs, out_specs=out_specs, check_vma=False)
```

time: 1100 us -> 370 us (0.34)
  waiting for transfers between devices: 824 us -> 158 us
  local copies, waits for them, and re-layouts: 139 us -> 16.4 us
  blocking collectives: 0 us -> 85.2 us
  Pallas kernels: 0 us -> 47.2 us
  matrix products: 44.7 us -> 2.24 us
  starting transfers between devices: 47.1 us -> 34.5 us
    all_to_all x5 -> x3, waiting for transfers between devices: 515 us -> 89.3 us  [all_to_all(): return lax.all_to_all(value, axes, split_axis=0, concat_axis=0, tiled=True)]
    psum x2 -> x0, waiting for transfers between devices: 309 us -> none  [the longest x1 253 us: local(): grad_weight = lax.psum(local_grad, ('wide', 'narrow'))]
    all_to_all x0 -> x3, blocking collectives: none -> 85.2 us  [all_to_all(): return lax.all_to_all(value, axes, split_axis=0, concat_axis=0, tiled=True)]
    ppermute x0 -> x8, waiting for transfers between devices: none -> 52.5 us  [the longest x7 48.5 us: local(): got1.append(lax.ppermute(send1[offset], ('y', 'c'), pairs))]
    pallas_call x0 -> x4, Pallas kernels: none -> 47.2 us  [the longest x3 38.6 us: products(): pl.pallas_call(kernel, out_shape=out_shape, in_specs=[SMEM_SPEC, SMEM_SPE...]
    dot_general x7 -> x1, matrix products: 40.9 us -> 1.01 us  [local(): mixed = jnp.dot(bundle_emb, weight, preferred_element_type=F32)]
    scatter x4 -> x0, local copies, waits for them, and re-layouts: 37.5 us -> none  [the longest x2 35.5 us: bucketed(): jnp.zeros((width * CAP, TILE, F), jnp.bfloat16).at[where].set(terms)]
    gather x4 -> x0, local copies, waits for them, and re-layouts: 30 us -> none  [the longest x1 9.4 us: local(): needed = back.reshape(width * CAP, TILE, F)[where2]]
  transfers between devices with their start and end apart: 7 -> 16, of which waited for: 5 -> 10; matrix products, arithmetic and copies ran while one was open for 9% -> 4% of each run, Pallas kernels for 0% -> 10%
where the time goes in v1:
time: 370 us; the launch traced here: 369 us
  waiting for transfers between devices  158 us (43%)
  blocking collectives  85.2 us (23%)
  Pallas kernels  47.2 us (13%)
  starting transfers between devices  34.5 us (9%)
  local copies, waits for them, and re-layouts  16.4 us (4%)
  between operations  14 us (4%)
  other arithmetic  12.3 us (3%)
    all_to_all x3, waiting for transfers between devices, all_to_all(): return lax.all_to_all(value, axes, split_axis=0, concat_axis=0, tiled=True)  89.3 us
    all_to_all x3, blocking collectives, all_to_all(): return lax.all_to_all(value, axes, split_axis=0, concat_axis=0, tiled=True)  85.2 us
    ppermute x7, waiting for transfers between devices, local(): got1.append(lax.ppermute(send1[offset], ('y', 'c'), pairs))  48.5 us
    pallas_call x3, Pallas kernels, products(): pl.pallas_call(kernel, out_shape=out_shape, in_specs=[SMEM_SPEC, SMEM_SPE...  38.6 us
    all_to_all x3, starting transfers between devices, all_to_all(): return lax.all_to_all(value, axes, split_axis=0, concat_axis=0, tiled=True)  21.2 us
    all_gather x1, waiting for transfers between devices, local(): near_act = lax.all_gather(activated, ('z', 'c'), axis=0, tiled=True)  15.1 us
    unnamed x34, local copies, waits for them, and re-layouts  13 us
    ppermute x7, starting transfers between devices, local(): got1.append(lax.ppermute(send1[offset], ('y', 'c'), pairs))  10.9 us
  transfers between devices with their start and end apart: 16, of which 10 were waited for; matrix products, arithmetic and copies ran while one was open for 4% of the time, Pallas kernels for 10%

profile of v1, /device:TPU:1, one launch (start us, length us, event | category | flops | bytes accessed | tf_op | source)
XLA Modules:
  0.0 369.5 jit_solution(2160526561641250899)
XLA Ops:
  11.2 8.6 %pack.1 = (bf16[2064,128]{1,0:T(8,128)(2,1)S(1)}, bf16[2064,128]{1,0:T(8,128)(2,1)S(1)}, bf16[2064,128]{1,0:T(8,128)(2,1)S(1)}, bf16[2064,128]{1,0:T(8,128)(2,1)...) custom-call(s32[2]{0:T(128)S(1)} %pad_add_fusion.me_ref, ...), custom_call_target="tpu_custom_call" | custom-call | bytes 16777216 | tf_op jit(solution)/shard_map/pack/pallas_call | solution.py:82
  22.2 10.0 %all-to-all-start = ((bf16[16,1040,128]{2,1,0:T(8,128)(2,1)}), bf16[16,1040,128]{2,1,0:T(8,128)(2,1)}, u32[]{:S(2)}, u32[]{:S(2)}) async-start(bf16[16,1040,128]{2,1,0:T(8,128)(2,1)} %get-tuple-element.22), calls=%async_computation | async-start | bytes 8519680 | tf_op jit(solution)/shard_map/all_to_all | solution.py:178
  33.0 2.9 collective-permute-start.6
  36.9 2.9 collective-permute-start.3
  43.4 4.5 %collective-permute-done.6.rest_7_ = bf16[2064,128]{1,0:T(8,128)(2,1)S(1)} collective-permute-done((bf16[2064,128]{1,0:T(8,128)(2,1)}, bf16[2064,128]{1,0:T(8,128)(2,1)S(1)}, u32[]{:S(2)}, u32[]{:S(2)}) %collective-permute-start.6) | collective-permute-done | bytes 528416 | tf_op jit(solution)/shard_map/ppermute | solution.py:225
  49.2 15.4 %collective-permute-done.5.rest_6_ = bf16[2064,128]{1,0:T(8,128)(2,1)S(1)} collective-permute-done((bf16[2064,128]{1,0:T(8,128)(2,1)}, bf16[2064,128]{1,0:T(8,128)(2,1)S(1)}, u32[]{:S(2)}, u32[]{:S(2)}) %collective-permute-start.5) | collective-permute-done | bytes 528416 | tf_op jit(solution)/shard_map/ppermute | solution.py:225
  68.5 14.5 %collective-permute-done.2.rest_3_ = bf16[2064,128]{1,0:T(8,128)(2,1)S(1)} collective-permute-done((bf16[2064,128]{1,0:T(8,128)(2,1)}, bf16[2064,128]{1,0:T(8,128)(2,1)S(1)}, u32[]{:S(2)}, u32[]{:S(2)}) %collective-permute-start.2) | collective-permute-done | bytes 528416 | tf_op jit(solution)/shard_map/ppermute | solution.py:225
  83.1 11.9 %collective-permute-done.1.rest_2_ = bf16[2064,128]{1,0:T(8,128)(2,1)S(1)} collective-permute-done((bf16[2064,128]{1,0:T(8,128)(2,1)}, bf16[2064,128]{1,0:T(8,128)(2,1)S(1)}, u32[]{:S(2)}, u32[]{:S(2)}) %collective-permute-start.1) | collective-permute-done | bytes 528416 | tf_op jit(solution)/shard_map/ppermute | solution.py:225
  98.8 11.6 %products.2 = f32[32,128,256]{2,1,0:T(8,128)} custom-call(s32[128]{0:T(128)S(1)} %concatenate.6.lab_ref, s32[8]{0:T(128)S(1)} %fusion.8.base_ref, bf16[2064,128]{1,0:T(8,128)(2,1)S(1)} %get-tuple-element.24.rest_0_, bf16[2064,128]{1,0:T(8,128)(2,1)S(1)} %copy-done.4, bf16[2064,128]{1,0:T(8,128)(2,1)S(1)} %copy-done.2, ...), custom_call_target="tpu_custom_call" | custom-call | flops 1073741824 | bytes 12582912 | tf_op jit(solution)/shard_map/products/pallas_call | solution.py:163
  110.4 16.7 %all-to-all-done.rest_0_ = bf16[16,1040,128]{2,1,0:T(8,128)(2,1)} async-done(((bf16[16,1040,128]{2,1,0:T(8,128)(2,1)}), bf16[16,1040,128]{2,1,0:T(8,128)(2,1)}, u32[]{:S(2)}, u32[]{:S(2)}) %all-to-all-start) | async-done | bytes 4259872 | tf_op jit(solution)/shard_map/all_to_all | solution.py:178
  127.2 2.4 broadcast_in_dim.11
  129.6 6.9 %all-to-all-start.1 = ((bf16[16,512,256]{2,1,0:T(8,128)(2,1)}), bf16[16,512,256]{2,1,0:T(8,128)(2,1)}, u32[]{:S(2)}, u32[]{:S(2)}) async-start(bf16[16,512,256]{2,1,0:T(8,128)(2,1)} %broadcast_in_dim.11), calls=%async_computation.2 | async-start | bytes 8388608 | tf_op jit(solution)/shard_map/all_to_all | solution.py:178
  136.6 61.7 %all-to-all-done.1 = bf16[16,512,256]{2,1,0:T(8,128)(2,1)} async-done(((bf16[16,512,256]{2,1,0:T(8,128)(2,1)}), bf16[16,512,256]{2,1,0:T(8,128)(2,1)}, u32[]{:S(2)}, u32[]{:S(2)}) %all-to-all-start.1) | async-done | bytes 4194336 | tf_op jit(solution)/shard_map/all_to_all | solution.py:178
  201.5 15.0 %back_products.1 = (f32[32,128,256]{2,1,0:T(8,128)}, bf16[32,128,256]{2,1,0:T(8,128)(2,1)S(1)}) custom-call(s32[128]{0:T(128)S(1)} %reshape.62.lab_ref, s32[16]{0:T(128)S(1)} %fusion.4.base_ref, bf16[16,1040,128]{2,1,0:T(8,128)(2,1)} %all-to-all-done.rest_0_, bf16[64,128,256]{2,1,0:T(8,128)(2,1)} %bitcast.14.rest_1_), custom_call_target="tpu_custom_call" | custom-call | flops 1073741824 | bytes 12582912 | tf_op jit(solution)/shard_map/back_products/pallas_call | solution.py:163
  218.5 3.9 %collective-permute-done.7 = bf16[32,128,256]{2,1,0:T(8,128)(2,1)S(1)} collective-permute-done((bf16[32,128,256]{2,1,0:T(8,128)(2,1)S(1)}, bf16[32,128,256]{2,1,0:T(8,128)(2,1)S(1)}, u32[]{:S(2)}, u32[]{:S(2)}) %collective-permute-start.7) | collective-permute-done | bytes 2097184 | tf_op jit(solution)/shard_map/ppermute | solution.py:255
  222.5 5.0 %convert_add_fusion = f32[32,128,256]{2,1,0:T(8,128)} fusion(f32[32,128,256]{2,1,0:T(8,128)} %get-tuple-element.37, bf16[32,128,256]{2,1,0:T(8,128)(2,1)S(1)} %collective-permute-done.7), kind=kLoop, calls=%fused_computation.1 | loop fusion | flops 2097152 | bytes 10485760 | tf_op jit(solution)/shard_map/add | solution.py:256
  227.5 15.1 %all-gather.6.cloned.1.call-done = bf16[8192,256]{1,0:T(8,128)(2,1)} async-done(((bf16[512,256]{1,0:T(8,128)(2,1)}), bf16[8192,256]{1,0:T(8,128)(2,1)}) %all-gather.6.cloned.1.call-update) | async-done | bytes 4194320 | tf_op jit(solution)/shard_map/all_gather | solution.py:247
  242.8 12.0 %products.3 = bf16[64,128,256]{2,1,0:T(8,128)(2,1)S(1)} custom-call(s32[128]{0:T(128)S(1)} %reshape.62.lab_ref, s32[16]{0:T(128)S(1)} %iota_multiply_fusion.base_ref, bf16[16,1040,128]{2,1,0:T(8,128)(2,1)} %all-to-all-done.rest_0_, bf16[64,128,256]{2,1,0:T(8,128)(2,1)} %bitcast.39), custom_call_target="tpu_custom_call" | custom-call | flops 1073741824 | bytes 12582912 | tf_op jit(solution)/shard_map/products/pallas_call | solution.py:163
  254.9 56.4 %all_to_all.30 = bf16[16,512,256]{2,1,0:T(8,128)(2,1)S(1)} all-to-all(bf16[16,512,256]{2,1,0:T(8,128)(2,1)S(1)} %bitcast.34), channel_id=1, replica_groups=mesh['y'=4,'z'=8,'c'=2,'x'=4] {'y','x'}, dimensions={0} | all-to-all | bytes 8388608 | tf_op jit(solution)/shard_map/all_to_all | solution.py:178
  314.3 17.5 %all_to_all.31 = f32[16,16,256]{2,1,0:T(8,128)S(1)} all-to-all(f32[16,16,256]{2,1,0:T(8,128)S(1)} %bitcast.41), channel_id=1, replica_groups=mesh['y'=4,'z'=8,'c'=2,'x'=4] {'z','c'}, dimensions={0} | all-to-all | bytes 524288 | tf_op jit(solution)/shard_map/all_to_all | solution.py:178
  331.8 11.3 %all_to_all.32 = f32[16,16,256]{2,1,0:T(8,128)S(1)} all-to-all(f32[16,16,256]{2,1,0:T(8,128)S(1)} %broadcast_in_dim.12), channel_id=1, replica_groups=mesh['y'=4,'z'=8,'c'=2,'x'=4] {'y','x'}, dimensions={0} | all-to-all | bytes 524288 | tf_op jit(solution)/shard_map/all_to_all | solution.py:178
  343.8 4.3 %all-to-all-start.5 = ((f32[16,16,256]{2,1,0:T(8,128)}), f32[16,16,256]{2,1,0:T(8,128)S(1)}, u32[]{:S(2)}, u32[]{:S(2)}) async-start(f32[16,16,256]{2,1,0:T(8,128)} %broadcast_in_dim.13), calls=%async_computation.7 | async-start | bytes 524288 | tf_op jit(solution)/shard_map/all_to_all | solution.py:178
  349.1 10.9 %all-to-all-done.5 = f32[16,16,256]{2,1,0:T(8,128)S(1)} async-done(((f32[16,16,256]{2,1,0:T(8,128)}), f32[16,16,256]{2,1,0:T(8,128)S(1)}, u32[]{:S(2)}, u32[]{:S(2)}) %all-to-all-start.5) | async-done | bytes 262176 | tf_op jit(solution)/shard_map/all_to_all | solution.py:178
  360.0 2.3 copy.18
  (86 shorter events, 31.7 us)
Async XLA Ops:
  7.2 192.4 %copy-start = (bf16[256,256]{1,0:T(8,128)(2,1)S(1)}, bf16[256,256]{1,0:T(8,128)(2,1)}, u32[]{:S(2)}) copy-start(bf16[256,256]{1,0:T(8,128)(2,1)} %param.22) | copy-start | bytes 393220
  19.8 0.8 copy-start.11
  20.6 0.8 copy-start.12
  21.4 0.8 copy-start.13
  22.2 104.9 %all-to-all-start = ((bf16[16,1040,128]{2,1,0:T(8,128)(2,1)}), bf16[16,1040,128]{2,1,0:T(8,128)(2,1)}, u32[]{:S(2)}, u32[]{:S(2)}) async-start(bf16[16,1040,128]{2,1,0:T(8,128)(2,1)} %get-tuple-element.22), calls=%async_computation | async-start | bytes 8519680 | tf_op jit(solution)/shard_map/all_to_all | solution.py:178
  32.2 64.5 %all-gather.4.cloned.1.call-start = ((), (), s32[]{:S(2)}) async-start(), calls=%async_computation.8 | async-start | bytes 2359296 | tf_op jit(solution)/shard_map/all_gather | solution.py:229
  32.9 165.4 %reduce-scatter.3.cloned.1.call-start = ((), (), s32[]{:S(2)}) async-start(), calls=%async_computation.9 | async-start | bytes 4718592 | tf_op jit(solution)/shard_map/reduce_scatter | solution.py:242
  33.0 14.9 %collective-permute-start.6 = (bf16[2064,128]{1,0:T(8,128)(2,1)}, bf16[2064,128]{1,0:T(8,128)(2,1)S(1)}, u32[]{:S(2)}, u32[]{:S(2)}) collective-permute-start(bf16[2064,128]{1,0:T(8,128)(2,1)} %get-tuple-element.31), channel_id=1, source_target_pairs={{0,196},{4,192},{64,4},{68,0},{128,68},{132,64},{192,132},{196,128... | collective-permute-start | bytes 1585160 | tf_op jit(solution)/shard_map/ppermute | solution.py:225
  35.8 28.8 %collective-permute-start.5 = (bf16[2064,128]{1,0:T(8,128)(2,1)}, bf16[2064,128]{1,0:T(8,128)(2,1)S(1)}, u32[]{:S(2)}, u32[]{:S(2)}) collective-permute-start(bf16[2064,128]{1,0:T(8,128)(2,1)} %get-tuple-element.30), channel_id=1, source_target_pairs={{0,192},{4,196},{64,0},{68,4},{128,64},{132,68},{192,128},{196,132... | collective-permute-start | bytes 1585160 | tf_op jit(solution)/shard_map/ppermute | solution.py:225
  36.3 30.1 %collective-permute-start.4 = (bf16[2064,128]{1,0:T(8,128)(2,1)}, bf16[2064,128]{1,0:T(8,128)(2,1)S(1)}, u32[]{:S(2)}, u32[]{:S(2)}) collective-permute-start(bf16[2064,128]{1,0:T(8,128)(2,1)} %get-tuple-element.29), channel_id=1, source_target_pairs={{0,132},{4,128},{64,196},{68,192},{128,4},{132,0},{192,68},{196,64... | collective-permute-start | bytes 1585160 | tf_op jit(solution)/shard_map/ppermute | solution.py:225
  36.9 31.7 %collective-permute-start.3 = (bf16[2064,128]{1,0:T(8,128)(2,1)}, bf16[2064,128]{1,0:T(8,128)(2,1)S(1)}, u32[]{:S(2)}, u32[]{:S(2)}) collective-permute-start(bf16[2064,128]{1,0:T(8,128)(2,1)} %get-tuple-element.28), channel_id=1, source_target_pairs={{0,128},{4,132},{64,192},{68,196},{128,0},{132,4},{192,64},{196,68... | collective-permute-start | bytes 1585160 | tf_op jit(solution)/shard_map/ppermute | solution.py:225
  39.8 43.3 %collective-permute-start.2 = (bf16[2064,128]{1,0:T(8,128)(2,1)}, bf16[2064,128]{1,0:T(8,128)(2,1)S(1)}, u32[]{:S(2)}, u32[]{:S(2)}) collective-permute-start(bf16[2064,128]{1,0:T(8,128)(2,1)} %copy-done.13), channel_id=1, source_target_pairs={{0,68},{4,64},{64,132},{68,128},{128,196},{132,192},{192,4},{196,0... | collective-permute-start | bytes 1585160 | tf_op jit(solution)/shard_map/ppermute | solution.py:225
  47.9 47.1 %collective-permute-start.1 = (bf16[2064,128]{1,0:T(8,128)(2,1)}, bf16[2064,128]{1,0:T(8,128)(2,1)S(1)}, u32[]{:S(2)}, u32[]{:S(2)}) collective-permute-start(bf16[2064,128]{1,0:T(8,128)(2,1)} %copy-done.12), channel_id=1, source_target_pairs={{0,64},{4,68},{64,128},{68,132},{128,192},{132,196},{192,0},{196,4... | collective-permute-start | bytes 1585160 | tf_op jit(solution)/shard_map/ppermute | solution.py:225
  64.6 31.2 %collective-permute-start = (bf16[2064,128]{1,0:T(8,128)(2,1)}, bf16[2064,128]{1,0:T(8,128)(2,1)S(1)}, u32[]{:S(2)}, u32[]{:S(2)}) collective-permute-start(bf16[2064,128]{1,0:T(8,128)(2,1)} %copy-done.11), channel_id=1, source_target_pairs={{0,4},{4,0},{64,68},{68,64},{128,132},{132,128},{192,196},{196,192... | collective-permute-start | bytes 1585160 | tf_op jit(solution)/shard_map/ppermute | solution.py:225
  96.7 1.0 copy-start.2
  97.8 1.0 copy-start.4
  110.4 16.8 %copy-start.14 = (bf16[512,256]{1,0:T(8,128)(2,1)S(1)}, bf16[512,256]{1,0:T(8,128)(2,1)}, u32[]{:S(2)}) copy-start(bf16[512,256]{1,0:T(8,128)(2,1)} %divide_convert_fusion.2) | copy-start | bytes 786436
  129.6 7.0 %copy-start.15 = (s32[512]{0:T(512)S(1)}, s32[512]{0:T(512)}, u32[]{:S(2)}) copy-start(s32[512]{0:T(512)} %param.23) | copy-start | bytes 6148
  129.6 68.7 %all-to-all-start.1 = ((bf16[16,512,256]{2,1,0:T(8,128)(2,1)}), bf16[16,512,256]{2,1,0:T(8,128)(2,1)}, u32[]{:S(2)}, u32[]{:S(2)}) async-start(bf16[16,512,256]{2,1,0:T(8,128)(2,1)} %broadcast_in_dim.11), calls=%async_computation.2 | async-start | bytes 8388608 | tf_op jit(solution)/shard_map/all_to_all | solution.py:178
  136.6 106.0 %all-gather.6.cloned.1.call-start = ((), (), s32[]{:S(2)}) async-start(), calls=%async_computation.10 | async-start | bytes 4456448 | tf_op jit(solution)/shard_map/all_gather | solution.py:247
  200.6 112.2 %reduce-scatter.5.cloned.1.call-start = ((), (), s32[]{:S(2)}) async-start(), calls=%async_computation.12 | async-start | bytes 4718592 | tf_op jit(solution)/shard_map/reduce_scatter | solution.py:258
  216.5 6.0 %collective-permute-start.7 = (bf16[32,128,256]{2,1,0:T(8,128)(2,1)S(1)}, bf16[32,128,256]{2,1,0:T(8,128)(2,1)S(1)}, u32[]{:S(2)}, u32[]{:S(2)}) collective-permute-start(bf16[32,128,256]{2,1,0:T(8,128)(2,1)S(1)} %get-tuple-element.38), channel_id=1, source_target_pairs={{0,4},{4,0},{1,5},{5,1},{2,6},{6,2},{3,7},{7,3},{8,12},{12,8},{9,1... | collective-permute-start | bytes 6291464 | tf_op jit(solution)/shard_map/ppermute | solution.py:255
  242.6 105.5 %all-gather.8.cloned.1.call-start = ((), (), s32[]{:S(2)}) async-start(), calls=%async_computation.11 | async-start | bytes 1310720 | tf_op jit(solution)/shard_map/all_gather | solution.py:274
  343.8 16.1 %all-to-all-start.5 = ((f32[16,16,256]{2,1,0:T(8,128)}), f32[16,16,256]{2,1,0:T(8,128)S(1)}, u32[]{:S(2)}, u32[]{:S(2)}) async-start(f32[16,16,256]{2,1,0:T(8,128)} %broadcast_in_dim.13), calls=%async_computation.7 | async-start | bytes 524288 | tf_op jit(solution)/shard_map/all_to_all | solution.py:178
  (8 other events, 5.5 us)
Sparse Core Ops, SparseCore 0:
  34.9 61.2 all-gather.3
  127.3 54.7 reduce-scatter.2
  200.7 41.8 all-gather.5
  245.0 53.4 reduce-scatter.4
  312.9 21.3 all-gather.7

commit v2 on v1

--- a/solution.py
+++ b/solution.py
@@ -28,15 +28,20 @@
     shapes = [(p["groups"], p["cap"] * TILE + LAB, TILE) for p in parts]
 
     def kernel(me_ref, *rest):
-        refs = (rest[0:4], rest[4:8])
+        given = (rest[0:4], rest[4:8])
         groups1 = shapes[0][0]
         outs1, out2 = rest[8 : 8 + groups1], rest[8 + groups1]
-        tiles1, tiles2, room1, room2, count, labels, in_sems, sems1, sem2 = rest[9 + groups1 :]
+        tiles1, tiles2, room1, room2, count, labels, in_sems, sems1, sem2 = rest[9 + groups1 : 18 + groups1]
+        indices = rest[18 + groups1 : 24 + groups1]
+        refs = (indices[0:3], indices[3:6])
+        small = [
+            pltpu.make_async_copy(given[i // 3][i % 3], indices[i], in_sems.at[2 + i]) for i in range(6)
+        ]
         loads = [
-            pltpu.make_async_copy(refs[1][3], tiles2, in_sems.at[1]),
-            pltpu.make_async_copy(refs[0][3], tiles1, in_sems.at[0]),
+            pltpu.make_async_copy(given[1][3], tiles2, in_sems.at[1]),
+            pltpu.make_async_copy(given[0][3], tiles1, in_sems.at[0]),
         ]
-        for load in loads:
+        for load in small + loads:
             load.start()
         lane = lax.broadcasted_iota(jnp.int32, (1, TILE), 1)
 
@@ -54,7 +59,7 @@
                 count[g] = rank + 1
                 row = pl.multiple_of(rank * TILE, TILE)
                 room[g, pl.ds(row, TILE), :] = tiles_ref[t]
-                label = (BLK * part["block_of"](own, slot_ref[t]) + source_ref[t]).astype(F32)
+                label = (BLK * part["block_of"](own, slot_ref[t], me_ref) + source_ref[t]).astype(F32)
                 old = labels[pl.ds(g, 1), :]
                 labels[pl.ds(g, 1), :] = jnp.where(lane == rank, label, old)
                 return carry
@@ -64,6 +69,8 @@
                 labels[0:groups][:, None, :], (groups, LAB, TILE)
             ).astype(BF16)
 
+        for load in small:
+            load.wait()
         loads[0].wait()
         lay(second, refs[1], tiles2, room2)
         copies = [pltpu.make_async_copy(room2, out2, sem2)]
@@ -82,7 +89,7 @@
     outs = pl.pallas_call(
         kernel,
         out_shape=out_shape,
-        in_specs=[SMEM_SPEC] + [SMEM_SPEC, SMEM_SPEC, SMEM_SPEC, ANY_SPEC] * 2,
+        in_specs=[SMEM_SPEC] + [ANY_SPEC] * 8,
         out_specs=[ANY_SPEC] * len(out_shape),
         scratch_shapes=[
             pltpu.VMEM((TILES, TILE, TILE), BF16),
@@ -91,10 +98,11 @@
             pltpu.VMEM(shapes[1], BF16),
             pltpu.SMEM((most,), jnp.int32),
             pltpu.VMEM((most, TILE), F32),
-            pltpu.SemaphoreType.DMA((2,)),
+            pltpu.SemaphoreType.DMA((8,)),
             pltpu.SemaphoreType.DMA((shapes[0][0],)),
             pltpu.SemaphoreType.DMA,
-        ],
+        ]
+        + [pltpu.SMEM((TILES,), jnp.int32)] * 6,
         compiler_params=pltpu.CompilerParams(vmem_limit_bytes=VMEM_LIMIT),
         cost_estimate=pl.CostEstimate(flops=0, bytes_accessed=16 * 1024 * 1024, transcendentals=0),
         name="pack",
@@ -106,48 +114,57 @@
     return received[..., cap * TILE, :cap].astype(jnp.int32)
 
 
-def products(labels, bases, received, blocks, cap, count, split_out, flip):
-    groups = len(received) if isinstance(received, (list, tuple)) else received.shape[0]
+def products(labels, bases, received, blocks, places, cap, count, split_out, flip):
     many = isinstance(received, (list, tuple))
     tiles_in = list(received) if many else [received]
+    groups = len(received) if many else received.shape[0]
     n_out = (split_out > 0) + (split_out < count)
-
-    def kernel(lab_ref, base_ref, *rest):
-        tile_refs, blocks_ref = rest[: len(tiles_in)], rest[len(tiles_in)]
-        outs, acc = rest[len(tiles_in) + 1 : -1], rest[-1]
+    n_in, n_blocks = len(tiles_in), len(blocks)
+    blocks = [b.reshape(-1, TILE, F) for b in blocks]
+    total = sum(b.shape[0] for b in blocks)
+
+    def kernel(lab_ref, base_ref, place_ref, *rest):
+        tile_refs, block_refs = rest[:n_in], rest[n_in : n_in + n_blocks]
+        outs = rest[n_in + n_blocks : n_in + n_blocks + n_out]
+        acc, room, tiles, sems, tile_sems = rest[n_in + n_blocks + n_out :]
+        loads = [
+            pltpu.make_async_copy(ref, room.at[pl.ds(place_ref[i], blocks[i].shape[0])], sems.at[i])
+            for i, ref in enumerate(block_refs)
+        ]
+        rows = cap * TILE
+        tile_loads = []
+        for g in range(groups):
+            source = tile_refs[g].at[pl.ds(0, rows), :] if many else tile_refs[0].at[g, pl.ds(0, rows), :]
+            tile_loads.append(pltpu.make_async_copy(source, tiles.at[g], tile_sems.at[g]))
+        for load in loads + tile_loads:
+            load.start()
         acc[...] = jnp.zeros_like(acc)
+        for load in loads:
+            load.wait()
 
         def one(i, g, tile):
             lab = lab_ref[i]
             near = base_ref[g] + lax.rem(lab, BLK)
             far = lax.div(lab, BLK)
             if flip:
-                empty = far >= blocks.shape[0]
+                empty = far >= total
                 into = jnp.where(empty, count, near)
-                block = blocks_ref[jnp.where(empty, 0, far)]
+                block = room[jnp.where(empty, 0, far)]
                 term = lax.dot_general(tile, block, (((0,), (0,)), ((), ())), preferred_element_type=F32)
             else:
                 into = far
-                term = jnp.dot(tile, blocks_ref[near], preferred_element_type=F32)
+                term = jnp.dot(tile, room[near], preferred_element_type=F32)
             acc[into] = acc[into] + term
 
-        if many:
-            for g, ref in enumerate(tile_refs):
-
-                def step(k, carry, g=g, ref=ref):
-                    row = pl.multiple_of(k * TILE, TILE)
-                    one(g * cap + k, g, ref[pl.ds(row, TILE), :])
-                    return carry
-
-                lax.fori_loop(0, cap, step, 0, unroll=4)
-        else:
-
-            def step(i, carry):
-                row = pl.multiple_of((i % cap) * TILE, TILE)
-                one(i, i // cap, tile_refs[0][i // cap, pl.ds(row, TILE), :])
+        for g in range(groups):
+
+            def step(k, carry, g=g):
+                row = pl.multiple_of(k * TILE, TILE)
+                one(g * cap + k, g, tiles[g, pl.ds(row, TILE), :])
                 return carry
 
-            lax.fori_loop(0, groups * cap, step, 0, unroll=4)
+            tile_loads[g].wait()
+            lax.fori_loop(0, cap, step, 0, unroll=4)
         at = 0
         if split_out > 0:
             outs[at][...] = acc[0:split_out]
@@ -163,15 +180,21 @@
     return pl.pallas_call(
         kernel,
         out_shape=out_shape,
-        in_specs=[SMEM_SPEC, SMEM_SPEC] + [VMEM_SPEC] * (len(tiles_in) + 1),
+        in_specs=[SMEM_SPEC, SMEM_SPEC, SMEM_SPEC] + [ANY_SPEC] * (n_in + n_blocks),
         out_specs=[VMEM_SPEC] * n_out,
-        scratch_shapes=[pltpu.VMEM((count + 1, TILE, F), F32)],
+        scratch_shapes=[
+            pltpu.VMEM((count + 1, TILE, F), F32),
+            pltpu.VMEM((total, TILE, F), BF16),
+            pltpu.VMEM((groups, cap * TILE, TILE), BF16),
+            pltpu.SemaphoreType.DMA((n_blocks,)),
+            pltpu.SemaphoreType.DMA((groups,)),
+        ],
         compiler_params=pltpu.CompilerParams(vmem_limit_bytes=VMEM_LIMIT),
         cost_estimate=pl.CostEstimate(
             flops=2 * groups * cap * TILE * TILE * F, bytes_accessed=12 * 1024 * 1024, transcendentals=0
         ),
         name="back_products" if flip else "products",
-    )(labels, bases, *tiles_in, blocks)
+    )(labels, bases, places, *tiles_in, *blocks)
 
 
 def all_to_all(value, axes):
@@ -195,52 +218,45 @@
 ):
     y, z, c, x = (lax.axis_index(a) for a in ALL)
     me = jnp.stack([y, c]).astype(jnp.int32)
-    near1, near2 = NY * NC, NZ * NC
+    near1, near2 = NY, NZ * NC
     cap1, cap2 = TILE // near1, TILE // near2
-
-    def group1(own, me_ref):
-        dest_y, dest_c = own // (NZ * NC), own % NC
-        return ((dest_y - me_ref[0] + NY) % NY) * NC + (dest_c - me_ref[1] + NC) % NC
-
+    both1 = NC * NZ * BLK
     send1, send2 = pack(
         me,
         dict(
             args=(tile1_source, tile1_owner[:, 0], tile1_slot, tile1_values),
-            groups=near1, cap=cap1, group_of=group1, dummy=NZ * BLK,
-            block_of=lambda own, slot: ((own // NC) % NZ) * BLK + slot,
+            groups=near1, cap=cap1, dummy=both1,
+            group_of=lambda own, me_ref: (own // (NZ * NC) - me_ref[0] + NY) % NY,
+            block_of=lambda own, slot, me_ref: (((own + me_ref[1]) % NC) * NZ + (own // NC) % NZ) * BLK + slot,
         ),
         dict(
             args=(tile2_source, tile2_owner[:, 0], tile2_slot, tile2_values),
-            groups=near2, cap=cap2, group_of=lambda own, me_ref: own % (NZ * NC), dummy=NY * UGRP,
-            block_of=lambda own, slot: (own // (NZ * NC)) * UGRP + slot,
+            groups=near2, cap=cap2, dummy=NY * UGRP,
+            group_of=lambda own, me_ref: own % (NZ * NC),
+            block_of=lambda own, slot, me_ref: (own // (NZ * NC)) * UGRP + slot,
         ),
     )
-    senders = jnp.arange(near1, dtype=jnp.int32)
-    got1 = [send1[0]]
-    for offset in range(1, near1):
-        pairs = [
-            (a * NC + b, ((a + offset // NC) % NY) * NC + (b + offset) % NC)
-            for a in range(NY) for b in range(NC)
-        ]
-        got1.append(lax.ppermute(send1[offset], ("y", "c"), pairs))
+    got1, near_items = [send1[0]], [items]
+    for dy in range(1, NY):
+        pairs = [(a, (a + dy) % NY) for a in range(NY)]
+        near_items.append(lax.ppermute(items, "y", pairs))
+        got1.append(lax.ppermute(send1[dy], "y", pairs))
     labels1 = jnp.concatenate([labels_of(part, cap1) for part in got1])
-    bases1 = (((y - senders // NC + NY) % NY) * NC + (c + senders) % NC) * BLK
+    places1 = jnp.arange(NY, dtype=jnp.int32) * BLK
     got2 = all_to_all(send2, ("z", "c"))
-    near_items = lax.all_gather(items, ("y", "c"), axis=0, tiled=True)
-
     rows = user_degree.shape[0] // NX
     degree = lax.dynamic_slice_in_dim(user_degree, x * rows, rows)[:, None].astype(F32)
+    zero = jnp.zeros((1,), jnp.int32)
     cot = lax.dynamic_slice_in_dim(cotangent, x * rows, rows)
     scaled_grad = (cot.astype(F32) / degree).astype(BF16)
-    got2, scaled_grad = lax.optimization_barrier((got2, scaled_grad))
-    near_grad = all_to_all(jnp.broadcast_to(scaled_grad, (NY * NX, rows, F)), ("y", "x"))
-
-    part1 = products(
-        labels1, bases1, got1, near_items.reshape(-1, TILE, F), cap1, NZ * BLK, NZ * BLK, False
-    )[0]
+    near_grad = lax.all_gather(scaled_grad, ("y", "x"), axis=0, tiled=True)
+
+    near_grad, labels1 = lax.optimization_barrier((near_grad, labels1))
+    mine, other = products(labels1, places1, got1, near_items, places1, cap1, both1, both1 // NC, False)
+    other = lax.ppermute(other, "c", [(0, 1), (1, 0)])
+    part1 = (mine + other.astype(F32)).reshape(-1, F)
     got2, part1 = lax.optimization_barrier((got2, part1))
-    summed = lax.psum_scatter(part1.reshape(-1, F), "z", scatter_dimension=0, tiled=True)
-    summed, near_grad = lax.optimization_barrier((summed, near_grad))
+    summed = lax.psum_scatter(part1, "z", scatter_dimension=0, tiled=True)
     bundle_emb = (summed / bundle_degree[:, None].astype(F32)).astype(BF16)
     mixed = jnp.dot(bundle_emb, weight, preferred_element_type=F32)
     activated = jax.nn.silu(mixed).astype(BF16)
@@ -250,7 +266,7 @@
     senders = jnp.arange(near2, dtype=jnp.int32)
     halves = ((senders + c) % NC) * (NZ * BLK) + (senders // NC) * BLK
     mine, other = products(
-        labels2, halves, got2, near_grad.reshape(-1, TILE, F), cap2, NC * NZ * BLK, NZ * BLK, True
+        labels2, halves, got2, [near_grad], zero, cap2, NC * NZ * BLK, NZ * BLK, True
     )
     other = lax.ppermute(other, "c", [(0, 1), (1, 0)])
     both = (mine + other.astype(F32)).reshape(-1, F)
@@ -266,7 +282,7 @@
     ).astype(BF16)
 
     part2 = products(
-        labels2, senders * BLK, got2, near_act.reshape(-1, TILE, F), cap2, NY * UGRP, 0, False
+        labels2, senders * BLK, got2, [near_act], zero, cap2, NY * UGRP, 0, False
     )[0]
     got_part = all_to_all(part2.reshape(NY * NX, rows, F), ("y", "x"))
     gathered = jnp.sum(got_part.astype(F32), axis=0)

time: 370 us -> 364 us (0.984)
  starting transfers between devices: 34.5 us -> 28.4 us
  other arithmetic: 12.3 us -> 18 us
  waiting for transfers between devices: 158 us -> 154 us
    all_to_all x3 -> x2, waiting for transfers between devices: 89.3 us -> 10.9 us  [all_to_all(): return lax.all_to_all(value, axes, split_axis=0, concat_axis=0, tiled=True)]
    reduce_scatter x1, waiting for transfers between devices: 0.01 us -> 53.3 us  [local(): summed = lax.psum_scatter(part1, 'z', scatter_dimension=0, tiled=True)]
    ppermute x7 -> x6, waiting for transfers between devices: 48.5 us -> 59.3 us  [the longest x3 57.6 us: local(): got1.append(lax.ppermute(send1[dy], 'y', pairs))]
    all_gather x1, waiting for transfers between devices: 0.01 us -> 7.17 us  [local(): near_grad = lax.all_gather(scaled_grad, ('y', 'x'), axis=0, tiled=True)]
    all_to_all x3 -> x2, starting transfers between devices: 21.2 us -> 14.4 us  [all_to_all(): return lax.all_to_all(value, axes, split_axis=0, concat_axis=0, tiled=True)]
    add x0 -> x1, other arithmetic: none -> 4.97 us  [local(): part1 = (mine + other.astype(F32)).reshape(-1, F)]
    ppermute x1 -> x2, waiting for transfers between devices: 3.93 us -> 8.16 us  [local(): other = lax.ppermute(other, 'c', [(0, 1), (1, 0)])]
    ppermute x7 -> x6, starting transfers between devices: 10.9 us -> 11.6 us  [the longest x3 7.71 us: local(): near_items.append(lax.ppermute(items, 'y', pairs))]
  transfers between devices with their start and end apart: 16 -> 15, of which waited for: 10 -> 9; matrix products, arithmetic and copies ran while one was open for 4% -> 4% of each run, Pallas kernels for 10% -> 13%
where the time goes in v2:
time: 364 us; the launch traced here: 363 us
  waiting for transfers between devices  154 us (42%)
  blocking collectives  85.4 us (23%)
  Pallas kernels  46.9 us (13%)
  starting transfers between devices  28.4 us (8%)
  other arithmetic  18 us (5%)
  between operations  13.9 us (4%)
  local copies, waits for them, and re-layouts  13.8 us (4%)
    all_to_all x3, blocking collectives, all_to_all(): return lax.all_to_all(value, axes, split_axis=0, concat_axis=0, tiled=True)  85.4 us
    ppermute x3, waiting for transfers between devices, local(): got1.append(lax.ppermute(send1[dy], 'y', pairs))  57.6 us
    reduce_scatter x1, waiting for transfers between devices, local(): summed = lax.psum_scatter(part1, 'z', scatter_dimension=0, tiled=True)  53.3 us
    pallas_call x3, Pallas kernels, products(): pl.pallas_call(kernel, out_shape=out_shape, in_specs=[SMEM_SPEC, SMEM_SPE...  38.8 us
    all_gather x1, waiting for transfers between devices, local(): near_act = lax.all_gather(activated, ('z', 'c'), axis=0, tiled=True)  15.4 us
    all_to_all x2, starting transfers between devices, all_to_all(): return lax.all_to_all(value, axes, split_axis=0, concat_axis=0, tiled=True)  14.4 us
    unnamed x34, local copies, waits for them, and re-layouts  13 us
    all_to_all x2, waiting for transfers between devices, all_to_all(): return lax.all_to_all(value, axes, split_axis=0, concat_axis=0, tiled=True)  10.9 us
  transfers between devices with their start and end apart: 15, of which 9 were waited for; matrix products, arithmetic and copies ran while one was open for 4% of the time, Pallas kernels for 13%

profile of v2, /device:TPU:1, one launch (start us, length us, event | category | flops | bytes accessed | tf_op | source)
XLA Modules:
  0.0 363.1 jit_solution(13785459143305802491)
XLA Ops:
  8.6 1.8 divide_convert_fusion.2
  14.4 8.1 %pack.1 = (bf16[4112,128]{1,0:T(8,128)(2,1)S(1)}, bf16[4112,128]{1,0:T(8,128)(2,1)S(1)}, bf16[4112,128]{1,0:T(8,128)(2,1)S(1)}, bf16[4112,128]{1,0:T(8,128)(2,1)}, bf16[16,1040,128]{2,1,0:T(8,128)(2,1)}) custom-call(s32[2]{0:T(128)S(1)} %pad_add_fusion.me_ref, s32[96]{0:T(128)S(1)} %copy-done.5, s32[96]{0:T(128)S(1)} %bitcast.31, s32[96]{0:T(128)S(1)} %copy-done.7, ...), custom_call_target="tpu_custom_call" | custom-call | bytes 16777216 | tf_op jit(solution)/shard_map/pack/pallas_call | solution.py:89
  24.5 10.1 %all-to-all-start = ((bf16[16,1040,128]{2,1,0:T(8,128)(2,1)}), bf16[16,1040,128]{2,1,0:T(8,128)(2,1)}, u32[]{:S(2)}, u32[]{:S(2)}) async-start(bf16[16,1040,128]{2,1,0:T(8,128)(2,1)} %get-tuple-element.18), calls=%async_computation | async-start | bytes 8519680 | tf_op jit(solution)/shard_map/all_to_all | solution.py:201
  34.7 2.8 collective-permute-start.2
  41.7 26.9 %collective-permute-done.2.rest_3_ = bf16[4112,128]{1,0:T(8,128)(2,1)S(1)} collective-permute-done((bf16[4112,128]{1,0:T(8,128)(2,1)}, bf16[4112,128]{1,0:T(8,128)(2,1)S(1)}, u32[]{:S(2)}, u32[]{:S(2)}) %collective-permute-start.2) | collective-permute-done | bytes 1052704 | tf_op jit(solution)/shard_map/ppermute | solution.py:243
  68.6 4.5 %collective-permute-start.5 = (bf16[512,256]{1,0:T(8,128)(2,1)S(1)}, bf16[512,256]{1,0:T(8,128)(2,1)}, u32[]{:S(2)}, u32[]{:S(2)}) collective-permute-start(bf16[512,256]{1,0:T(8,128)(2,1)S(1)} %copy-done.3), channel_id=1, source_target_pairs={{0,192},{64,0},{128,64},{192,128},{1,193},{65,1},{129,65},{193,129... | collective-permute-start | bytes 786440 | tf_op jit(solution)/shard_map/ppermute | solution.py:242
  73.1 30.8 %collective-permute-done.rest_1_ = bf16[4112,128]{1,0:T(8,128)(2,1)S(1)} collective-permute-done((bf16[4112,128]{1,0:T(8,128)(2,1)}, bf16[4112,128]{1,0:T(8,128)(2,1)S(1)}, u32[]{:S(2)}, u32[]{:S(2)}) %collective-permute-start) | collective-permute-done | bytes 1052704 | tf_op jit(solution)/shard_map/ppermute | solution.py:243
  105.5 7.2 %all-gather.4.cloned.1.call-done = bf16[8192,256]{1,0:T(8,128)(2,1)} async-done(((bf16[512,256]{1,0:T(8,128)(2,1)}), bf16[8192,256]{1,0:T(8,128)(2,1)}) %all-gather.4.cloned.1.call-update) | async-done | bytes 4194320 | tf_op jit(solution)/shard_map/all_gather | solution.py:252
  112.7 1.7 collective-permute-done.4
  116.3 12.0 %products.2 = (f32[32,128,256]{2,1,0:T(8,128)}, bf16[32,128,256]{2,1,0:T(8,128)(2,1)}) custom-call(s32[128]{0:T(128)S(1)} %copy-done.4, s32[4]{0:T(128)S(1)} %iota_multiply_fusion.1.base_ref.place_ref, s32[4]{0:T(128)S(1)} %iota_multiply_fusion.1.base_ref.place_ref, bf16[4112,128]{1,0:T(8,128)(2,1)S(1)} %get-tuple-element.19.rest_0_, ...), custom_call_target="tpu_custom_call" | custom-call | flops 1073741824 | bytes 12582912 | tf_op jit(solution)/shard_map/products/pallas_call | solution.py:180
  129.7 4.0 %collective-permute-done.6 = bf16[32,128,256]{2,1,0:T(8,128)(2,1)S(1)} collective-permute-done((bf16[32,128,256]{2,1,0:T(8,128)(2,1)}, bf16[32,128,256]{2,1,0:T(8,128)(2,1)S(1)}, u32[]{:S(2)}, u32[]{:S(2)}) %collective-permute-start.6) | collective-permute-done | bytes 2097184 | tf_op jit(solution)/shard_map/ppermute | solution.py:256
  133.7 5.0 %convert_add_fusion.1 = f32[32,128,256]{2,1,0:T(8,128)} fusion(f32[32,128,256]{2,1,0:T(8,128)} %get-tuple-element.24, bf16[32,128,256]{2,1,0:T(8,128)(2,1)S(1)} %collective-permute-done.6), kind=kLoop, calls=%fused_computation.2 | loop fusion | flops 2097152 | bytes 10485760 | tf_op jit(solution)/shard_map/add | solution.py:257
  139.3 53.3 %reduce-scatter.3.cloned.1.call-done = f32[512,256]{1,0:T(8,128)} async-done(((f32[4096,256]{1,0:T(8,128)}), f32[512,256]{1,0:T(8,128)}) %reduce-scatter.3.cloned.1.call-update) | async-done | bytes 524304 | tf_op jit(solution)/shard_map/reduce_scatter | solution.py:259
  196.0 14.8 %back_products.1 = (f32[32,128,256]{2,1,0:T(8,128)}, bf16[32,128,256]{2,1,0:T(8,128)(2,1)S(1)}) custom-call(s32[128]{0:T(128)S(1)} %reshape.66.lab_ref, s32[16]{0:T(128)S(1)} %fusion.1.base_ref, s32[1]{0:T(128)} %constant.52.clone.1.place_ref, bf16[16,1040,128]{2,1,0:T(8,128)(2,1)} %all-to-all-done.rest_0_, bf16[64,128,256]{2,1,0:T(8,128)(2,1)} %bitcast.35), custom_call_target="tpu_custom_call" | custom-call | flops 1073741824 | bytes 12582912 | tf_op jit(solution)/shard_map/back_products/pallas_call | solution.py:180
  211.6 4.2 %collective-permute-done.7 = bf16[32,128,256]{2,1,0:T(8,128)(2,1)S(1)} collective-permute-done((bf16[32,128,256]{2,1,0:T(8,128)(2,1)S(1)}, bf16[32,128,256]{2,1,0:T(8,128)(2,1)S(1)}, u32[]{:S(2)}, u32[]{:S(2)}) %collective-permute-start.7) | collective-permute-done | bytes 2097184 | tf_op jit(solution)/shard_map/ppermute | solution.py:271
  215.7 5.1 %convert_add_fusion = f32[32,128,256]{2,1,0:T(8,128)} fusion(f32[32,128,256]{2,1,0:T(8,128)} %get-tuple-element.29, bf16[32,128,256]{2,1,0:T(8,128)(2,1)S(1)} %collective-permute-done.7), kind=kLoop, calls=%fused_computation.1 | loop fusion | flops 2097152 | bytes 10485760 | tf_op jit(solution)/shard_map/add | solution.py:272
  220.8 15.4 %all-gather.6.cloned.1.call-done = bf16[8192,256]{1,0:T(8,128)(2,1)} async-done(((bf16[512,256]{1,0:T(8,128)(2,1)}), bf16[8192,256]{1,0:T(8,128)(2,1)}) %all-gather.6.cloned.1.call-update) | async-done | bytes 4194320 | tf_op jit(solution)/shard_map/all_gather | solution.py:263
  236.3 11.9 %products.3 = bf16[64,128,256]{2,1,0:T(8,128)(2,1)S(1)} custom-call(s32[128]{0:T(128)S(1)} %reshape.66.lab_ref, s32[16]{0:T(128)S(1)} %iota_multiply_fusion.base_ref, s32[1]{0:T(128)} %constant.52.clone.1.place_ref, bf16[16,1040,128]{2,1,0:T(8,128)(2,1)} %all-to-all-done.rest_0_, bf16[64,128,256]{2,1,0:T(8,128)(2,1)} %bitcast.36), custom_call_target="tpu_custom_call" | custom-call | flops 1073741824 | bytes 12582912 | tf_op jit(solution)/shard_map/products/pallas_call | solution.py:180
  248.2 56.8 %all_to_all.25 = bf16[16,512,256]{2,1,0:T(8,128)(2,1)S(1)} all-to-all(bf16[16,512,256]{2,1,0:T(8,128)(2,1)S(1)} %bitcast.29), channel_id=1, replica_groups=mesh['y'=4,'z'=8,'c'=2,'x'=4] {'y','x'}, dimensions={0} | all-to-all | bytes 8388608 | tf_op jit(solution)/shard_map/all_to_all | solution.py:201
  308.2 17.3 %all_to_all.26 = f32[16,16,256]{2,1,0:T(8,128)S(1)} all-to-all(f32[16,16,256]{2,1,0:T(8,128)S(1)} %bitcast.37), channel_id=1, replica_groups=mesh['y'=4,'z'=8,'c'=2,'x'=4] {'z','c'}, dimensions={0} | all-to-all | bytes 524288 | tf_op jit(solution)/shard_map/all_to_all | solution.py:201
  325.5 11.3 %all_to_all.27 = f32[16,16,256]{2,1,0:T(8,128)S(1)} all-to-all(f32[16,16,256]{2,1,0:T(8,128)S(1)} %broadcast_in_dim.8), channel_id=1, replica_groups=mesh['y'=4,'z'=8,'c'=2,'x'=4] {'y','x'}, dimensions={0} | all-to-all | bytes 524288 | tf_op jit(solution)/shard_map/all_to_all | solution.py:201
  337.5 4.3 %all-to-all-start.4 = ((f32[16,16,256]{2,1,0:T(8,128)}), f32[16,16,256]{2,1,0:T(8,128)S(1)}, u32[]{:S(2)}, u32[]{:S(2)}) async-start(f32[16,16,256]{2,1,0:T(8,128)} %broadcast_in_dim.9), calls=%async_computation.6 | async-start | bytes 524288 | tf_op jit(solution)/shard_map/all_to_all | solution.py:201
  342.8 10.9 %all-to-all-done.4 = f32[16,16,256]{2,1,0:T(8,128)S(1)} async-done(((f32[16,16,256]{2,1,0:T(8,128)}), f32[16,16,256]{2,1,0:T(8,128)S(1)}, u32[]{:S(2)}, u32[]{:S(2)}) %all-to-all-start.4) | async-done | bytes 262176 | tf_op jit(solution)/shard_map/all_to_all | solution.py:201
  353.7 2.3 copy.18
  (79 shorter events, 26.8 us)
Async XLA Ops:
  7.2 186.7 %copy-start = (bf16[256,256]{1,0:T(8,128)(2,1)S(1)}, bf16[256,256]{1,0:T(8,128)(2,1)}, u32[]{:S(2)}) copy-start(bf16[256,256]{1,0:T(8,128)(2,1)} %param.22) | copy-start | bytes 393220
  7.2 105.5 %all-gather.4.cloned.1.call-start = ((), (), s32[]{:S(2)}) async-start(), calls=%async_computation.7 | async-start | bytes 4456448 | tf_op jit(solution)/shard_map/all_gather | solution.py:252
  22.5 1.0 copy-start.11
  23.5 1.0 copy-start.12
  24.5 14.0 %copy-start.3 = (bf16[512,256]{1,0:T(8,128)(2,1)S(1)}, bf16[512,256]{1,0:T(8,128)(2,1)}, u32[]{:S(2)}) copy-start(bf16[512,256]{1,0:T(8,128)(2,1)} %param.13) | copy-start | bytes 786436
  24.5 114.1 %all-to-all-start = ((bf16[16,1040,128]{2,1,0:T(8,128)(2,1)}), bf16[16,1040,128]{2,1,0:T(8,128)(2,1)}, u32[]{:S(2)}, u32[]{:S(2)}) async-start(bf16[16,1040,128]{2,1,0:T(8,128)(2,1)} %get-tuple-element.18), calls=%async_computation | async-start | bytes 8519680 | tf_op jit(solution)/shard_map/all_to_all | solution.py:201
  34.6 158.1 %reduce-scatter.3.cloned.1.call-start = ((), (), s32[]{:S(2)}) async-start(), calls=%async_computation.8 | async-start | bytes 4718592 | tf_op jit(solution)/shard_map/reduce_scatter | solution.py:259
  34.7 33.9 %collective-permute-start.2 = (bf16[4112,128]{1,0:T(8,128)(2,1)}, bf16[4112,128]{1,0:T(8,128)(2,1)S(1)}, u32[]{:S(2)}, u32[]{:S(2)}) collective-permute-start(bf16[4112,128]{1,0:T(8,128)(2,1)} %get-tuple-element.22), channel_id=1, source_target_pairs={{0,192},{64,0},{128,64},{192,128},{1,193},{65,1},{129,65},{193,129... | collective-permute-start | bytes 3158024 | tf_op jit(solution)/shard_map/ppermute | solution.py:243
  37.5 35.6 %collective-permute-start.1 = (bf16[4112,128]{1,0:T(8,128)(2,1)}, bf16[4112,128]{1,0:T(8,128)(2,1)S(1)}, u32[]{:S(2)}, u32[]{:S(2)}) collective-permute-start(bf16[4112,128]{1,0:T(8,128)(2,1)} %copy-done.12), channel_id=1, source_target_pairs={{0,128},{64,192},{128,0},{192,64},{1,129},{65,193},{129,1},{193,65... | collective-permute-start | bytes 3158024 | tf_op jit(solution)/shard_map/ppermute | solution.py:243
  37.8 66.0 %collective-permute-start = (bf16[4112,128]{1,0:T(8,128)(2,1)}, bf16[4112,128]{1,0:T(8,128)(2,1)S(1)}, u32[]{:S(2)}, u32[]{:S(2)}) collective-permute-start(bf16[4112,128]{1,0:T(8,128)(2,1)} %copy-done.11), channel_id=1, source_target_pairs={{0,64},{64,128},{128,192},{192,0},{1,65},{65,129},{129,193},{193,1... | collective-permute-start | bytes 3158024 | tf_op jit(solution)/shard_map/ppermute | solution.py:243
  38.5 74.2 %collective-permute-start.3 = (bf16[512,256]{1,0:T(8,128)(2,1)S(1)}, bf16[512,256]{1,0:T(8,128)(2,1)}, u32[]{:S(2)}, u32[]{:S(2)}) collective-permute-start(bf16[512,256]{1,0:T(8,128)(2,1)S(1)} %copy-done.3), channel_id=1, source_target_pairs={{0,64},{64,128},{128,192},{192,0},{1,65},{65,129},{129,193},{193,1... | collective-permute-start | bytes 786440 | tf_op jit(solution)/shard_map/ppermute | solution.py:242
  40.1 74.2 %collective-permute-start.4 = (bf16[512,256]{1,0:T(8,128)(2,1)S(1)}, bf16[512,256]{1,0:T(8,128)(2,1)}, u32[]{:S(2)}, u32[]{:S(2)}) collective-permute-start(bf16[512,256]{1,0:T(8,128)(2,1)S(1)} %copy-done.3), channel_id=1, source_target_pairs={{0,128},{64,192},{128,0},{192,64},{1,129},{65,193},{129,1},{193,65... | collective-permute-start | bytes 786440 | tf_op jit(solution)/shard_map/ppermute | solution.py:242
  68.6 45.8 %collective-permute-start.5 = (bf16[512,256]{1,0:T(8,128)(2,1)S(1)}, bf16[512,256]{1,0:T(8,128)(2,1)}, u32[]{:S(2)}, u32[]{:S(2)}) collective-permute-start(bf16[512,256]{1,0:T(8,128)(2,1)S(1)} %copy-done.3), channel_id=1, source_target_pairs={{0,192},{64,0},{128,64},{192,128},{1,193},{65,1},{129,65},{193,129... | collective-permute-start | bytes 786440 | tf_op jit(solution)/shard_map/ppermute | solution.py:242
  103.9 1.0 copy-start.1
  114.4 1.2 copy-start.2
  115.6 0.7 copy-start.4
  128.3 5.4 %collective-permute-start.6 = (bf16[32,128,256]{2,1,0:T(8,128)(2,1)}, bf16[32,128,256]{2,1,0:T(8,128)(2,1)S(1)}, u32[]{:S(2)}, u32[]{:S(2)}) collective-permute-start(bf16[32,128,256]{2,1,0:T(8,128)(2,1)} %get-tuple-element.25), channel_id=1, source_target_pairs={{0,4},{4,0},{1,5},{5,1},{2,6},{6,2},{3,7},{7,3},{8,12},{12,8},{9,1... | collective-permute-start | bytes 6291464 | tf_op jit(solution)/shard_map/ppermute | solution.py:256
  138.6 0.7 copy-start.15
  138.7 97.5 %all-gather.6.cloned.1.call-start = ((), (), s32[]{:S(2)}) async-start(), calls=%async_computation.9 | async-start | bytes 4456448 | tf_op jit(solution)/shard_map/all_gather | solution.py:263
  194.9 111.7 %reduce-scatter.5.cloned.1.call-start = ((), (), s32[]{:S(2)}) async-start(), calls=%async_computation.11 | async-start | bytes 4718592 | tf_op jit(solution)/shard_map/reduce_scatter | solution.py:274
  210.8 4.9 %collective-permute-start.7 = (bf16[32,128,256]{2,1,0:T(8,128)(2,1)S(1)}, bf16[32,128,256]{2,1,0:T(8,128)(2,1)S(1)}, u32[]{:S(2)}, u32[]{:S(2)}) collective-permute-start(bf16[32,128,256]{2,1,0:T(8,128)(2,1)S(1)} %get-tuple-element.30), channel_id=1, source_target_pairs={{0,4},{4,0},{1,5},{5,1},{2,6},{6,2},{3,7},{7,3},{8,12},{12,8},{9,1... | collective-permute-start | bytes 6291464 | tf_op jit(solution)/shard_map/ppermute | solution.py:271
  236.2 105.6 %all-gather.8.cloned.1.call-start = ((), (), s32[]{:S(2)}) async-start(), calls=%async_computation.10 | async-start | bytes 1310720 | tf_op jit(solution)/shard_map/all_gather | solution.py:290
  305.1 0.7 copy-start.14
  337.5 16.2 %all-to-all-start.4 = ((f32[16,16,256]{2,1,0:T(8,128)}), f32[16,16,256]{2,1,0:T(8,128)S(1)}, u32[]{:S(2)}, u32[]{:S(2)}) async-start(f32[16,16,256]{2,1,0:T(8,128)} %broadcast_in_dim.9), calls=%async_computation.6 | async-start | bytes 524288 | tf_op jit(solution)/shard_map/all_to_all | solution.py:201
  (7 other events, 4.5 us)
Sparse Core Ops, SparseCore 0:
  11.0 101.6 all-gather.3
  138.8 53.8 reduce-scatter.2
  195.1 41.0 all-gather.5
  238.6 53.6 reduce-scatter.4
  306.8 21.1 all-gather.7

commit v3 on v2

--- a/solution.py
+++ b/solution.py
@@ -23,43 +23,37 @@
 ANY_SPEC = pl.BlockSpec(memory_space=pl.ANY)
 
 
-def pack(me, first, second):
+def pack(indices, first, second):
     parts = (first, second)
     shapes = [(p["groups"], p["cap"] * TILE + LAB, TILE) for p in parts]
 
-    def kernel(me_ref, *rest):
-        given = (rest[0:4], rest[4:8])
+    def kernel(index_ref, *rest):
         groups1 = shapes[0][0]
-        outs1, out2 = rest[8 : 8 + groups1], rest[8 + groups1]
-        tiles1, tiles2, room1, room2, count, labels, in_sems, sems1, sem2 = rest[9 + groups1 : 18 + groups1]
-        indices = rest[18 + groups1 : 24 + groups1]
-        refs = (indices[0:3], indices[3:6])
-        small = [
-            pltpu.make_async_copy(given[i // 3][i % 3], indices[i], in_sems.at[2 + i]) for i in range(6)
+        outs1, out2 = rest[2 : 2 + groups1], rest[2 + groups1]
+        tiles1, tiles2, room1, room2, count, labels, in_sems, sems1, sem2 = rest[3 + groups1 :]
+        loads = [
+            pltpu.make_async_copy(rest[1], tiles2, in_sems.at[1]),
+            pltpu.make_async_copy(rest[0], tiles1, in_sems.at[0]),
         ]
-        loads = [
-            pltpu.make_async_copy(given[1][3], tiles2, in_sems.at[1]),
-            pltpu.make_async_copy(given[0][3], tiles1, in_sems.at[0]),
-        ]
-        for load in small + loads:
+        for load in loads:
             load.start()
+        own_y, own_c = index_ref[6 * TILES], index_ref[6 * TILES + 1]
         lane = lax.broadcasted_iota(jnp.int32, (1, TILE), 1)
 
-        def lay(part, part_refs, tiles_ref, room):
-            source_ref, owner_ref, slot_ref = part_refs[:3]
+        def lay(part, at, tiles_ref, room):
             groups, rows, _ = room.shape
             for g in range(groups):
                 count[g] = 0
             labels[...] = jnp.full(labels.shape, float(BLK * part["dummy"]), F32)
 
             def step(t, carry):
-                own = owner_ref[t]
-                g = part["group_of"](own, me_ref)
+                source, own, slot = (index_ref[at + i * TILES + t] for i in range(3))
+                g = part["group_of"](own, own_y)
                 rank = count[g]
                 count[g] = rank + 1
                 row = pl.multiple_of(rank * TILE, TILE)
                 room[g, pl.ds(row, TILE), :] = tiles_ref[t]
-                label = (BLK * part["block_of"](own, slot_ref[t], me_ref) + source_ref[t]).astype(F32)
+                label = (BLK * part["block_of"](own, slot, own_c) + source).astype(F32)
                 old = labels[pl.ds(g, 1), :]
                 labels[pl.ds(g, 1), :] = jnp.where(lane == rank, label, old)
                 return carry
@@ -69,14 +63,12 @@
                 labels[0:groups][:, None, :], (groups, LAB, TILE)
             ).astype(BF16)
 
-        for load in small:
-            load.wait()
         loads[0].wait()
-        lay(second, refs[1], tiles2, room2)
+        lay(second, 3 * TILES, tiles2, room2)
         copies = [pltpu.make_async_copy(room2, out2, sem2)]
         copies[0].start()
         loads[1].wait()
-        lay(first, refs[0], tiles1, room1)
+        lay(first, 0, tiles1, room1)
         for g in range(groups1):
             copies.append(pltpu.make_async_copy(room1.at[g], outs1[g], sems1.at[g]))
             copies[-1].start()
@@ -89,7 +81,7 @@
     outs = pl.pallas_call(
         kernel,
         out_shape=out_shape,
-        in_specs=[SMEM_SPEC] + [ANY_SPEC] * 8,
+        in_specs=[SMEM_SPEC, ANY_SPEC, ANY_SPEC],
         out_specs=[ANY_SPEC] * len(out_shape),
         scratch_shapes=[
             pltpu.VMEM((TILES, TILE, TILE), BF16),
@@ -98,15 +90,14 @@
             pltpu.VMEM(shapes[1], BF16),
             pltpu.SMEM((most,), jnp.int32),
             pltpu.VMEM((most, TILE), F32),
-            pltpu.SemaphoreType.DMA((8,)),
+            pltpu.SemaphoreType.DMA((2,)),
             pltpu.SemaphoreType.DMA((shapes[0][0],)),
             pltpu.SemaphoreType.DMA,
-        ]
-        + [pltpu.SMEM((TILES,), jnp.int32)] * 6,
+        ],
         compiler_params=pltpu.CompilerParams(vmem_limit_bytes=VMEM_LIMIT),
         cost_estimate=pl.CostEstimate(flops=0, bytes_accessed=16 * 1024 * 1024, transcendentals=0),
         name="pack",
-    )(me, *first["args"], *second["args"])
+    )(indices, first["tiles"], second["tiles"])
     return outs[:-1], outs[-1]
 
 
@@ -114,21 +105,22 @@
     return received[..., cap * TILE, :cap].astype(jnp.int32)
 
 
-def products(labels, bases, received, blocks, places, cap, count, split_out, flip):
+def products(labels, bases, received, blocks, order, cap, count, split_out, flip):
     many = isinstance(received, (list, tuple))
     tiles_in = list(received) if many else [received]
     groups = len(received) if many else received.shape[0]
     n_out = (split_out > 0) + (split_out < count)
     n_in, n_blocks = len(tiles_in), len(blocks)
     blocks = [b.reshape(-1, TILE, F) for b in blocks]
+    starts = [sum(b.shape[0] for b in blocks[:i]) for i in range(len(blocks))]
     total = sum(b.shape[0] for b in blocks)
 
-    def kernel(lab_ref, base_ref, place_ref, *rest):
+    def kernel(lab_ref, base_ref, order_ref, *rest):
         tile_refs, block_refs = rest[:n_in], rest[n_in : n_in + n_blocks]
         outs = rest[n_in + n_blocks : n_in + n_blocks + n_out]
         acc, room, tiles, sems, tile_sems = rest[n_in + n_blocks + n_out :]
         loads = [
-            pltpu.make_async_copy(ref, room.at[pl.ds(place_ref[i], blocks[i].shape[0])], sems.at[i])
+            pltpu.make_async_copy(ref, room.at[pl.ds(starts[i], blocks[i].shape[0])], sems.at[i])
             for i, ref in enumerate(block_refs)
         ]
         rows = cap * TILE
@@ -149,7 +141,7 @@
             if flip:
                 empty = far >= total
                 into = jnp.where(empty, count, near)
-                block = room[jnp.where(empty, 0, far)]
+                block = room[order_ref[jnp.where(empty, 0, far)]]
                 term = lax.dot_general(tile, block, (((0,), (0,)), ((), ())), preferred_element_type=F32)
             else:
                 into = far
@@ -194,7 +186,7 @@
             flops=2 * groups * cap * TILE * TILE * F, bytes_accessed=12 * 1024 * 1024, transcendentals=0
         ),
         name="back_products" if flip else "products",
-    )(labels, bases, places, *tiles_in, *blocks)
+    )(labels, bases, order, *tiles_in, *blocks)
 
 
 def all_to_all(value, axes):
@@ -217,45 +209,55 @@
     cotangent,
 ):
     y, z, c, x = (lax.axis_index(a) for a in ALL)
-    me = jnp.stack([y, c]).astype(jnp.int32)
+    indices = jnp.concatenate(
+        [
+            tile1_source, tile1_owner[:, 0], tile1_slot,
+            tile2_source, tile2_owner[:, 0], tile2_slot,
+            jnp.stack([y, c]).astype(jnp.int32),
+        ]
+    )
     near1, near2 = NY, NZ * NC
     cap1, cap2 = TILE // near1, TILE // near2
     both1 = NC * NZ * BLK
     send1, send2 = pack(
-        me,
+        indices,
         dict(
-            args=(tile1_source, tile1_owner[:, 0], tile1_slot, tile1_values),
+            tiles=tile1_values,
             groups=near1, cap=cap1, dummy=both1,
-            group_of=lambda own, me_ref: (own // (NZ * NC) - me_ref[0] + NY) % NY,
-            block_of=lambda own, slot, me_ref: (((own + me_ref[1]) % NC) * NZ + (own // NC) % NZ) * BLK + slot,
+            group_of=lambda own, own_y: (own // (NZ * NC) - own_y + NY) % NY,
+            block_of=lambda own, slot, own_c: (((own + own_c) % NC) * NZ + (own // NC) % NZ) * BLK + slot,
         ),
         dict(
-            args=(tile2_source, tile2_owner[:, 0], tile2_slot, tile2_values),
+            tiles=tile2_values,
             groups=near2, cap=cap2, dummy=NY * UGRP,
-            group_of=lambda own, me_ref: own % (NZ * NC),
-            block_of=lambda own, slot, me_ref: (own // (NZ * NC)) * UGRP + slot,
+            group_of=lambda own, own_y: own % (NZ * NC),
+            block_of=lambda own, slot, own_c: (own // (NZ * NC)) * UGRP + slot,
         ),
     )
-    got1, near_items = [send1[0]], [items]
+    rows = user_degree.shape[0] // NX
+    zero = jnp.zeros((1,), jnp.int32)
+    send1, send2, user_degree, cotangent = lax.optimization_barrier((send1, send2, user_degree, cotangent))
+    degree = lax.dynamic_slice_in_dim(user_degree, x * rows, rows)[:, None].astype(F32)
+    cot = lax.dynamic_slice_in_dim(cotangent, x * rows, rows)
+    scaled_grad = (cot.astype(F32) / degree).astype(BF16)
+    blocks1, got1 = [jnp.concatenate([items, scaled_grad])], [send1[0]]
     for dy in range(1, NY):
         pairs = [(a, (a + dy) % NY) for a in range(NY)]
-        near_items.append(lax.ppermute(items, "y", pairs))
+        blocks1.append(lax.ppermute(blocks1[0], "y", pairs))
         got1.append(lax.ppermute(send1[dy], "y", pairs))
+    near_grad = lax.all_gather(
+        jnp.concatenate([scaled_grad] + [part[BLK * TILE :] for part in blocks1[1:]]), "x", axis=0, tiled=True
+    )
+    target = jnp.arange(NY * UGRP, dtype=jnp.int32)
+    part = target % UGRP
+    order3 = (part // BLK) * UGRP + ((y - target // UGRP + NY) % NY) * BLK + part % BLK
     labels1 = jnp.concatenate([labels_of(part, cap1) for part in got1])
-    places1 = jnp.arange(NY, dtype=jnp.int32) * BLK
+    bases1 = jnp.arange(NY, dtype=jnp.int32) * (2 * BLK)
     got2 = all_to_all(send2, ("z", "c"))
-    rows = user_degree.shape[0] // NX
-    degree = lax.dynamic_slice_in_dim(user_degree, x * rows, rows)[:, None].astype(F32)
-    zero = jnp.zeros((1,), jnp.int32)
-    cot = lax.dynamic_slice_in_dim(cotangent, x * rows, rows)
-    scaled_grad = (cot.astype(F32) / degree).astype(BF16)
-    near_grad = lax.all_gather(scaled_grad, ("y", "x"), axis=0, tiled=True)
-
-    near_grad, labels1 = lax.optimization_barrier((near_grad, labels1))
-    mine, other = products(labels1, places1, got1, near_items, places1, cap1, both1, both1 // NC, False)
+    mine, other = products(labels1, bases1, got1, blocks1, zero, cap1, both1, both1 // NC, False)
     other = lax.ppermute(other, "c", [(0, 1), (1, 0)])
     part1 = (mine + other.astype(F32)).reshape(-1, F)
-    got2, part1 = lax.optimization_barrier((got2, part1))
+    got2, near_grad, part1 = lax.optimization_barrier((got2, near_grad, part1))
     summed = lax.psum_scatter(part1, "z", scatter_dimension=0, tiled=True)
     bundle_emb = (summed / bundle_degree[:, None].astype(F32)).astype(BF16)
     mixed = jnp.dot(bundle_emb, weight, preferred_element_type=F32)
@@ -266,7 +268,7 @@
     senders = jnp.arange(near2, dtype=jnp.int32)
     halves = ((senders + c) % NC) * (NZ * BLK) + (senders // NC) * BLK
     mine, other = products(
-        labels2, halves, got2, [near_grad], zero, cap2, NC * NZ * BLK, NZ * BLK, True
+        labels2, halves, got2, [near_grad], order3, cap2, NC * NZ * BLK, NZ * BLK, True
     )
     other = lax.ppermute(other, "c", [(0, 1), (1, 0)])
     both = (mine + other.astype(F32)).reshape(-1, F)

time: 364 us -> 357 us (0.981)
  local copies, waits for them, and re-layouts: 13.8 us -> 8.32 us
  waiting for transfers between devices: 154 us -> 159 us
  starting transfers between devices: 28.4 us -> 24.2 us
    ppermute x3, waiting for transfers between devices: 1.68 us -> 22.2 us  [local(): blocks1.append(lax.ppermute(blocks1[0], 'y', pairs))]
    ppermute x3, waiting for transfers between devices: 57.6 us -> 48.6 us  [local(): got1.append(lax.ppermute(send1[dy], 'y', pairs))]
    all_gather x1, waiting for transfers between devices: 7.17 us -> 0.01 us  [local(): lax.all_gather(jnp.concatenate([scaled_grad] + [part[BLK * TILE:] for par...]
    unnamed x34 -> x16, local copies, waits for them, and re-layouts: 13 us -> 6.58 us
  transfers between devices with their start and end apart: 15 -> 15, of which waited for: 9 -> 10; matrix products, arithmetic and copies ran while one was open for 4% -> 5% of each run, Pallas kernels for 13% -> 11%
where the time goes in v3:
time: 357 us
  waiting for transfers between devices  159 us (45%)
  blocking collectives  85.4 us (24%)
  Pallas kernels  45.8 us (13%)
  starting transfers between devices  24.2 us (7%)
  other arithmetic  17.7 us (5%)
  between operations  14 us (4%)
  local copies, waits for them, and re-layouts  8.32 us (2%)
    all_to_all x3, blocking collectives, all_to_all(): return lax.all_to_all(value, axes, split_axis=0, concat_axis=0, tiled=True)  85.4 us
    reduce_scatter x1, waiting for transfers between devices, local(): summed = lax.psum_scatter(part1, 'z', scatter_dimension=0, tiled=True)  53.7 us
    ppermute x3, waiting for transfers between devices, local(): got1.append(lax.ppermute(send1[dy], 'y', pairs))  48.6 us
    pallas_call x3, Pallas kernels, products(): pl.pallas_call(kernel, out_shape=out_shape, in_specs=[SMEM_SPEC, SMEM_SPE...  38.5 us
    ppermute x3, waiting for transfers between devices, local(): blocks1.append(lax.ppermute(blocks1[0], 'y', pairs))  22.2 us
    all_gather x1, waiting for transfers between devices, local(): near_act = lax.all_gather(activated, ('z', 'c'), axis=0, tiled=True)  15.4 us
    all_to_all x2, starting transfers between devices, all_to_all(): return lax.all_to_all(value, axes, split_axis=0, concat_axis=0, tiled=True)  14.4 us
    all_to_all x2, waiting for transfers between devices, all_to_all(): return lax.all_to_all(value, axes, split_axis=0, concat_axis=0, tiled=True)  10.9 us
  transfers between devices with their start and end apart: 15, of which 10 were waited for; matrix products, arithmetic and copies ran while one was open for 5% of the time, Pallas kernels for 11%

profile of v3, /device:TPU:1, one launch (start us, length us, event | category | flops | bytes accessed | tf_op | source)
XLA Modules:
  0.0 356.8 jit_solution(8696421114588354772)
XLA Ops:
  8.0 7.3 %pack.1 = (bf16[4112,128]{1,0:T(8,128)(2,1)S(1)}, bf16[4112,128]{1,0:T(8,128)(2,1)S(1)}, bf16[4112,128]{1,0:T(8,128)(2,1)S(1)}, bf16[4112,128]{1,0:T(8,128)(2,1)S(1)}, bf16[16,1040,128]{2,1,0:T(8,128)(2,1)}) custom-call(s32[578]{0:T(1024)S(1)} %concatenate.14.index_ref, bf16[96,128,128]{2,1,0:T(8,128)(2,1)} %rest_0_.1, bf16[96,128,128]{2,1,0:T(8,128)(2,1)} %rest_1_.1), custom_call_target="tpu_custom_call" | custom-call | bytes 16777216 | tf_op jit(solution)/shard_map/pack/pallas_call | solution.py:81
  18.3 10.1 %all-to-all-start = ((bf16[16,1040,128]{2,1,0:T(8,128)(2,1)}), bf16[16,1040,128]{2,1,0:T(8,128)(2,1)}, u32[]{:S(2)}, u32[]{:S(2)}) async-start(bf16[16,1040,128]{2,1,0:T(8,128)(2,1)} %get-tuple-element.29), calls=%async_computation | async-start | bytes 8519680 | tf_op jit(solution)/shard_map/all_to_all | solution.py:193
  31.8 2.6 collective-permute-start.1
  35.5 9.8 %collective-permute-done = bf16[1024,256]{1,0:T(8,128)(2,1)S(1)} collective-permute-done((bf16[1024,256]{1,0:T(8,128)(2,1)S(1)}, bf16[1024,256]{1,0:T(8,128)(2,1)S(1)}, u32[]{:S(2)}, u32[]{:S(2)}) %collective-permute-start) | collective-permute-done | bytes 524320 | tf_op jit(solution)/shard_map/ppermute | solution.py:246
  45.3 12.3 %collective-permute-done.1 = bf16[1024,256]{1,0:T(8,128)(2,1)S(1)} collective-permute-done((bf16[1024,256]{1,0:T(8,128)(2,1)S(1)}, bf16[1024,256]{1,0:T(8,128)(2,1)S(1)}, u32[]{:S(2)}, u32[]{:S(2)}) %collective-permute-start.1) | collective-permute-done | bytes 524320 | tf_op jit(solution)/shard_map/ppermute | solution.py:246
  58.8 2.4 collective-permute-start.5
  61.9 23.0 %collective-permute-done.5.rest_3_ = bf16[4112,128]{1,0:T(8,128)(2,1)S(1)} collective-permute-done((bf16[4112,128]{1,0:T(8,128)(2,1)}, bf16[4112,128]{1,0:T(8,128)(2,1)S(1)}, u32[]{:S(2)}, u32[]{:S(2)}) %collective-permute-start.5) | collective-permute-done | bytes 1052704 | tf_op jit(solution)/shard_map/ppermute | solution.py:247
  85.0 2.3 collective-permute-done.4.rest_2_
  87.3 23.3 %collective-permute-done.3.rest_1_ = bf16[4112,128]{1,0:T(8,128)(2,1)S(1)} collective-permute-done((bf16[4112,128]{1,0:T(8,128)(2,1)}, bf16[4112,128]{1,0:T(8,128)(2,1)S(1)}, u32[]{:S(2)}, u32[]{:S(2)}) %collective-permute-start.3) | collective-permute-done | bytes 1052704 | tf_op jit(solution)/shard_map/ppermute | solution.py:247
  110.6 11.8 %products.2 = (f32[32,128,256]{2,1,0:T(8,128)}, bf16[32,128,256]{2,1,0:T(8,128)(2,1)}) custom-call(s32[128]{0:T(128)S(1)} %maximum_convert_fusion.lab_ref, s32[4]{0:T(128)S(1)} %iota_multiply_fusion.1.base_ref, s32[1]{0:T(128)} %constant.101.clone.1.order_ref, bf16[4112,128]{1,0:T(8,128)(2,1)S(1)} %get-tuple-element.32.rest_0_, ...), custom_call_target="tpu_custom_call" | custom-call | flops 1073741824 | bytes 12582912 | tf_op jit(solution)/shard_map/products/pallas_call | solution.py:172
  123.0 4.0 %collective-permute-done.6 = bf16[32,128,256]{2,1,0:T(8,128)(2,1)S(1)} collective-permute-done((bf16[32,128,256]{2,1,0:T(8,128)(2,1)}, bf16[32,128,256]{2,1,0:T(8,128)(2,1)S(1)}, u32[]{:S(2)}, u32[]{:S(2)}) %collective-permute-start.6) | collective-permute-done | bytes 2097184 | tf_op jit(solution)/shard_map/ppermute | solution.py:258
  127.0 4.9 %convert_add_fusion.1 = f32[32,128,256]{2,1,0:T(8,128)} fusion(f32[32,128,256]{2,1,0:T(8,128)} %get-tuple-element.36, bf16[32,128,256]{2,1,0:T(8,128)(2,1)S(1)} %collective-permute-done.6), kind=kLoop, calls=%fused_computation.2 | loop fusion | flops 2097152 | bytes 10485760 | tf_op jit(solution)/shard_map/add | solution.py:259
  132.7 53.7 %reduce-scatter.3.cloned.1.call-done = f32[512,256]{1,0:T(8,128)} async-done(((f32[4096,256]{1,0:T(8,128)}), f32[512,256]{1,0:T(8,128)}) %reduce-scatter.3.cloned.1.call-update) | async-done | bytes 524304 | tf_op jit(solution)/shard_map/reduce_scatter | solution.py:261
  189.8 14.8 %back_products.1 = (f32[32,128,256]{2,1,0:T(8,128)}, bf16[32,128,256]{2,1,0:T(8,128)(2,1)S(1)}) custom-call(s32[128]{0:T(128)S(1)} %reshape.66.lab_ref, s32[16]{0:T(128)S(1)} %fusion.2.base_ref, s32[64]{0:T(128)S(1)} %fusion.order_ref, bf16[16,1040,128]{2,1,0:T(8,128)(2,1)} %all-to-all-done.rest_0_, bf16[64,128,256]{2,1,0:T(8,128)(2,1)} %bitcast.36), custom_call_target="tpu_custom_call" | custom-call | flops 1073741824 | bytes 12582912 | tf_op jit(solution)/shard_map/back_products/pallas_call | solution.py:172
  205.3 4.2 %collective-permute-done.7 = bf16[32,128,256]{2,1,0:T(8,128)(2,1)S(1)} collective-permute-done((bf16[32,128,256]{2,1,0:T(8,128)(2,1)S(1)}, bf16[32,128,256]{2,1,0:T(8,128)(2,1)S(1)}, u32[]{:S(2)}, u32[]{:S(2)}) %collective-permute-start.7) | collective-permute-done | bytes 2097184 | tf_op jit(solution)/shard_map/ppermute | solution.py:273
  209.4 5.0 %convert_add_fusion = f32[32,128,256]{2,1,0:T(8,128)} fusion(f32[32,128,256]{2,1,0:T(8,128)} %get-tuple-element.41, bf16[32,128,256]{2,1,0:T(8,128)(2,1)S(1)} %collective-permute-done.7), kind=kLoop, calls=%fused_computation.1 | loop fusion | flops 2097152 | bytes 10485760 | tf_op jit(solution)/shard_map/add | solution.py:274
  214.5 15.4 %all-gather.6.cloned.1.call-done = bf16[8192,256]{1,0:T(8,128)(2,1)} async-done(((bf16[512,256]{1,0:T(8,128)(2,1)}), bf16[8192,256]{1,0:T(8,128)(2,1)}) %all-gather.6.cloned.1.call-update) | async-done | bytes 4194320 | tf_op jit(solution)/shard_map/all_gather | solution.py:265
  230.0 11.9 %products.3 = bf16[64,128,256]{2,1,0:T(8,128)(2,1)S(1)} custom-call(s32[128]{0:T(128)S(1)} %reshape.66.lab_ref, s32[16]{0:T(128)S(1)} %iota_multiply_fusion.base_ref, s32[1]{0:T(128)} %constant.101.clone.1.order_ref, bf16[16,1040,128]{2,1,0:T(8,128)(2,1)} %all-to-all-done.rest_0_, bf16[64,128,256]{2,1,0:T(8,128)(2,1)} %bitcast.37), custom_call_target="tpu_custom_call" | custom-call | flops 1073741824 | bytes 12582912 | tf_op jit(solution)/shard_map/products/pallas_call | solution.py:172
  241.9 56.9 %all_to_all.25 = bf16[16,512,256]{2,1,0:T(8,128)(2,1)S(1)} all-to-all(bf16[16,512,256]{2,1,0:T(8,128)(2,1)S(1)} %bitcast.29), channel_id=1, replica_groups=mesh['y'=4,'z'=8,'c'=2,'x'=4] {'y','x'}, dimensions={0} | all-to-all | bytes 8388608 | tf_op jit(solution)/shard_map/all_to_all | solution.py:193
  301.8 17.2 %all_to_all.26 = f32[16,16,256]{2,1,0:T(8,128)S(1)} all-to-all(f32[16,16,256]{2,1,0:T(8,128)S(1)} %bitcast.38), channel_id=1, replica_groups=mesh['y'=4,'z'=8,'c'=2,'x'=4] {'z','c'}, dimensions={0} | all-to-all | bytes 524288 | tf_op jit(solution)/shard_map/all_to_all | solution.py:193
  319.1 11.3 %all_to_all.27 = f32[16,16,256]{2,1,0:T(8,128)S(1)} all-to-all(f32[16,16,256]{2,1,0:T(8,128)S(1)} %broadcast_in_dim.8), channel_id=1, replica_groups=mesh['y'=4,'z'=8,'c'=2,'x'=4] {'y','x'}, dimensions={0} | all-to-all | bytes 524288 | tf_op jit(solution)/shard_map/all_to_all | solution.py:193
  331.1 4.3 %all-to-all-start.4 = ((f32[16,16,256]{2,1,0:T(8,128)}), f32[16,16,256]{2,1,0:T(8,128)S(1)}, u32[]{:S(2)}, u32[]{:S(2)}) async-start(f32[16,16,256]{2,1,0:T(8,128)} %broadcast_in_dim.9), calls=%async_computation.6 | async-start | bytes 524288 | tf_op jit(solution)/shard_map/all_to_all | solution.py:193
  336.4 10.9 %all-to-all-done.4 = f32[16,16,256]{2,1,0:T(8,128)S(1)} async-done(((f32[16,16,256]{2,1,0:T(8,128)}), f32[16,16,256]{2,1,0:T(8,128)S(1)}, u32[]{:S(2)}, u32[]{:S(2)}) %all-to-all-start.4) | async-done | bytes 262176 | tf_op jit(solution)/shard_map/all_to_all | solution.py:193
  347.3 2.3 copy.18
  (67 shorter events, 20.9 us)
Async XLA Ops:
  7.2 180.4 %copy-start = (bf16[256,256]{1,0:T(8,128)(2,1)S(1)}, bf16[256,256]{1,0:T(8,128)(2,1)}, u32[]{:S(2)}) copy-start(bf16[256,256]{1,0:T(8,128)(2,1)} %param.22) | copy-start | bytes 393220
  15.3 1.0 copy-start.1
  16.4 1.0 copy-start.2
  17.3 1.0 copy-start.3
  18.3 12.0 %copy-start.5 = (bf16[512,256]{1,0:T(8,128)(2,1)S(1)}, bf16[512,256]{1,0:T(8,128)(2,1)}, u32[]{:S(2)}) copy-start(bf16[512,256]{1,0:T(8,128)(2,1)} %param.13) | copy-start | bytes 786436
  18.3 113.6 %all-to-all-start = ((bf16[16,1040,128]{2,1,0:T(8,128)(2,1)}), bf16[16,1040,128]{2,1,0:T(8,128)(2,1)}, u32[]{:S(2)}, u32[]{:S(2)}) async-start(bf16[16,1040,128]{2,1,0:T(8,128)(2,1)} %get-tuple-element.29), calls=%async_computation | async-start | bytes 8519680 | tf_op jit(solution)/shard_map/all_to_all | solution.py:193
  28.5 103.5 %all-gather.4.cloned.1.call-start = ((), (), s32[]{:S(2)}) async-start(), calls=%async_computation.7 | async-start | bytes 5242880 | tf_op jit(solution)/shard_map/all_gather | solution.py:248
  30.4 14.9 %collective-permute-start = (bf16[1024,256]{1,0:T(8,128)(2,1)S(1)}, bf16[1024,256]{1,0:T(8,128)(2,1)S(1)}, u32[]{:S(2)}, u32[]{:S(2)}) collective-permute-start(bf16[1024,256]{1,0:T(8,128)(2,1)S(1)} %pad_maximum_fusion.1), channel_id=1, source_target_pairs={{0,64},{64,128},{128,192},{192,0},{1,65},{65,129},{129,193},{193,1... | collective-permute-start | bytes 1572872 | tf_op jit(solution)/shard_map/ppermute | solution.py:246
  31.8 25.9 %collective-permute-start.1 = (bf16[1024,256]{1,0:T(8,128)(2,1)S(1)}, bf16[1024,256]{1,0:T(8,128)(2,1)S(1)}, u32[]{:S(2)}, u32[]{:S(2)}) collective-permute-start(bf16[1024,256]{1,0:T(8,128)(2,1)S(1)} %pad_maximum_fusion.1), channel_id=1, source_target_pairs={{0,128},{64,192},{128,0},{192,64},{1,129},{65,193},{129,1},{193,65... | collective-permute-start | bytes 1572872 | tf_op jit(solution)/shard_map/ppermute | solution.py:246
  34.4 23.3 %collective-permute-start.2 = (bf16[1024,256]{1,0:T(8,128)(2,1)S(1)}, bf16[1024,256]{1,0:T(8,128)(2,1)S(1)}, u32[]{:S(2)}, u32[]{:S(2)}) collective-permute-start(bf16[1024,256]{1,0:T(8,128)(2,1)S(1)} %pad_maximum_fusion.1), channel_id=1, source_target_pairs={{0,192},{64,0},{128,64},{192,128},{1,193},{65,1},{129,65},{193,129... | collective-permute-start | bytes 1572872 | tf_op jit(solution)/shard_map/ppermute | solution.py:246
  58.8 127.6 %reduce-scatter.3.cloned.1.call-start = ((), (), s32[]{:S(2)}) async-start(), calls=%async_computation.8 | async-start | bytes 4718592 | tf_op jit(solution)/shard_map/reduce_scatter | solution.py:261
  58.8 26.1 %collective-permute-start.5 = (bf16[4112,128]{1,0:T(8,128)(2,1)}, bf16[4112,128]{1,0:T(8,128)(2,1)S(1)}, u32[]{:S(2)}, u32[]{:S(2)}) collective-permute-start(bf16[4112,128]{1,0:T(8,128)(2,1)} %copy-done.3), channel_id=1, source_target_pairs={{0,192},{64,0},{128,64},{192,128},{1,193},{65,1},{129,65},{193,129... | collective-permute-start | bytes 3158024 | tf_op jit(solution)/shard_map/ppermute | solution.py:247
  61.2 26.0 %collective-permute-start.4 = (bf16[4112,128]{1,0:T(8,128)(2,1)}, bf16[4112,128]{1,0:T(8,128)(2,1)S(1)}, u32[]{:S(2)}, u32[]{:S(2)}) collective-permute-start(bf16[4112,128]{1,0:T(8,128)(2,1)} %copy-done.2), channel_id=1, source_target_pairs={{0,128},{64,192},{128,0},{192,64},{1,129},{65,193},{129,1},{193,65... | collective-permute-start | bytes 3158024 | tf_op jit(solution)/shard_map/ppermute | solution.py:247
  61.4 49.1 %collective-permute-start.3 = (bf16[4112,128]{1,0:T(8,128)(2,1)}, bf16[4112,128]{1,0:T(8,128)(2,1)S(1)}, u32[]{:S(2)}, u32[]{:S(2)}) collective-permute-start(bf16[4112,128]{1,0:T(8,128)(2,1)} %copy-done.1), channel_id=1, source_target_pairs={{0,64},{64,128},{128,192},{192,0},{1,65},{65,129},{129,193},{193,1... | collective-permute-start | bytes 3158024 | tf_op jit(solution)/shard_map/ppermute | solution.py:247
  85.0 25.7 %copy-start.4 = (bf16[4112,128]{1,0:T(8,128)(2,1)}, bf16[4112,128]{1,0:T(8,128)(2,1)S(1)}, u32[]{:S(2)}) copy-start(bf16[4112,128]{1,0:T(8,128)(2,1)S(1)} %collective-permute-done.5.rest_3_) | copy-start | bytes 3158020
  122.4 4.6 %collective-permute-start.6 = (bf16[32,128,256]{2,1,0:T(8,128)(2,1)}, bf16[32,128,256]{2,1,0:T(8,128)(2,1)S(1)}, u32[]{:S(2)}, u32[]{:S(2)}) collective-permute-start(bf16[32,128,256]{2,1,0:T(8,128)(2,1)} %get-tuple-element.37), channel_id=1, source_target_pairs={{0,4},{4,0},{1,5},{5,1},{2,6},{6,2},{3,7},{7,3},{8,12},{12,8},{9,1... | collective-permute-start | bytes 6291464 | tf_op jit(solution)/shard_map/ppermute | solution.py:258
  132.0 0.7 copy-start.6
  132.0 97.9 %all-gather.6.cloned.1.call-start = ((), (), s32[]{:S(2)}) async-start(), calls=%async_computation.9 | async-start | bytes 4456448 | tf_op jit(solution)/shard_map/all_gather | solution.py:265
  188.6 111.7 %reduce-scatter.5.cloned.1.call-start = ((), (), s32[]{:S(2)}) async-start(), calls=%async_computation.11 | async-start | bytes 4718592 | tf_op jit(solution)/shard_map/reduce_scatter | solution.py:276
  204.6 4.8 %collective-permute-start.7 = (bf16[32,128,256]{2,1,0:T(8,128)(2,1)S(1)}, bf16[32,128,256]{2,1,0:T(8,128)(2,1)S(1)}, u32[]{:S(2)}, u32[]{:S(2)}) collective-permute-start(bf16[32,128,256]{2,1,0:T(8,128)(2,1)S(1)} %get-tuple-element.42), channel_id=1, source_target_pairs={{0,4},{4,0},{1,5},{5,1},{2,6},{6,2},{3,7},{7,3},{8,12},{12,8},{9,1... | collective-permute-start | bytes 6291464 | tf_op jit(solution)/shard_map/ppermute | solution.py:273
  229.9 105.5 %all-gather.8.cloned.1.call-start = ((), (), s32[]{:S(2)}) async-start(), calls=%async_computation.10 | async-start | bytes 1310720 | tf_op jit(solution)/shard_map/all_gather | solution.py:292
  331.1 16.1 %all-to-all-start.4 = ((f32[16,16,256]{2,1,0:T(8,128)}), f32[16,16,256]{2,1,0:T(8,128)S(1)}, u32[]{:S(2)}, u32[]{:S(2)}) async-start(f32[16,16,256]{2,1,0:T(8,128)} %broadcast_in_dim.9), calls=%async_computation.6 | async-start | bytes 524288 | tf_op jit(solution)/shard_map/all_to_all | solution.py:193
Sparse Core Ops, SparseCore 0:
  58.9 51.6 all-gather.3
  132.1 54.2 reduce-scatter.2
  188.8 41.0 all-gather.5
  232.3 53.6 reduce-scatter.4
  300.4 21.1 all-gather.7

commit v4 on v3

--- a/solution.py
+++ b/solution.py
@@ -94,7 +94,7 @@
             pltpu.SemaphoreType.DMA((shapes[0][0],)),
             pltpu.SemaphoreType.DMA,
         ],
-        compiler_params=pltpu.CompilerParams(vmem_limit_bytes=VMEM_LIMIT),
+        compiler_params=pltpu.CompilerParams(vmem_limit_bytes=60 * 1024 * 1024),
         cost_estimate=pl.CostEstimate(flops=0, bytes_accessed=16 * 1024 * 1024, transcendentals=0),
         name="pack",
     )(indices, first["tiles"], second["tiles"])
@@ -240,21 +240,19 @@
     degree = lax.dynamic_slice_in_dim(user_degree, x * rows, rows)[:, None].astype(F32)
     cot = lax.dynamic_slice_in_dim(cotangent, x * rows, rows)
     scaled_grad = (cot.astype(F32) / degree).astype(BF16)
-    blocks1, got1 = [jnp.concatenate([items, scaled_grad])], [send1[0]]
+    near = lax.all_gather(jnp.concatenate([items, scaled_grad]), "y", axis=0, tiled=True)
+    column = near.reshape(NY, -1, F)[:, BLK * TILE :]
+    near_grad = lax.all_gather(column.reshape(-1, F), "x", axis=0, tiled=True)
+    got1 = [send1[0]]
     for dy in range(1, NY):
-        pairs = [(a, (a + dy) % NY) for a in range(NY)]
-        blocks1.append(lax.ppermute(blocks1[0], "y", pairs))
-        got1.append(lax.ppermute(send1[dy], "y", pairs))
-    near_grad = lax.all_gather(
-        jnp.concatenate([scaled_grad] + [part[BLK * TILE :] for part in blocks1[1:]]), "x", axis=0, tiled=True
-    )
+        got1.append(lax.ppermute(send1[dy], "y", [(a, (a + dy) % NY) for a in range(NY)]))
     target = jnp.arange(NY * UGRP, dtype=jnp.int32)
     part = target % UGRP
-    order3 = (part // BLK) * UGRP + ((y - target // UGRP + NY) % NY) * BLK + part % BLK
+    order3 = (part // BLK) * UGRP + (target // UGRP) * BLK + part % BLK
     labels1 = jnp.concatenate([labels_of(part, cap1) for part in got1])
-    bases1 = jnp.arange(NY, dtype=jnp.int32) * (2 * BLK)
+    bases1 = ((y - jnp.arange(NY, dtype=jnp.int32) + NY) % NY) * (2 * BLK)
     got2 = all_to_all(send2, ("z", "c"))
-    mine, other = products(labels1, bases1, got1, blocks1, zero, cap1, both1, both1 // NC, False)
+    mine, other = products(labels1, bases1, got1, [near], zero, cap1, both1, both1 // NC, False)
     other = lax.ppermute(other, "c", [(0, 1), (1, 0)])
     part1 = (mine + other.astype(F32)).reshape(-1, F)
     got2, near_grad, part1 = lax.optimization_barrier((got2, near_grad, part1))

time: 357 us -> 359 us (level)
  starting transfers between devices: 24.2 us -> 18.5 us
  waiting for transfers between devices: 159 us -> 164 us
    all_gather x1 -> x2, waiting for transfers between devices: 0.01 us -> 27.2 us  [the longest x1 27.2 us: local(): lax.all_gather(jnp.concatenate([items, scaled_grad]), 'y', axis=0, tiled=...]
    ppermute x6 -> x3, waiting for transfers between devices: 70.8 us -> 47.5 us  [local(): lax.ppermute(send1[dy], 'y', [(a, (a + dy) % NY) for a in range(NY)])]
    ppermute x6 -> x3, starting transfers between devices: 8.14 us -> 2.41 us  [local(): lax.ppermute(send1[dy], 'y', [(a, (a + dy) % NY) for a in range(NY)])]
  transfers between devices with their start and end apart: 15 -> 13, of which waited for: 10 -> 9; matrix products, arithmetic and copies ran while one was open for 5% -> 5% of each run, Pallas kernels for 11% -> 11%
where the time goes in v4:
time: 359 us; the launch traced here: 358 us
  waiting for transfers between devices  164 us (46%)
  blocking collectives  85.2 us (24%)
  Pallas kernels  48.5 us (14%)
  starting transfers between devices  18.5 us (5%)
  other arithmetic  17.4 us (5%)
  between operations  14.3 us (4%)
  local copies, waits for them, and re-layouts  8.09 us (2%)
    all_to_all x3, blocking collectives, all_to_all(): return lax.all_to_all(value, axes, split_axis=0, concat_axis=0, tiled=True)  85.2 us
    reduce_scatter x1, waiting for transfers between devices, local(): summed = lax.psum_scatter(part1, 'z', scatter_dimension=0, tiled=True)  54.6 us
    ppermute x3, waiting for transfers between devices, local(): lax.ppermute(send1[dy], 'y', [(a, (a + dy) % NY) for a in range(NY)])  47.5 us
    pallas_call x3, Pallas kernels, products(): pl.pallas_call(kernel, out_shape=out_shape, in_specs=[SMEM_SPEC, SMEM_SPE...  39.2 us
    all_gather x1, waiting for transfers between devices, local(): lax.all_gather(jnp.concatenate([items, scaled_grad]), 'y', axis=0, tiled=...  27.2 us
    all_gather x1, waiting for transfers between devices, local(): near_act = lax.all_gather(activated, ('z', 'c'), axis=0, tiled=True)  16 us
    all_to_all x2, starting transfers between devices, all_to_all(): return lax.all_to_all(value, axes, split_axis=0, concat_axis=0, tiled=True)  14.4 us
    all_to_all x2, waiting for transfers between devices, all_to_all(): return lax.all_to_all(value, axes, split_axis=0, concat_axis=0, tiled=True)  10.9 us
  transfers between devices with their start and end apart: 13, of which 9 were waited for; matrix products, arithmetic and copies ran while one was open for 5% of the time, Pallas kernels for 11%

profile of v4, /device:TPU:1, one launch (start us, length us, event | category | flops | bytes accessed | tf_op | source)
XLA Modules:
  0.0 358.2 jit_solution(18062463642340958175)
XLA Ops:
  7.2 1.4 concatenate.11.index_ref
  8.6 9.2 %pack.1 = (bf16[4112,128]{1,0:T(8,128)(2,1)}, bf16[4112,128]{1,0:T(8,128)(2,1)}, bf16[4112,128]{1,0:T(8,128)(2,1)}, bf16[4112,128]{1,0:T(8,128)(2,1)}, bf16[16,1040,128]{2,1,0:T(8,128)(2,1)}) custom-call(s32[578]{0:T(1024)} %concatenate.11.index_ref, bf16[96,128,128]{2,1,0:T(8,128)(2,1)} %rest_0_.1, bf16[96,128,128]{2,1,0:T(8,128)(2,1)} %rest_1_.1), custom_call_target="tpu_custom_call" | custom-call | bytes 16777216 | tf_op jit(solution)/shard_map/pack/pallas_call | solution.py:81
  20.6 10.1 %all-to-all-start = ((bf16[16,1040,128]{2,1,0:T(8,128)(2,1)}), bf16[16,1040,128]{2,1,0:T(8,128)(2,1)}, u32[]{:S(2)}, u32[]{:S(2)}) async-start(bf16[16,1040,128]{2,1,0:T(8,128)(2,1)} %get-tuple-element.29), calls=%async_computation | async-start | bytes 8519680 | tf_op jit(solution)/shard_map/all_to_all | solution.py:193
  30.8 27.2 %all-gather.5.cloned.1.call-done = bf16[4096,256]{1,0:T(8,128)(2,1)} async-done(((bf16[1024,256]{1,0:T(8,128)(2,1)}), bf16[4096,256]{1,0:T(8,128)(2,1)}) %all-gather.5.cloned.1.call-update) | async-done | bytes 2097168 | tf_op jit(solution)/shard_map/all_gather | solution.py:243
  58.0 2.3 slice.24
  61.0 1.5 collective-permute-start.1
  62.8 22.1 %collective-permute-done.2.rest_3_ = bf16[4112,128]{1,0:T(8,128)(2,1)S(1)} collective-permute-done((bf16[4112,128]{1,0:T(8,128)(2,1)}, bf16[4112,128]{1,0:T(8,128)(2,1)S(1)}, u32[]{:S(2)}, u32[]{:S(2)}) %collective-permute-start.2) | collective-permute-done | bytes 1052704 | tf_op jit(solution)/shard_map/ppermute | solution.py:248
  84.8 1.6 collective-permute-done.1.rest_2_
  86.4 23.9 %collective-permute-done.rest_1_ = bf16[4112,128]{1,0:T(8,128)(2,1)S(1)} collective-permute-done((bf16[4112,128]{1,0:T(8,128)(2,1)S(1)}, bf16[4112,128]{1,0:T(8,128)(2,1)S(1)}, u32[]{:S(2)}, u32[]{:S(2)}) %collective-permute-start) | collective-permute-done | bytes 1052704 | tf_op jit(solution)/shard_map/ppermute | solution.py:248
  110.4 12.5 %products.2 = (f32[32,128,256]{2,1,0:T(8,128)}, bf16[32,128,256]{2,1,0:T(8,128)(2,1)}) custom-call(s32[128]{0:T(128)S(1)} %maximum_convert_fusion.lab_ref, s32[4]{0:T(128)S(1)} %fusion.5.base_ref, s32[1]{0:T(128)} %constant.107.clone.1.order_ref, bf16[4112,128]{1,0:T(8,128)(2,1)S(1)} %copy-done.1, bf16[4112,128]{1,0:T(8,128)(2,1)S(1)} %collective-permute-done.rest_1_, ...), custom_call_target="tpu_custom_call" | custom-call | flops 1073741824 | bytes 12582912 | tf_op jit(solution)/shard_map/products/pallas_call | solution.py:172
  123.3 4.0 %collective-permute-done.3 = bf16[32,128,256]{2,1,0:T(8,128)(2,1)S(1)} collective-permute-done((bf16[32,128,256]{2,1,0:T(8,128)(2,1)}, bf16[32,128,256]{2,1,0:T(8,128)(2,1)S(1)}, u32[]{:S(2)}, u32[]{:S(2)}) %collective-permute-start.3) | collective-permute-done | bytes 2097184 | tf_op jit(solution)/shard_map/ppermute | solution.py:256
  127.3 4.9 %convert_add_fusion.1 = f32[32,128,256]{2,1,0:T(8,128)} fusion(f32[32,128,256]{2,1,0:T(8,128)} %get-tuple-element.36, bf16[32,128,256]{2,1,0:T(8,128)(2,1)S(1)} %collective-permute-done.3), kind=kLoop, calls=%fused_computation.2 | loop fusion | flops 2097152 | bytes 10485760 | tf_op jit(solution)/shard_map/add | solution.py:257
  132.9 54.6 %reduce-scatter.3.cloned.1.call-done = f32[512,256]{1,0:T(8,128)} async-done(((f32[4096,256]{1,0:T(8,128)}), f32[512,256]{1,0:T(8,128)}) %reduce-scatter.3.cloned.1.call-update) | async-done | bytes 524304 | tf_op jit(solution)/shard_map/reduce_scatter | solution.py:259
  190.7 14.8 %back_products.1 = (f32[32,128,256]{2,1,0:T(8,128)}, bf16[32,128,256]{2,1,0:T(8,128)(2,1)S(1)}) custom-call(s32[128]{0:T(128)S(1)} %reshape.62.lab_ref, s32[16]{0:T(128)S(1)} %fusion.2.base_ref, s32[64]{0:T(128)S(1)} %fusion.order_ref, bf16[16,1040,128]{2,1,0:T(8,128)(2,1)} %all-to-all-done.rest_0_, bf16[64,128,256]{2,1,0:T(8,128)(2,1)} %bitcast.33), custom_call_target="tpu_custom_call" | custom-call | flops 1073741824 | bytes 12582912 | tf_op jit(solution)/shard_map/back_products/pallas_call | solution.py:172
  206.3 3.8 %collective-permute-done.4 = bf16[32,128,256]{2,1,0:T(8,128)(2,1)S(1)} collective-permute-done((bf16[32,128,256]{2,1,0:T(8,128)(2,1)S(1)}, bf16[32,128,256]{2,1,0:T(8,128)(2,1)S(1)}, u32[]{:S(2)}, u32[]{:S(2)}) %collective-permute-start.4) | collective-permute-done | bytes 2097184 | tf_op jit(solution)/shard_map/ppermute | solution.py:271
  210.0 5.0 %convert_add_fusion = f32[32,128,256]{2,1,0:T(8,128)} fusion(f32[32,128,256]{2,1,0:T(8,128)} %get-tuple-element.41, bf16[32,128,256]{2,1,0:T(8,128)(2,1)S(1)} %collective-permute-done.4), kind=kLoop, calls=%fused_computation.1 | loop fusion | flops 2097152 | bytes 10485760 | tf_op jit(solution)/shard_map/add | solution.py:272
  215.1 16.0 %all-gather.9.cloned.1.call-done = bf16[8192,256]{1,0:T(8,128)(2,1)} async-done(((bf16[512,256]{1,0:T(8,128)(2,1)}), bf16[8192,256]{1,0:T(8,128)(2,1)}) %all-gather.9.cloned.1.call-update) | async-done | bytes 4194320 | tf_op jit(solution)/shard_map/all_gather | solution.py:263
  231.3 11.9 %products.3 = bf16[64,128,256]{2,1,0:T(8,128)(2,1)S(1)} custom-call(s32[128]{0:T(128)S(1)} %reshape.62.lab_ref, s32[16]{0:T(128)S(1)} %iota_multiply_fusion.base_ref, s32[1]{0:T(128)} %constant.107.clone.1.order_ref, bf16[16,1040,128]{2,1,0:T(8,128)(2,1)} %all-to-all-done.rest_0_, bf16[64,128,256]{2,1,0:T(8,128)(2,1)} %bitcast.34), custom_call_target="tpu_custom_call" | custom-call | flops 1073741824 | bytes 12582912 | tf_op jit(solution)/shard_map/products/pallas_call | solution.py:172
  243.3 56.5 %all_to_all.25 = bf16[16,512,256]{2,1,0:T(8,128)(2,1)S(1)} all-to-all(bf16[16,512,256]{2,1,0:T(8,128)(2,1)S(1)} %bitcast.28), channel_id=1, replica_groups=mesh['y'=4,'z'=8,'c'=2,'x'=4] {'y','x'}, dimensions={0} | all-to-all | bytes 8388608 | tf_op jit(solution)/shard_map/all_to_all | solution.py:193
  302.8 17.4 %all_to_all.26 = f32[16,16,256]{2,1,0:T(8,128)S(1)} all-to-all(f32[16,16,256]{2,1,0:T(8,128)S(1)} %bitcast.36), channel_id=1, replica_groups=mesh['y'=4,'z'=8,'c'=2,'x'=4] {'z','c'}, dimensions={0} | all-to-all | bytes 524288 | tf_op jit(solution)/shard_map/all_to_all | solution.py:193
  320.2 11.2 %all_to_all.27 = f32[16,16,256]{2,1,0:T(8,128)S(1)} all-to-all(f32[16,16,256]{2,1,0:T(8,128)S(1)} %broadcast_in_dim.8), channel_id=1, replica_groups=mesh['y'=4,'z'=8,'c'=2,'x'=4] {'y','x'}, dimensions={0} | all-to-all | bytes 524288 | tf_op jit(solution)/shard_map/all_to_all | solution.py:193
  332.2 4.3 %all-to-all-start.4 = ((f32[16,16,256]{2,1,0:T(8,128)}), f32[16,16,256]{2,1,0:T(8,128)S(1)}, u32[]{:S(2)}, u32[]{:S(2)}) async-start(f32[16,16,256]{2,1,0:T(8,128)} %broadcast_in_dim.9), calls=%async_computation.6 | async-start | bytes 524288 | tf_op jit(solution)/shard_map/all_to_all | solution.py:193
  337.5 10.9 %all-to-all-done.4 = f32[16,16,256]{2,1,0:T(8,128)S(1)} async-done(((f32[16,16,256]{2,1,0:T(8,128)}), f32[16,16,256]{2,1,0:T(8,128)S(1)}, u32[]{:S(2)}, u32[]{:S(2)}) %all-to-all-start.4) | async-done | bytes 262176 | tf_op jit(solution)/shard_map/all_to_all | solution.py:193
  348.4 2.3 copy.18
  (59 shorter events, 14.6 us)
Async XLA Ops:
  7.2 181.5 %copy-start = (bf16[256,256]{1,0:T(8,128)(2,1)S(1)}, bf16[256,256]{1,0:T(8,128)(2,1)}, u32[]{:S(2)}) copy-start(bf16[256,256]{1,0:T(8,128)(2,1)} %param.22) | copy-start | bytes 393220
  7.2 50.8 %all-gather.5.cloned.1.call-start = ((), (), s32[]{:S(2)}) async-start(), calls=%async_computation.7 | async-start | bytes 2621440 | tf_op jit(solution)/shard_map/all_gather | solution.py:243
  8.6 11.1 %copy-start.2 = (bf16[512,256]{1,0:T(8,128)(2,1)S(1)}, bf16[512,256]{1,0:T(8,128)(2,1)}, u32[]{:S(2)}) copy-start(bf16[512,256]{1,0:T(8,128)(2,1)} %param.13) | copy-start | bytes 786436
  20.6 40.3 %copy-start.5 = (bf16[4112,128]{1,0:T(8,128)(2,1)S(1)}, bf16[4112,128]{1,0:T(8,128)(2,1)}, u32[]{:S(2)}) copy-start(bf16[4112,128]{1,0:T(8,128)(2,1)} %get-tuple-element.34) | copy-start | bytes 3158020
  20.6 111.6 %all-to-all-start = ((bf16[16,1040,128]{2,1,0:T(8,128)(2,1)}), bf16[16,1040,128]{2,1,0:T(8,128)(2,1)}, u32[]{:S(2)}, u32[]{:S(2)}) async-start(bf16[16,1040,128]{2,1,0:T(8,128)(2,1)} %get-tuple-element.29), calls=%async_computation | async-start | bytes 8519680 | tf_op jit(solution)/shard_map/all_to_all | solution.py:193
  30.8 31.7 %copy-start.4 = (bf16[4112,128]{1,0:T(8,128)(2,1)S(1)}, bf16[4112,128]{1,0:T(8,128)(2,1)}, u32[]{:S(2)}) copy-start(bf16[4112,128]{1,0:T(8,128)(2,1)} %get-tuple-element.33) | copy-start | bytes 3158020
  30.8 32.0 %copy-start.1 = (bf16[4112,128]{1,0:T(8,128)(2,1)S(1)}, bf16[4112,128]{1,0:T(8,128)(2,1)}, u32[]{:S(2)}) copy-start(bf16[4112,128]{1,0:T(8,128)(2,1)} %get-tuple-element.32.rest_0_) | copy-start | bytes 3158020
  30.8 101.5 %all-gather.7.cloned.1.call-start = ((), (), s32[]{:S(2)}) async-start(), calls=%async_computation.8 | async-start | bytes 5242880 | tf_op jit(solution)/shard_map/all_gather | solution.py:245
  60.3 127.2 %reduce-scatter.3.cloned.1.call-start = ((), (), s32[]{:S(2)}) async-start(), calls=%async_computation.9 | async-start | bytes 4718592 | tf_op jit(solution)/shard_map/reduce_scatter | solution.py:259
  60.3 24.5 %collective-permute-start.2 = (bf16[4112,128]{1,0:T(8,128)(2,1)}, bf16[4112,128]{1,0:T(8,128)(2,1)S(1)}, u32[]{:S(2)}, u32[]{:S(2)}) collective-permute-start(bf16[4112,128]{1,0:T(8,128)(2,1)} %get-tuple-element.35), channel_id=1, source_target_pairs={{0,192},{64,0},{128,64},{192,128},{1,193},{65,1},{129,65},{193,129... | collective-permute-start | bytes 3158024 | tf_op jit(solution)/shard_map/ppermute | solution.py:248
  61.0 25.4 %collective-permute-start.1 = (bf16[4112,128]{1,0:T(8,128)(2,1)S(1)}, bf16[4112,128]{1,0:T(8,128)(2,1)S(1)}, u32[]{:S(2)}, u32[]{:S(2)}) collective-permute-start(bf16[4112,128]{1,0:T(8,128)(2,1)S(1)} %copy-done.5), channel_id=1, source_target_pairs={{0,128},{64,192},{128,0},{192,64},{1,129},{65,193},{129,1},{193,65... | collective-permute-start | bytes 3158024 | tf_op jit(solution)/shard_map/ppermute | solution.py:248
  62.4 47.9 %collective-permute-start = (bf16[4112,128]{1,0:T(8,128)(2,1)S(1)}, bf16[4112,128]{1,0:T(8,128)(2,1)S(1)}, u32[]{:S(2)}, u32[]{:S(2)}) collective-permute-start(bf16[4112,128]{1,0:T(8,128)(2,1)S(1)} %copy-done.4), channel_id=1, source_target_pairs={{0,64},{64,128},{128,192},{192,0},{1,65},{65,129},{129,193},{193,1... | collective-permute-start | bytes 3158024 | tf_op jit(solution)/shard_map/ppermute | solution.py:248
  122.9 4.5 %collective-permute-start.3 = (bf16[32,128,256]{2,1,0:T(8,128)(2,1)}, bf16[32,128,256]{2,1,0:T(8,128)(2,1)S(1)}, u32[]{:S(2)}, u32[]{:S(2)}) collective-permute-start(bf16[32,128,256]{2,1,0:T(8,128)(2,1)} %get-tuple-element.37), channel_id=1, source_target_pairs={{0,4},{4,0},{1,5},{5,1},{2,6},{6,2},{3,7},{7,3},{8,12},{12,8},{9,1... | collective-permute-start | bytes 6291464 | tf_op jit(solution)/shard_map/ppermute | solution.py:256
  132.2 0.7 copy-start.3
  132.3 98.8 %all-gather.9.cloned.1.call-start = ((), (), s32[]{:S(2)}) async-start(), calls=%async_computation.10 | async-start | bytes 4456448 | tf_op jit(solution)/shard_map/all_gather | solution.py:263
  189.8 111.5 %reduce-scatter.5.cloned.1.call-start = ((), (), s32[]{:S(2)}) async-start(), calls=%async_computation.12 | async-start | bytes 4718592 | tf_op jit(solution)/shard_map/reduce_scatter | solution.py:274
  205.5 4.5 %collective-permute-start.4 = (bf16[32,128,256]{2,1,0:T(8,128)(2,1)S(1)}, bf16[32,128,256]{2,1,0:T(8,128)(2,1)S(1)}, u32[]{:S(2)}, u32[]{:S(2)}) collective-permute-start(bf16[32,128,256]{2,1,0:T(8,128)(2,1)S(1)} %get-tuple-element.42), channel_id=1, source_target_pairs={{0,4},{4,0},{1,5},{5,1},{2,6},{6,2},{3,7},{7,3},{8,12},{12,8},{9,1... | collective-permute-start | bytes 6291464 | tf_op jit(solution)/shard_map/ppermute | solution.py:271
  231.1 105.5 %all-gather.11.cloned.1.call-start = ((), (), s32[]{:S(2)}) async-start(), calls=%async_computation.11 | async-start | bytes 1310720 | tf_op jit(solution)/shard_map/all_gather | solution.py:290
  332.2 16.2 %all-to-all-start.4 = ((f32[16,16,256]{2,1,0:T(8,128)}), f32[16,16,256]{2,1,0:T(8,128)S(1)}, u32[]{:S(2)}, u32[]{:S(2)}) async-start(f32[16,16,256]{2,1,0:T(8,128)} %broadcast_in_dim.9), calls=%async_computation.6 | async-start | bytes 524288 | tf_op jit(solution)/shard_map/all_to_all | solution.py:193
Sparse Core Ops, SparseCore 0:
  20.7 37.2 all-gather.4
  60.4 50.8 all-gather.6
  132.4 55.0 reduce-scatter.2
  189.9 41.1 all-gather.8
  233.4 53.4 reduce-scatter.4
  301.3 21.3 all-gather.10

commit v5 on v4

--- a/solution.py
+++ b/solution.py
@@ -241,11 +241,12 @@
     cot = lax.dynamic_slice_in_dim(cotangent, x * rows, rows)
     scaled_grad = (cot.astype(F32) / degree).astype(BF16)
     near = lax.all_gather(jnp.concatenate([items, scaled_grad]), "y", axis=0, tiled=True)
-    column = near.reshape(NY, -1, F)[:, BLK * TILE :]
-    near_grad = lax.all_gather(column.reshape(-1, F), "x", axis=0, tiled=True)
     got1 = [send1[0]]
     for dy in range(1, NY):
         got1.append(lax.ppermute(send1[dy], "y", [(a, (a + dy) % NY) for a in range(NY)]))
+    near, got1[2], got1[3] = lax.optimization_barrier((near, got1[2], got1[3]))
+    column = near.reshape(NY, -1, F)[:, BLK * TILE :]
+    near_grad = lax.all_gather(column.reshape(-1, F), "x", axis=0, tiled=True)
     target = jnp.arange(NY * UGRP, dtype=jnp.int32)
     part = target % UGRP
     order3 = (part // BLK) * UGRP + (target // UGRP) * BLK + part % BLK

time: 359 us -> 381 us (1.061)
  waiting for transfers between devices: 164 us -> 183 us
    ppermute x3, waiting for transfers between devices: 47.5 us -> 87 us  [local(): lax.ppermute(send1[dy], 'y', [(a, (a + dy) % NY) for a in range(NY)])]
    all_gather x1, waiting for transfers between devices: 27.2 us -> 0.01 us  [local(): lax.all_gather(jnp.concatenate([items, scaled_grad]), 'y', axis=0, tiled=...]
  transfers between devices with their start and end apart: 13 -> 13, of which waited for: 9 -> 9; matrix products, arithmetic and copies ran while one was open for 5% -> 5% of each run, Pallas kernels for 11% -> 10%
where the time goes in v5:
time: 381 us; the launch traced here: 380 us
  waiting for transfers between devices  183 us (48%)
  blocking collectives  85.4 us (22%)
  Pallas kernels  48.5 us (13%)
  starting transfers between devices  22.2 us (6%)
  other arithmetic  17.4 us (5%)
  between operations  14.3 us (4%)
  local copies, waits for them, and re-layouts  7.49 us (2%)
    ppermute x3, waiting for transfers between devices, local(): lax.ppermute(send1[dy], 'y', [(a, (a + dy) % NY) for a in range(NY)])  87 us
    all_to_all x3, blocking collectives, all_to_all(): return lax.all_to_all(value, axes, split_axis=0, concat_axis=0, tiled=True)  85.4 us
    reduce_scatter x1, waiting for transfers between devices, local(): summed = lax.psum_scatter(part1, 'z', scatter_dimension=0, tiled=True)  58.2 us
    pallas_call x3, Pallas kernels, products(): pl.pallas_call(kernel, out_shape=out_shape, in_specs=[SMEM_SPEC, SMEM_SPE...  39.3 us
    all_gather x1, waiting for transfers between devices, local(): near_act = lax.all_gather(activated, ('z', 'c'), axis=0, tiled=True)  16 us
    all_to_all x2, starting transfers between devices, all_to_all(): return lax.all_to_all(value, axes, split_axis=0, concat_axis=0, tiled=True)  14.3 us
    all_to_all x2, waiting for transfers between devices, all_to_all(): return lax.all_to_all(value, axes, split_axis=0, concat_axis=0, tiled=True)  10.9 us
    pallas_call x1, Pallas kernels, pack(): pl.pallas_call(kernel, out_shape=out_shape, in_specs=[SMEM_SPEC, ANY_SPEC...  9.28 us
  transfers between devices with their start and end apart: 13, of which 9 were waited for; matrix products, arithmetic and copies ran while one was open for 5% of the time, Pallas kernels for 10%

profile of v5, /device:TPU:1, one launch (start us, length us, event | category | flops | bytes accessed | tf_op | source)
XLA Modules:
  0.0 380.5 jit_solution(1714759772999192018)
XLA Ops:
  8.6 9.3 %pack.1 = (bf16[4112,128]{1,0:T(8,128)(2,1)}, bf16[4112,128]{1,0:T(8,128)(2,1)}, bf16[4112,128]{1,0:T(8,128)(2,1)}, bf16[4112,128]{1,0:T(8,128)(2,1)}, bf16[16,1040,128]{2,1,0:T(8,128)(2,1)}) custom-call(s32[578]{0:T(1024)} %concatenate.11.index_ref, bf16[96,128,128]{2,1,0:T(8,128)(2,1)} %rest_0_.1, bf16[96,128,128]{2,1,0:T(8,128)(2,1)} %rest_1_.1), custom_call_target="tpu_custom_call" | custom-call | bytes 16777216 | tf_op jit(solution)/shard_map/pack/pallas_call | solution.py:81
  20.6 10.0 %all-to-all-start = ((bf16[16,1040,128]{2,1,0:T(8,128)(2,1)}), bf16[16,1040,128]{2,1,0:T(8,128)(2,1)}, u32[]{:S(2)}, u32[]{:S(2)}) async-start(bf16[16,1040,128]{2,1,0:T(8,128)(2,1)} %get-tuple-element.32), calls=%async_computation | async-start | bytes 8519680 | tf_op jit(solution)/shard_map/all_to_all | solution.py:193
  30.7 3.0 collective-permute-start
  34.5 38.9 %collective-permute-done.rest_2_ = bf16[4112,128]{1,0:T(8,128)(2,1)S(1)} collective-permute-done((bf16[4112,128]{1,0:T(8,128)(2,1)}, bf16[4112,128]{1,0:T(8,128)(2,1)S(1)}, u32[]{:S(2)}, u32[]{:S(2)}) %collective-permute-start) | collective-permute-done | bytes 1052704 | tf_op jit(solution)/shard_map/ppermute | solution.py:246
  73.4 23.7 %collective-permute-done.1.rest_3_ = bf16[4112,128]{1,0:T(8,128)(2,1)S(1)} collective-permute-done((bf16[4112,128]{1,0:T(8,128)(2,1)}, bf16[4112,128]{1,0:T(8,128)(2,1)S(1)}, u32[]{:S(2)}, u32[]{:S(2)}) %collective-permute-start.1) | collective-permute-done | bytes 1052704 | tf_op jit(solution)/shard_map/ppermute | solution.py:246
  97.1 2.3 slice.24
  100.9 24.3 %collective-permute-done.2.rest_1_ = bf16[4112,128]{1,0:T(8,128)(2,1)S(1)} collective-permute-done((bf16[4112,128]{1,0:T(8,128)(2,1)}, bf16[4112,128]{1,0:T(8,128)(2,1)S(1)}, u32[]{:S(2)}, u32[]{:S(2)}) %collective-permute-start.2) | collective-permute-done | bytes 1052704 | tf_op jit(solution)/shard_map/ppermute | solution.py:246
  125.4 12.5 %products.2 = (f32[32,128,256]{2,1,0:T(8,128)}, bf16[32,128,256]{2,1,0:T(8,128)(2,1)}) custom-call(s32[128]{0:T(128)S(1)} %maximum_convert_fusion.lab_ref, s32[4]{0:T(128)S(1)} %fusion.5.base_ref, s32[1]{0:T(128)} %constant.107.clone.1.order_ref, bf16[4112,128]{1,0:T(8,128)(2,1)S(1)} %copy-done.1, bf16[4112,128]{1,0:T(8,128)(2,1)S(1)} %collective-permute-done.2.rest_1_, ...), custom_call_target="tpu_custom_call" | custom-call | flops 1073741824 | bytes 12582912 | tf_op jit(solution)/shard_map/products/pallas_call | solution.py:172
  137.9 1.6 collective-permute-start.3
  139.5 4.0 %collective-permute-done.3 = bf16[32,128,256]{2,1,0:T(8,128)(2,1)S(1)} collective-permute-done((bf16[32,128,256]{2,1,0:T(8,128)(2,1)}, bf16[32,128,256]{2,1,0:T(8,128)(2,1)S(1)}, u32[]{:S(2)}, u32[]{:S(2)}) %collective-permute-start.3) | collective-permute-done | bytes 2097184 | tf_op jit(solution)/shard_map/ppermute | solution.py:257
  143.5 4.9 %convert_add_fusion.1 = f32[32,128,256]{2,1,0:T(8,128)} fusion(f32[32,128,256]{2,1,0:T(8,128)} %get-tuple-element.42, bf16[32,128,256]{2,1,0:T(8,128)(2,1)S(1)} %collective-permute-done.3), kind=kLoop, calls=%fused_computation.2 | loop fusion | flops 2097152 | bytes 10485760 | tf_op jit(solution)/shard_map/add | solution.py:258
  148.4 2.9 all-gather.7.cloned.1.call-done
  151.4 58.2 %reduce-scatter.3.cloned.1.call-done = f32[512,256]{1,0:T(8,128)} async-done(((f32[4096,256]{1,0:T(8,128)}), f32[512,256]{1,0:T(8,128)}) %reduce-scatter.3.cloned.1.call-update) | async-done | bytes 524304 | tf_op jit(solution)/shard_map/reduce_scatter | solution.py:260
  212.8 14.8 %back_products.1 = (f32[32,128,256]{2,1,0:T(8,128)}, bf16[32,128,256]{2,1,0:T(8,128)(2,1)S(1)}) custom-call(s32[128]{0:T(128)S(1)} %reshape.62.lab_ref, s32[16]{0:T(128)S(1)} %fusion.2.base_ref, s32[64]{0:T(128)S(1)} %fusion.order_ref, bf16[16,1040,128]{2,1,0:T(8,128)(2,1)} %all-to-all-done.rest_0_, bf16[64,128,256]{2,1,0:T(8,128)(2,1)} %bitcast.33), custom_call_target="tpu_custom_call" | custom-call | flops 1073741824 | bytes 12582912 | tf_op jit(solution)/shard_map/back_products/pallas_call | solution.py:172
  228.3 3.8 collective-permute-done.4
  232.1 5.0 %convert_add_fusion = f32[32,128,256]{2,1,0:T(8,128)} fusion(f32[32,128,256]{2,1,0:T(8,128)} %get-tuple-element.47, bf16[32,128,256]{2,1,0:T(8,128)(2,1)S(1)} %collective-permute-done.4), kind=kLoop, calls=%fused_computation.1 | loop fusion | flops 2097152 | bytes 10485760 | tf_op jit(solution)/shard_map/add | solution.py:273
  237.1 16.0 %all-gather.9.cloned.1.call-done = bf16[8192,256]{1,0:T(8,128)(2,1)} async-done(((bf16[512,256]{1,0:T(8,128)(2,1)}), bf16[8192,256]{1,0:T(8,128)(2,1)}) %all-gather.9.cloned.1.call-update) | async-done | bytes 4194320 | tf_op jit(solution)/shard_map/all_gather | solution.py:264
  253.4 11.9 %products.3 = bf16[64,128,256]{2,1,0:T(8,128)(2,1)S(1)} custom-call(s32[128]{0:T(128)S(1)} %reshape.62.lab_ref, s32[16]{0:T(128)S(1)} %iota_multiply_fusion.base_ref, s32[1]{0:T(128)} %constant.107.clone.1.order_ref, bf16[16,1040,128]{2,1,0:T(8,128)(2,1)} %all-to-all-done.rest_0_, bf16[64,128,256]{2,1,0:T(8,128)(2,1)} %bitcast.34), custom_call_target="tpu_custom_call" | custom-call | flops 1073741824 | bytes 12582912 | tf_op jit(solution)/shard_map/products/pallas_call | solution.py:172
  265.4 56.5 %all_to_all.25 = bf16[16,512,256]{2,1,0:T(8,128)(2,1)S(1)} all-to-all(bf16[16,512,256]{2,1,0:T(8,128)(2,1)S(1)} %bitcast.28), channel_id=1, replica_groups=mesh['y'=4,'z'=8,'c'=2,'x'=4] {'y','x'}, dimensions={0} | all-to-all | bytes 8388608 | tf_op jit(solution)/shard_map/all_to_all | solution.py:193
  324.9 17.6 %all_to_all.26 = f32[16,16,256]{2,1,0:T(8,128)S(1)} all-to-all(f32[16,16,256]{2,1,0:T(8,128)S(1)} %bitcast.36), channel_id=1, replica_groups=mesh['y'=4,'z'=8,'c'=2,'x'=4] {'z','c'}, dimensions={0} | all-to-all | bytes 524288 | tf_op jit(solution)/shard_map/all_to_all | solution.py:193
  342.5 11.3 %all_to_all.27 = f32[16,16,256]{2,1,0:T(8,128)S(1)} all-to-all(f32[16,16,256]{2,1,0:T(8,128)S(1)} %broadcast_in_dim.8), channel_id=1, replica_groups=mesh['y'=4,'z'=8,'c'=2,'x'=4] {'y','x'}, dimensions={0} | all-to-all | bytes 524288 | tf_op jit(solution)/shard_map/all_to_all | solution.py:193
  354.5 4.3 %all-to-all-start.4 = ((f32[16,16,256]{2,1,0:T(8,128)}), f32[16,16,256]{2,1,0:T(8,128)S(1)}, u32[]{:S(2)}, u32[]{:S(2)}) async-start(f32[16,16,256]{2,1,0:T(8,128)} %broadcast_in_dim.9), calls=%async_computation.6 | async-start | bytes 524288 | tf_op jit(solution)/shard_map/all_to_all | solution.py:193
  359.8 10.9 %all-to-all-done.4 = f32[16,16,256]{2,1,0:T(8,128)S(1)} async-done(((f32[16,16,256]{2,1,0:T(8,128)}), f32[16,16,256]{2,1,0:T(8,128)S(1)}, u32[]{:S(2)}, u32[]{:S(2)}) %all-to-all-start.4) | async-done | bytes 262176 | tf_op jit(solution)/shard_map/all_to_all | solution.py:193
  370.7 2.3 copy.18
  (54 shorter events, 16.2 us)
Async XLA Ops:
  7.2 203.6 %copy-start = (bf16[256,256]{1,0:T(8,128)(2,1)S(1)}, bf16[256,256]{1,0:T(8,128)(2,1)}, u32[]{:S(2)}) copy-start(bf16[256,256]{1,0:T(8,128)(2,1)} %param.22) | copy-start | bytes 393220
  7.2 89.9 %all-gather.5.cloned.1.call-start = ((), (), s32[]{:S(2)}) async-start(), calls=%async_computation.7 | async-start | bytes 2621440 | tf_op jit(solution)/shard_map/all_gather | solution.py:243
  8.6 11.2 %copy-start.2 = (bf16[512,256]{1,0:T(8,128)(2,1)S(1)}, bf16[512,256]{1,0:T(8,128)(2,1)}, u32[]{:S(2)}) copy-start(bf16[512,256]{1,0:T(8,128)(2,1)} %param.13) | copy-start | bytes 786436
  20.6 127.8 %all-to-all-start = ((bf16[16,1040,128]{2,1,0:T(8,128)(2,1)}), bf16[16,1040,128]{2,1,0:T(8,128)(2,1)}, u32[]{:S(2)}, u32[]{:S(2)}) async-start(bf16[16,1040,128]{2,1,0:T(8,128)(2,1)} %get-tuple-element.32), calls=%async_computation | async-start | bytes 8519680 | tf_op jit(solution)/shard_map/all_to_all | solution.py:193
  30.6 70.3 %copy-start.1 = (bf16[4112,128]{1,0:T(8,128)(2,1)S(1)}, bf16[4112,128]{1,0:T(8,128)(2,1)}, u32[]{:S(2)}) copy-start(bf16[4112,128]{1,0:T(8,128)(2,1)} %get-tuple-element.38.rest_0_) | copy-start | bytes 3158020
  30.6 120.7 %all-gather.7.cloned.1.call-start = ((), (), s32[]{:S(2)}) async-start(), calls=%async_computation.8 | async-start | bytes 5242880 | tf_op jit(solution)/shard_map/all_gather | solution.py:249
  30.7 42.7 %collective-permute-start = (bf16[4112,128]{1,0:T(8,128)(2,1)}, bf16[4112,128]{1,0:T(8,128)(2,1)S(1)}, u32[]{:S(2)}, u32[]{:S(2)}) collective-permute-start(bf16[4112,128]{1,0:T(8,128)(2,1)} %get-tuple-element.35), channel_id=1, source_target_pairs={{0,128},{64,192},{128,0},{192,64},{1,129},{65,193},{129,1},{193,65... | collective-permute-start | bytes 3158024 | tf_op jit(solution)/shard_map/ppermute | solution.py:246
  33.7 63.4 %collective-permute-start.1 = (bf16[4112,128]{1,0:T(8,128)(2,1)}, bf16[4112,128]{1,0:T(8,128)(2,1)S(1)}, u32[]{:S(2)}, u32[]{:S(2)}) collective-permute-start(bf16[4112,128]{1,0:T(8,128)(2,1)} %get-tuple-element.36), channel_id=1, source_target_pairs={{0,192},{64,0},{128,64},{192,128},{1,193},{65,1},{129,65},{193,129... | collective-permute-start | bytes 3158024 | tf_op jit(solution)/shard_map/ppermute | solution.py:246
  99.4 110.2 %reduce-scatter.3.cloned.1.call-start = ((), (), s32[]{:S(2)}) async-start(), calls=%async_computation.9 | async-start | bytes 4718592 | tf_op jit(solution)/shard_map/reduce_scatter | solution.py:260
  99.4 25.8 %collective-permute-start.2 = (bf16[4112,128]{1,0:T(8,128)(2,1)}, bf16[4112,128]{1,0:T(8,128)(2,1)S(1)}, u32[]{:S(2)}, u32[]{:S(2)}) collective-permute-start(bf16[4112,128]{1,0:T(8,128)(2,1)} %get-tuple-element.39), channel_id=1, source_target_pairs={{0,64},{64,128},{128,192},{192,0},{1,65},{65,129},{129,193},{193,1... | collective-permute-start | bytes 3158024 | tf_op jit(solution)/shard_map/ppermute | solution.py:246
  137.9 5.6 %collective-permute-start.3 = (bf16[32,128,256]{2,1,0:T(8,128)(2,1)}, bf16[32,128,256]{2,1,0:T(8,128)(2,1)S(1)}, u32[]{:S(2)}, u32[]{:S(2)}) collective-permute-start(bf16[32,128,256]{2,1,0:T(8,128)(2,1)} %get-tuple-element.43), channel_id=1, source_target_pairs={{0,4},{4,0},{1,5},{5,1},{2,6},{6,2},{3,7},{7,3},{8,12},{12,8},{9,1... | collective-permute-start | bytes 6291464 | tf_op jit(solution)/shard_map/ppermute | solution.py:257
  148.4 3.0 copy-start.3
  151.3 101.8 %all-gather.9.cloned.1.call-start = ((), (), s32[]{:S(2)}) async-start(), calls=%async_computation.10 | async-start | bytes 4456448 | tf_op jit(solution)/shard_map/all_gather | solution.py:264
  211.9 111.5 %reduce-scatter.5.cloned.1.call-start = ((), (), s32[]{:S(2)}) async-start(), calls=%async_computation.12 | async-start | bytes 4718592 | tf_op jit(solution)/shard_map/reduce_scatter | solution.py:275
  227.6 4.5 %collective-permute-start.4 = (bf16[32,128,256]{2,1,0:T(8,128)(2,1)S(1)}, bf16[32,128,256]{2,1,0:T(8,128)(2,1)S(1)}, u32[]{:S(2)}, u32[]{:S(2)}) collective-permute-start(bf16[32,128,256]{2,1,0:T(8,128)(2,1)S(1)} %get-tuple-element.48), channel_id=1, source_target_pairs={{0,4},{4,0},{1,5},{5,1},{2,6},{6,2},{3,7},{7,3},{8,12},{12,8},{9,1... | collective-permute-start | bytes 6291464 | tf_op jit(solution)/shard_map/ppermute | solution.py:272
  253.2 105.7 %all-gather.11.cloned.1.call-start = ((), (), s32[]{:S(2)}) async-start(), calls=%async_computation.11 | async-start | bytes 1310720 | tf_op jit(solution)/shard_map/all_gather | solution.py:291
  354.5 16.2 %all-to-all-start.4 = ((f32[16,16,256]{2,1,0:T(8,128)}), f32[16,16,256]{2,1,0:T(8,128)S(1)}, u32[]{:S(2)}, u32[]{:S(2)}) async-start(f32[16,16,256]{2,1,0:T(8,128)} %broadcast_in_dim.9), calls=%async_computation.6 | async-start | bytes 524288 | tf_op jit(solution)/shard_map/all_to_all | solution.py:193
Sparse Core Ops, SparseCore 0:
  20.8 70.1 all-gather.4
  99.5 51.7 all-gather.6
  153.9 55.7 reduce-scatter.2
  212.0 41.1 all-gather.8
  255.5 53.6 reduce-scatter.4
  323.4 21.5 all-gather.10

commit v6 on v3

--- a/solution.py
+++ b/solution.py
@@ -234,31 +234,29 @@
             block_of=lambda own, slot, own_c: (own // (NZ * NC)) * UGRP + slot,
         ),
     )
+    zero = jnp.zeros((1,), jnp.int32)
+    along_y = [[(a, (a + dy) % NY) for a in range(NY)] for dy in range(NY)]
+    blocks1, got1 = [items], [send1[0]]
+    for dy in range(1, NY):
+        blocks1.append(lax.ppermute(items, "y", along_y[dy]))
+        got1.append(lax.ppermute(send1[dy], "y", along_y[dy]))
+    got1, user_degree, cotangent = lax.optimization_barrier((got1, user_degree, cotangent))
     rows = user_degree.shape[0] // NX
-    zero = jnp.zeros((1,), jnp.int32)
-    send1, send2, user_degree, cotangent = lax.optimization_barrier((send1, send2, user_degree, cotangent))
+    degrees = user_degree[:, None].astype(F32)
     degree = lax.dynamic_slice_in_dim(user_degree, x * rows, rows)[:, None].astype(F32)
-    cot = lax.dynamic_slice_in_dim(cotangent, x * rows, rows)
-    scaled_grad = (cot.astype(F32) / degree).astype(BF16)
-    blocks1, got1 = [jnp.concatenate([items, scaled_grad])], [send1[0]]
-    for dy in range(1, NY):
-        pairs = [(a, (a + dy) % NY) for a in range(NY)]
-        blocks1.append(lax.ppermute(blocks1[0], "y", pairs))
-        got1.append(lax.ppermute(send1[dy], "y", pairs))
-    near_grad = lax.all_gather(
-        jnp.concatenate([scaled_grad] + [part[BLK * TILE :] for part in blocks1[1:]]), "x", axis=0, tiled=True
-    )
+    scaled_grad = (cotangent.astype(F32) / degrees).astype(BF16)
+    near_grad = [scaled_grad] + [lax.ppermute(scaled_grad, "y", along_y[dy]) for dy in range(1, NY)]
     target = jnp.arange(NY * UGRP, dtype=jnp.int32)
-    part = target % UGRP
-    order3 = (part // BLK) * UGRP + ((y - target // UGRP + NY) % NY) * BLK + part % BLK
+    order3 = ((y - target // UGRP + NY) % NY) * UGRP + target % UGRP
     labels1 = jnp.concatenate([labels_of(part, cap1) for part in got1])
-    bases1 = jnp.arange(NY, dtype=jnp.int32) * (2 * BLK)
+    bases1 = jnp.arange(NY, dtype=jnp.int32) * BLK
     got2 = all_to_all(send2, ("z", "c"))
     mine, other = products(labels1, bases1, got1, blocks1, zero, cap1, both1, both1 // NC, False)
     other = lax.ppermute(other, "c", [(0, 1), (1, 0)])
     part1 = (mine + other.astype(F32)).reshape(-1, F)
-    got2, near_grad, part1 = lax.optimization_barrier((got2, near_grad, part1))
+    got2, part1 = lax.optimization_barrier((got2, part1))
     summed = lax.psum_scatter(part1, "z", scatter_dimension=0, tiled=True)
+    summed, near_grad, degree = lax.optimization_barrier((summed, near_grad, degree))
     bundle_emb = (summed / bundle_degree[:, None].astype(F32)).astype(BF16)
     mixed = jnp.dot(bundle_emb, weight, preferred_element_type=F32)
     activated = jax.nn.silu(mixed).astype(BF16)
@@ -268,7 +266,7 @@
     senders = jnp.arange(near2, dtype=jnp.int32)
     halves = ((senders + c) % NC) * (NZ * BLK) + (senders // NC) * BLK
     mine, other = products(
-        labels2, halves, got2, [near_grad], order3, cap2, NC * NZ * BLK, NZ * BLK, True
+        labels2, halves, got2, near_grad, order3, cap2, NC * NZ * BLK, NZ * BLK, True
     )
     other = lax.ppermute(other, "c", [(0, 1), (1, 0)])
     both = (mine + other.astype(F32)).reshape(-1, F)

time: 357 us -> 348 us (0.975)
  waiting for transfers between devices: 159 us -> 148 us
  starting transfers between devices: 24.2 us -> 28.9 us
    reduce_scatter x1, waiting for transfers between devices: 53.7 us -> 5.63 us  [local(): summed = lax.psum_scatter(part1, 'z', scatter_dimension=0, tiled=True)]
    ppermute x6 -> x9, waiting for transfers between devices: 70.8 us -> 97.5 us  [the longest x3 43.7 us: local(): lax.ppermute(scaled_grad, 'y', along_y[dy])]
    all_to_all x2, waiting for transfers between devices: 10.9 us -> 22.6 us  [all_to_all(): return lax.all_to_all(value, axes, split_axis=0, concat_axis=0, tiled=True)]
    ppermute x6 -> x9, starting transfers between devices: 8.14 us -> 12.9 us  [the longest x3 5.06 us: local(): lax.ppermute(scaled_grad, 'y', along_y[dy])]
  transfers between devices with their start and end apart: 15 -> 17, of which waited for: 10 -> 13; matrix products, arithmetic and copies ran while one was open for 5% -> 5% of each run, Pallas kernels for 11% -> 11%
where the time goes in v6:
time: 348 us; the launch traced here: 347 us
  waiting for transfers between devices  148 us (43%)
  blocking collectives  85.3 us (25%)
  Pallas kernels  46 us (13%)
  starting transfers between devices  28.9 us (8%)
  other arithmetic  15.8 us (5%)
  between operations  14 us (4%)
  local copies, waits for them, and re-layouts  6.42 us (2%)
    all_to_all x3, blocking collectives, all_to_all(): return lax.all_to_all(value, axes, split_axis=0, concat_axis=0, tiled=True)  85.3 us
    ppermute x3, waiting for transfers between devices, local(): lax.ppermute(scaled_grad, 'y', along_y[dy])  43.7 us
    ppermute x3, waiting for transfers between devices, local(): got1.append(lax.ppermute(send1[dy], 'y', along_y[dy]))  42.2 us
    pallas_call x3, Pallas kernels, products(): pl.pallas_call(kernel, out_shape=out_shape, in_specs=[SMEM_SPEC, SMEM_SPE...  38.7 us
    all_to_all x2, waiting for transfers between devices, all_to_all(): return lax.all_to_all(value, axes, split_axis=0, concat_axis=0, tiled=True)  22.6 us
    all_to_all x2, starting transfers between devices, all_to_all(): return lax.all_to_all(value, axes, split_axis=0, concat_axis=0, tiled=True)  14.4 us
    all_gather x1, waiting for transfers between devices, local(): near_act = lax.all_gather(activated, ('z', 'c'), axis=0, tiled=True)  14.3 us
    ppermute x3, waiting for transfers between devices, local(): blocks1.append(lax.ppermute(items, 'y', along_y[dy]))  11.7 us
  transfers between devices with their start and end apart: 17, of which 13 were waited for; matrix products, arithmetic and copies ran while one was open for 5% of the time, Pallas kernels for 11%

profile of v6, /device:TPU:1, one launch (start us, length us, event | category | flops | bytes accessed | tf_op | source)
XLA Modules:
  0.0 346.8 jit_solution(17958061152609338208)
XLA Ops:
  8.0 7.3 %pack.1 = (bf16[4112,128]{1,0:T(8,128)(2,1)S(1)}, bf16[4112,128]{1,0:T(8,128)(2,1)S(1)}, bf16[4112,128]{1,0:T(8,128)(2,1)S(1)}, bf16[4112,128]{1,0:T(8,128)(2,1)S(1)}, bf16[16,1040,128]{2,1,0:T(8,128)(2,1)}) custom-call(s32[578]{0:T(1024)S(1)} %concatenate.8.index_ref, bf16[96,128,128]{2,1,0:T(8,128)(2,1)} %rest_0_.1, bf16[96,128,128]{2,1,0:T(8,128)(2,1)} %rest_1_.1), custom_call_target="tpu_custom_call" | custom-call | bytes 16777216 | tf_op jit(solution)/shard_map/pack/pallas_call | solution.py:81
  16.4 10.1 %all-to-all-start = ((bf16[16,1040,128]{2,1,0:T(8,128)(2,1)}), bf16[16,1040,128]{2,1,0:T(8,128)(2,1)}, u32[]{:S(2)}, u32[]{:S(2)}) async-start(bf16[16,1040,128]{2,1,0:T(8,128)(2,1)} %get-tuple-element.28), calls=%async_computation | async-start | bytes 8519680 | tf_op jit(solution)/shard_map/all_to_all | solution.py:193
  34.4 18.6 %collective-permute-done.rest_1_ = bf16[4112,128]{1,0:T(8,128)(2,1)S(1)} collective-permute-done((bf16[4112,128]{1,0:T(8,128)(2,1)}, bf16[4112,128]{1,0:T(8,128)(2,1)S(1)}, u32[]{:S(2)}, u32[]{:S(2)}) %collective-permute-start) | collective-permute-done | bytes 1052704 | tf_op jit(solution)/shard_map/ppermute | solution.py:242
  53.0 23.6 %collective-permute-done.1.rest_2_ = bf16[4112,128]{1,0:T(8,128)(2,1)S(1)} collective-permute-done((bf16[4112,128]{1,0:T(8,128)(2,1)S(1)}, bf16[4112,128]{1,0:T(8,128)(2,1)S(1)}, u32[]{:S(2)}, u32[]{:S(2)}) %collective-permute-start.1) | collective-permute-done | bytes 1052704 | tf_op jit(solution)/shard_map/ppermute | solution.py:242
  76.7 5.6 %collective-permute-done.4 = bf16[512,256]{1,0:T(8,128)(2,1)S(1)} collective-permute-done((bf16[512,256]{1,0:T(8,128)(2,1)S(1)}, bf16[512,256]{1,0:T(8,128)(2,1)S(1)}, u32[]{:S(2)}, u32[]{:S(2)}) %collective-permute-start.4) | collective-permute-done | bytes 262176 | tf_op jit(solution)/shard_map/ppermute | solution.py:241
  82.3 4.8 %collective-permute-done.5 = bf16[512,256]{1,0:T(8,128)(2,1)S(1)} collective-permute-done((bf16[512,256]{1,0:T(8,128)(2,1)S(1)}, bf16[512,256]{1,0:T(8,128)(2,1)S(1)}, u32[]{:S(2)}, u32[]{:S(2)}) %collective-permute-start.5) | collective-permute-done | bytes 262176 | tf_op jit(solution)/shard_map/ppermute | solution.py:241
  88.4 11.9 %products.2 = (f32[32,128,256]{2,1,0:T(8,128)}, bf16[32,128,256]{2,1,0:T(8,128)(2,1)}) custom-call(s32[128]{0:T(128)S(1)} %maximum_convert_fusion.lab_ref, s32[4]{0:T(128)S(1)} %iota_multiply_fusion.1.base_ref, s32[1]{0:T(128)} %constant.85.clone.1.order_ref, bf16[4112,128]{1,0:T(8,128)(2,1)S(1)} %get-tuple-element.33.rest_0_, ...), custom_call_target="tpu_custom_call" | custom-call | flops 1073741824 | bytes 12582912 | tf_op jit(solution)/shard_map/products/pallas_call | solution.py:172
  100.7 4.0 %collective-permute-done.6 = bf16[32,128,256]{2,1,0:T(8,128)(2,1)S(1)} collective-permute-done((bf16[32,128,256]{2,1,0:T(8,128)(2,1)}, bf16[32,128,256]{2,1,0:T(8,128)(2,1)S(1)}, u32[]{:S(2)}, u32[]{:S(2)}) %collective-permute-start.6) | collective-permute-done | bytes 2097184 | tf_op jit(solution)/shard_map/ppermute | solution.py:255
  104.7 5.0 %convert_add_fusion.1 = f32[32,128,256]{2,1,0:T(8,128)} fusion(f32[32,128,256]{2,1,0:T(8,128)} %get-tuple-element.37, bf16[32,128,256]{2,1,0:T(8,128)(2,1)S(1)} %collective-permute-done.6), kind=kLoop, calls=%fused_computation.2 | loop fusion | flops 2097152 | bytes 10485760 | tf_op jit(solution)/shard_map/add | solution.py:256
  109.7 11.7 %all-to-all-done.rest_0_ = bf16[16,1040,128]{2,1,0:T(8,128)(2,1)} async-done(((bf16[16,1040,128]{2,1,0:T(8,128)(2,1)}), bf16[16,1040,128]{2,1,0:T(8,128)(2,1)}, u32[]{:S(2)}, u32[]{:S(2)}) %all-to-all-start) | async-done | bytes 4259872 | tf_op jit(solution)/shard_map/all_to_all | solution.py:193
  123.3 2.6 collective-permute-start.8
  127.1 20.2 %collective-permute-done.7 = bf16[2048,256]{1,0:T(8,128)(2,1)S(1)} collective-permute-done((bf16[2048,256]{1,0:T(8,128)(2,1)S(1)}, bf16[2048,256]{1,0:T(8,128)(2,1)S(1)}, u32[]{:S(2)}, u32[]{:S(2)}) %collective-permute-start.7) | collective-permute-done | bytes 1048608 | tf_op jit(solution)/shard_map/ppermute | solution.py:248
  147.3 23.5 %collective-permute-done.8 = bf16[2048,256]{1,0:T(8,128)(2,1)S(1)} collective-permute-done((bf16[2048,256]{1,0:T(8,128)(2,1)S(1)}, bf16[2048,256]{1,0:T(8,128)(2,1)S(1)}, u32[]{:S(2)}, u32[]{:S(2)}) %collective-permute-start.8) | collective-permute-done | bytes 1048608 | tf_op jit(solution)/shard_map/ppermute | solution.py:248
  170.7 5.6 %reduce-scatter.3.cloned.1.call-done = f32[512,256]{1,0:T(8,128)} async-done(((f32[4096,256]{1,0:T(8,128)}), f32[512,256]{1,0:T(8,128)}) %reduce-scatter.3.cloned.1.call-update) | async-done | bytes 524304 | tf_op jit(solution)/shard_map/reduce_scatter | solution.py:258
  181.1 14.9 %back_products.1 = (f32[32,128,256]{2,1,0:T(8,128)}, bf16[32,128,256]{2,1,0:T(8,128)(2,1)}) custom-call(s32[128]{0:T(128)S(1)} %reshape.79.lab_ref, s32[16]{0:T(128)S(1)} %fusion.2.base_ref, s32[64]{0:T(128)S(1)} %fusion.order_ref, bf16[16,1040,128]{2,1,0:T(8,128)(2,1)} %all-to-all-done.rest_0_, bf16[16,128,256]{2,1,0:T(8,128)(2,1)S(1)} %bitcast.35, ...), custom_call_target="tpu_custom_call" | custom-call | flops 1073741824 | bytes 12582912 | tf_op jit(solution)/shard_map/back_products/pallas_call | solution.py:172
  196.7 4.0 %collective-permute-done.10 = bf16[32,128,256]{2,1,0:T(8,128)(2,1)S(1)} collective-permute-done((bf16[32,128,256]{2,1,0:T(8,128)(2,1)}, bf16[32,128,256]{2,1,0:T(8,128)(2,1)S(1)}, u32[]{:S(2)}, u32[]{:S(2)}) %collective-permute-start.10) | collective-permute-done | bytes 2097184 | tf_op jit(solution)/shard_map/ppermute | solution.py:271
  200.7 5.0 %convert_add_fusion = f32[32,128,256]{2,1,0:T(8,128)} fusion(f32[32,128,256]{2,1,0:T(8,128)} %get-tuple-element.48, bf16[32,128,256]{2,1,0:T(8,128)(2,1)S(1)} %collective-permute-done.10), kind=kLoop, calls=%fused_computation.1 | loop fusion | flops 2097152 | bytes 10485760 | tf_op jit(solution)/shard_map/add | solution.py:272
  205.7 14.3 %all-gather.3.cloned.1.call-done = bf16[8192,256]{1,0:T(8,128)(2,1)} async-done(((bf16[512,256]{1,0:T(8,128)(2,1)}), bf16[8192,256]{1,0:T(8,128)(2,1)}) %all-gather.3.cloned.1.call-update) | async-done | bytes 4194320 | tf_op jit(solution)/shard_map/all_gather | solution.py:263
  220.1 11.9 %products.3 = bf16[64,128,256]{2,1,0:T(8,128)(2,1)S(1)} custom-call(s32[128]{0:T(128)S(1)} %reshape.79.lab_ref, s32[16]{0:T(128)S(1)} %iota_multiply_fusion.base_ref, s32[1]{0:T(128)} %constant.85.clone.1.order_ref, bf16[16,1040,128]{2,1,0:T(8,128)(2,1)} %all-to-all-done.rest_0_, bf16[64,128,256]{2,1,0:T(8,128)(2,1)} %bitcast.44), custom_call_target="tpu_custom_call" | custom-call | flops 1073741824 | bytes 12582912 | tf_op jit(solution)/shard_map/products/pallas_call | solution.py:172
  232.1 56.5 %all_to_all.25 = bf16[16,512,256]{2,1,0:T(8,128)(2,1)S(1)} all-to-all(bf16[16,512,256]{2,1,0:T(8,128)(2,1)S(1)} %bitcast.34), channel_id=1, replica_groups=mesh['y'=4,'z'=8,'c'=2,'x'=4] {'y','x'}, dimensions={0} | all-to-all | bytes 8388608 | tf_op jit(solution)/shard_map/all_to_all | solution.py:193
  291.5 17.6 %all_to_all.26 = f32[16,16,256]{2,1,0:T(8,128)S(1)} all-to-all(f32[16,16,256]{2,1,0:T(8,128)S(1)} %bitcast.45), channel_id=1, replica_groups=mesh['y'=4,'z'=8,'c'=2,'x'=4] {'z','c'}, dimensions={0} | all-to-all | bytes 524288 | tf_op jit(solution)/shard_map/all_to_all | solution.py:193
  309.2 11.3 %all_to_all.27 = f32[16,16,256]{2,1,0:T(8,128)S(1)} all-to-all(f32[16,16,256]{2,1,0:T(8,128)S(1)} %broadcast_in_dim.4), channel_id=1, replica_groups=mesh['y'=4,'z'=8,'c'=2,'x'=4] {'y','x'}, dimensions={0} | all-to-all | bytes 524288 | tf_op jit(solution)/shard_map/all_to_all | solution.py:193
  321.2 4.3 %all-to-all-start.4 = ((f32[16,16,256]{2,1,0:T(8,128)}), f32[16,16,256]{2,1,0:T(8,128)S(1)}, u32[]{:S(2)}, u32[]{:S(2)}) async-start(f32[16,16,256]{2,1,0:T(8,128)} %broadcast_in_dim.10), calls=%async_computation.6 | async-start | bytes 524288 | tf_op jit(solution)/shard_map/all_to_all | solution.py:193
  326.5 10.9 %all-to-all-done.4 = f32[16,16,256]{2,1,0:T(8,128)S(1)} async-done(((f32[16,16,256]{2,1,0:T(8,128)}), f32[16,16,256]{2,1,0:T(8,128)S(1)}, u32[]{:S(2)}, u32[]{:S(2)}) %all-to-all-start.4) | async-done | bytes 262176 | tf_op jit(solution)/shard_map/all_to_all | solution.py:193
  (64 shorter events, 27.7 us)
Async XLA Ops:
  7.2 170.4 %copy-start = (bf16[256,256]{1,0:T(8,128)(2,1)S(1)}, bf16[256,256]{1,0:T(8,128)(2,1)}, u32[]{:S(2)}) copy-start(bf16[256,256]{1,0:T(8,128)(2,1)} %param.22) | copy-start | bytes 393220
  15.3 1.0 copy-start.2
  16.4 15.2 %copy-start.1 = (bf16[512,256]{1,0:T(8,128)(2,1)S(1)}, bf16[512,256]{1,0:T(8,128)(2,1)}, u32[]{:S(2)}) copy-start(bf16[512,256]{1,0:T(8,128)(2,1)} %param.13) | copy-start | bytes 786436
  16.4 105.1 %all-to-all-start = ((bf16[16,1040,128]{2,1,0:T(8,128)(2,1)}), bf16[16,1040,128]{2,1,0:T(8,128)(2,1)}, u32[]{:S(2)}, u32[]{:S(2)}) async-start(bf16[16,1040,128]{2,1,0:T(8,128)(2,1)} %get-tuple-element.28), calls=%async_computation | async-start | bytes 8519680 | tf_op jit(solution)/shard_map/all_to_all | solution.py:193
  26.5 149.9 %reduce-scatter.3.cloned.1.call-start = ((), (), s32[]{:S(2)}) async-start(), calls=%async_computation.7 | async-start | bytes 4718592 | tf_op jit(solution)/shard_map/reduce_scatter | solution.py:258
  26.5 26.4 %collective-permute-start = (bf16[4112,128]{1,0:T(8,128)(2,1)}, bf16[4112,128]{1,0:T(8,128)(2,1)S(1)}, u32[]{:S(2)}, u32[]{:S(2)}) collective-permute-start(bf16[4112,128]{1,0:T(8,128)(2,1)} %copy-done.2), channel_id=1, source_target_pairs={{0,64},{64,128},{128,192},{192,0},{1,65},{65,129},{129,193},{193,1... | collective-permute-start | bytes 3158024 | tf_op jit(solution)/shard_map/ppermute | solution.py:242
  27.9 48.7 %collective-permute-start.1 = (bf16[4112,128]{1,0:T(8,128)(2,1)S(1)}, bf16[4112,128]{1,0:T(8,128)(2,1)S(1)}, u32[]{:S(2)}, u32[]{:S(2)}) collective-permute-start(bf16[4112,128]{1,0:T(8,128)(2,1)S(1)} %get-tuple-element.31), channel_id=1, source_target_pairs={{0,128},{64,192},{128,0},{192,64},{1,129},{65,193},{129,1},{193,65... | collective-permute-start | bytes 3158024 | tf_op jit(solution)/shard_map/ppermute | solution.py:242
  30.5 46.0 %collective-permute-start.2 = (bf16[4112,128]{1,0:T(8,128)(2,1)S(1)}, bf16[4112,128]{1,0:T(8,128)(2,1)S(1)}, u32[]{:S(2)}, u32[]{:S(2)}) collective-permute-start(bf16[4112,128]{1,0:T(8,128)(2,1)S(1)} %get-tuple-element.32), channel_id=1, source_target_pairs={{0,192},{64,0},{128,64},{192,128},{1,193},{65,1},{129,65},{193,129... | collective-permute-start | bytes 3158024 | tf_op jit(solution)/shard_map/ppermute | solution.py:242
  31.6 50.7 %collective-permute-start.4 = (bf16[512,256]{1,0:T(8,128)(2,1)S(1)}, bf16[512,256]{1,0:T(8,128)(2,1)S(1)}, u32[]{:S(2)}, u32[]{:S(2)}) collective-permute-start(bf16[512,256]{1,0:T(8,128)(2,1)S(1)} %copy-done.1), channel_id=1, source_target_pairs={{0,128},{64,192},{128,0},{192,64},{1,129},{65,193},{129,1},{193,65... | collective-permute-start | bytes 786440 | tf_op jit(solution)/shard_map/ppermute | solution.py:241
  31.8 55.3 %collective-permute-start.5 = (bf16[512,256]{1,0:T(8,128)(2,1)S(1)}, bf16[512,256]{1,0:T(8,128)(2,1)S(1)}, u32[]{:S(2)}, u32[]{:S(2)}) collective-permute-start(bf16[512,256]{1,0:T(8,128)(2,1)S(1)} %copy-done.1), channel_id=1, source_target_pairs={{0,192},{64,0},{128,64},{192,128},{1,193},{65,1},{129,65},{193,129... | collective-permute-start | bytes 786440 | tf_op jit(solution)/shard_map/ppermute | solution.py:241
  53.0 35.4 %collective-permute-start.3 = (bf16[512,256]{1,0:T(8,128)(2,1)S(1)}, bf16[512,256]{1,0:T(8,128)(2,1)S(1)}, u32[]{:S(2)}, u32[]{:S(2)}) collective-permute-start(bf16[512,256]{1,0:T(8,128)(2,1)S(1)} %copy-done.1), channel_id=1, source_target_pairs={{0,64},{64,128},{128,192},{192,0},{1,65},{65,129},{129,193},{193,1... | collective-permute-start | bytes 786440 | tf_op jit(solution)/shard_map/ppermute | solution.py:241
  100.3 4.5 %collective-permute-start.6 = (bf16[32,128,256]{2,1,0:T(8,128)(2,1)}, bf16[32,128,256]{2,1,0:T(8,128)(2,1)S(1)}, u32[]{:S(2)}, u32[]{:S(2)}) collective-permute-start(bf16[32,128,256]{2,1,0:T(8,128)(2,1)} %get-tuple-element.38), channel_id=1, source_target_pairs={{0,4},{4,0},{1,5},{5,1},{2,6},{6,2},{3,7},{7,3},{8,12},{12,8},{9,1... | collective-permute-start | bytes 6291464 | tf_op jit(solution)/shard_map/ppermute | solution.py:255
  109.7 11.8 %copy-start.5 = (s32[2048]{0:T(1024)S(1)}, s32[2048]{0:T(1024)}, u32[]{:S(2)}) copy-start(s32[2048]{0:T(1024)} %param.24) | copy-start | bytes 24580
  109.7 11.8 %copy-start.3 = (bf16[2048,256]{1,0:T(8,128)(2,1)S(1)}, bf16[2048,256]{1,0:T(8,128)(2,1)}, u32[]{:S(2)}) copy-start(bf16[2048,256]{1,0:T(8,128)(2,1)} %param.25) | copy-start | bytes 3145732
  121.5 5.5 %copy-start.6 = (s32[512]{0:T(512)S(1)}, s32[512]{0:T(512)}, u32[]{:S(2)}) copy-start(s32[512]{0:T(512)} %param.23) | copy-start | bytes 6148
  121.5 98.5 %all-gather.3.cloned.1.call-start = ((), (), s32[]{:S(2)}) async-start(), calls=%async_computation.8 | async-start | bytes 4456448 | tf_op jit(solution)/shard_map/all_gather | solution.py:263
  121.9 25.3 %collective-permute-start.7 = (bf16[2048,256]{1,0:T(8,128)(2,1)S(1)}, bf16[2048,256]{1,0:T(8,128)(2,1)S(1)}, u32[]{:S(2)}, u32[]{:S(2)}) collective-permute-start(bf16[2048,256]{1,0:T(8,128)(2,1)S(1)} %divide_convert_fusion), channel_id=1, source_target_pairs={{0,64},{64,128},{128,192},{192,0},{1,65},{65,129},{129,193},{193,1... | collective-permute-start | bytes 3145736 | tf_op jit(solution)/shard_map/ppermute | solution.py:248
  123.3 47.4 %collective-permute-start.8 = (bf16[2048,256]{1,0:T(8,128)(2,1)S(1)}, bf16[2048,256]{1,0:T(8,128)(2,1)S(1)}, u32[]{:S(2)}, u32[]{:S(2)}) collective-permute-start(bf16[2048,256]{1,0:T(8,128)(2,1)S(1)} %divide_convert_fusion), channel_id=1, source_target_pairs={{0,128},{64,192},{128,0},{192,64},{1,129},{65,193},{129,1},{193,65... | collective-permute-start | bytes 3145736 | tf_op jit(solution)/shard_map/ppermute | solution.py:248
  125.9 44.8 %collective-permute-start.9 = (bf16[2048,256]{1,0:T(8,128)(2,1)S(1)}, bf16[2048,256]{1,0:T(8,128)(2,1)}, u32[]{:S(2)}, u32[]{:S(2)}) collective-permute-start(bf16[2048,256]{1,0:T(8,128)(2,1)S(1)} %divide_convert_fusion), channel_id=1, source_target_pairs={{0,192},{64,0},{128,64},{192,128},{1,193},{65,1},{129,65},{193,129... | collective-permute-start | bytes 3145736 | tf_op jit(solution)/shard_map/ppermute | solution.py:248
  178.7 111.3 %reduce-scatter.5.cloned.1.call-start = ((), (), s32[]{:S(2)}) async-start(), calls=%async_computation.10 | async-start | bytes 4718592 | tf_op jit(solution)/shard_map/reduce_scatter | solution.py:274
  196.0 4.7 %collective-permute-start.10 = (bf16[32,128,256]{2,1,0:T(8,128)(2,1)}, bf16[32,128,256]{2,1,0:T(8,128)(2,1)S(1)}, u32[]{:S(2)}, u32[]{:S(2)}) collective-permute-start(bf16[32,128,256]{2,1,0:T(8,128)(2,1)} %get-tuple-element.49), channel_id=1, source_target_pairs={{0,4},{4,0},{1,5},{5,1},{2,6},{6,2},{3,7},{7,3},{8,12},{12,8},{9,1... | collective-permute-start | bytes 6291464 | tf_op jit(solution)/shard_map/ppermute | solution.py:271
  220.1 105.4 %all-gather.5.cloned.1.call-start = ((), (), s32[]{:S(2)}) async-start(), calls=%async_computation.9 | async-start | bytes 1310720 | tf_op jit(solution)/shard_map/all_gather | solution.py:290
  288.5 1.5 copy-start.4
  321.2 16.1 %all-to-all-start.4 = ((f32[16,16,256]{2,1,0:T(8,128)}), f32[16,16,256]{2,1,0:T(8,128)S(1)}, u32[]{:S(2)}, u32[]{:S(2)}) async-start(f32[16,16,256]{2,1,0:T(8,128)} %broadcast_in_dim.10), calls=%async_computation.6 | async-start | bytes 524288 | tf_op jit(solution)/shard_map/all_to_all | solution.py:193
Sparse Core Ops, SparseCore 0:
  121.6 54.7 reduce-scatter.2
  178.8 41.1 all-gather.2
  222.6 53.5 reduce-scatter.4
  290.1 21.5 all-gather.4

commit v7 on v6

--- a/solution.py
+++ b/solution.py
@@ -156,7 +156,7 @@
                 return carry
 
             tile_loads[g].wait()
-            lax.fori_loop(0, cap, step, 0, unroll=4)
+            lax.fori_loop(0, cap, step, 0, unroll=8)
         at = 0
         if split_out > 0:
             outs[at][...] = acc[0:split_out]

time: 348 us -> 345 us (level)
  Pallas kernels: 46 us -> 37.7 us
  waiting for transfers between devices: 148 us -> 154 us
    pallas_call x3, Pallas kernels: 38.7 us -> 30.4 us  [products(): pl.pallas_call(kernel, out_shape=out_shape, in_specs=[SMEM_SPEC, SMEM_SPE...]
  transfers between devices with their start and end apart: 17 -> 17, of which waited for: 13 -> 13; matrix products, arithmetic and copies ran while one was open for 5% -> 5% of each run, Pallas kernels for 11% -> 9%
where the time goes in v7:
time: 345 us; the launch traced here: 344 us
  waiting for transfers between devices  154 us (45%)
  blocking collectives  85.2 us (25%)
  Pallas kernels  37.7 us (11%)
  starting transfers between devices  29.1 us (8%)
  other arithmetic  15.8 us (5%)
  between operations  14 us (4%)
  local copies, waits for them, and re-layouts  6.42 us (2%)
    all_to_all x3, blocking collectives, all_to_all(): return lax.all_to_all(value, axes, split_axis=0, concat_axis=0, tiled=True)  85.2 us
    ppermute x3, waiting for transfers between devices, local(): lax.ppermute(scaled_grad, 'y', along_y[dy])  43.7 us
    ppermute x3, waiting for transfers between devices, local(): got1.append(lax.ppermute(send1[dy], 'y', along_y[dy]))  42.2 us
    pallas_call x3, Pallas kernels, products(): pl.pallas_call(kernel, out_shape=out_shape, in_specs=[SMEM_SPEC, SMEM_SPE...  30.4 us
    all_to_all x2, waiting for transfers between devices, all_to_all(): return lax.all_to_all(value, axes, split_axis=0, concat_axis=0, tiled=True)  25.2 us
    all_gather x1, waiting for transfers between devices, local(): near_act = lax.all_gather(activated, ('z', 'c'), axis=0, tiled=True)  17.4 us
    all_to_all x2, starting transfers between devices, all_to_all(): return lax.all_to_all(value, axes, split_axis=0, concat_axis=0, tiled=True)  14.4 us
    ppermute x3, waiting for transfers between devices, local(): blocks1.append(lax.ppermute(items, 'y', along_y[dy]))  11.7 us
  transfers between devices with their start and end apart: 17, of which 13 were waited for; matrix products, arithmetic and copies ran while one was open for 5% of the time, Pallas kernels for 9%

profile of v7, /device:TPU:1, one launch (start us, length us, event | category | flops | bytes accessed | tf_op | source)
XLA Modules:
  0.0 344.3 jit_solution(13636528056776133426)
XLA Ops:
  8.0 7.3 %pack.1 = (bf16[4112,128]{1,0:T(8,128)(2,1)S(1)}, bf16[4112,128]{1,0:T(8,128)(2,1)S(1)}, bf16[4112,128]{1,0:T(8,128)(2,1)S(1)}, bf16[4112,128]{1,0:T(8,128)(2,1)S(1)}, bf16[16,1040,128]{2,1,0:T(8,128)(2,1)}) custom-call(s32[578]{0:T(1024)S(1)} %concatenate.8.index_ref, bf16[96,128,128]{2,1,0:T(8,128)(2,1)} %rest_0_.1, bf16[96,128,128]{2,1,0:T(8,128)(2,1)} %rest_1_.1), custom_call_target="tpu_custom_call" | custom-call | bytes 16777216 | tf_op jit(solution)/shard_map/pack/pallas_call | solution.py:81
  16.4 10.1 %all-to-all-start = ((bf16[16,1040,128]{2,1,0:T(8,128)(2,1)}), bf16[16,1040,128]{2,1,0:T(8,128)(2,1)}, u32[]{:S(2)}, u32[]{:S(2)}) async-start(bf16[16,1040,128]{2,1,0:T(8,128)(2,1)} %get-tuple-element.28), calls=%async_computation | async-start | bytes 8519680 | tf_op jit(solution)/shard_map/all_to_all | solution.py:193
  34.4 18.6 %collective-permute-done.rest_1_ = bf16[4112,128]{1,0:T(8,128)(2,1)S(1)} collective-permute-done((bf16[4112,128]{1,0:T(8,128)(2,1)}, bf16[4112,128]{1,0:T(8,128)(2,1)S(1)}, u32[]{:S(2)}, u32[]{:S(2)}) %collective-permute-start) | collective-permute-done | bytes 1052704 | tf_op jit(solution)/shard_map/ppermute | solution.py:242
  53.0 23.6 %collective-permute-done.1.rest_2_ = bf16[4112,128]{1,0:T(8,128)(2,1)S(1)} collective-permute-done((bf16[4112,128]{1,0:T(8,128)(2,1)S(1)}, bf16[4112,128]{1,0:T(8,128)(2,1)S(1)}, u32[]{:S(2)}, u32[]{:S(2)}) %collective-permute-start.1) | collective-permute-done | bytes 1052704 | tf_op jit(solution)/shard_map/ppermute | solution.py:242
  76.7 5.6 %collective-permute-done.4 = bf16[512,256]{1,0:T(8,128)(2,1)S(1)} collective-permute-done((bf16[512,256]{1,0:T(8,128)(2,1)S(1)}, bf16[512,256]{1,0:T(8,128)(2,1)S(1)}, u32[]{:S(2)}, u32[]{:S(2)}) %collective-permute-start.4) | collective-permute-done | bytes 262176 | tf_op jit(solution)/shard_map/ppermute | solution.py:241
  82.3 4.8 %collective-permute-done.5 = bf16[512,256]{1,0:T(8,128)(2,1)S(1)} collective-permute-done((bf16[512,256]{1,0:T(8,128)(2,1)S(1)}, bf16[512,256]{1,0:T(8,128)(2,1)S(1)}, u32[]{:S(2)}, u32[]{:S(2)}) %collective-permute-start.5) | collective-permute-done | bytes 262176 | tf_op jit(solution)/shard_map/ppermute | solution.py:241
  88.4 9.3 %products.2 = (f32[32,128,256]{2,1,0:T(8,128)}, bf16[32,128,256]{2,1,0:T(8,128)(2,1)}) custom-call(s32[128]{0:T(128)S(1)} %maximum_convert_fusion.lab_ref, s32[4]{0:T(128)S(1)} %iota_multiply_fusion.1.base_ref, s32[1]{0:T(128)} %constant.85.clone.1.order_ref, bf16[4112,128]{1,0:T(8,128)(2,1)S(1)} %get-tuple-element.33.rest_0_, ...), custom_call_target="tpu_custom_call" | custom-call | flops 1073741824 | bytes 12582912 | tf_op jit(solution)/shard_map/products/pallas_call | solution.py:172
  98.2 4.0 %collective-permute-done.6 = bf16[32,128,256]{2,1,0:T(8,128)(2,1)S(1)} collective-permute-done((bf16[32,128,256]{2,1,0:T(8,128)(2,1)}, bf16[32,128,256]{2,1,0:T(8,128)(2,1)S(1)}, u32[]{:S(2)}, u32[]{:S(2)}) %collective-permute-start.6) | collective-permute-done | bytes 2097184 | tf_op jit(solution)/shard_map/ppermute | solution.py:255
  102.2 5.0 %convert_add_fusion.1 = f32[32,128,256]{2,1,0:T(8,128)} fusion(f32[32,128,256]{2,1,0:T(8,128)} %get-tuple-element.37, bf16[32,128,256]{2,1,0:T(8,128)(2,1)S(1)} %collective-permute-done.6), kind=kLoop, calls=%fused_computation.2 | loop fusion | flops 2097152 | bytes 10485760 | tf_op jit(solution)/shard_map/add | solution.py:256
  107.2 14.3 %all-to-all-done.rest_0_ = bf16[16,1040,128]{2,1,0:T(8,128)(2,1)} async-done(((bf16[16,1040,128]{2,1,0:T(8,128)(2,1)}), bf16[16,1040,128]{2,1,0:T(8,128)(2,1)}, u32[]{:S(2)}, u32[]{:S(2)}) %all-to-all-start) | async-done | bytes 4259872 | tf_op jit(solution)/shard_map/all_to_all | solution.py:193
  123.3 2.6 collective-permute-start.8
  127.1 20.2 %collective-permute-done.7 = bf16[2048,256]{1,0:T(8,128)(2,1)S(1)} collective-permute-done((bf16[2048,256]{1,0:T(8,128)(2,1)S(1)}, bf16[2048,256]{1,0:T(8,128)(2,1)S(1)}, u32[]{:S(2)}, u32[]{:S(2)}) %collective-permute-start.7) | collective-permute-done | bytes 1048608 | tf_op jit(solution)/shard_map/ppermute | solution.py:248
  147.3 23.5 %collective-permute-done.8 = bf16[2048,256]{1,0:T(8,128)(2,1)S(1)} collective-permute-done((bf16[2048,256]{1,0:T(8,128)(2,1)S(1)}, bf16[2048,256]{1,0:T(8,128)(2,1)S(1)}, u32[]{:S(2)}, u32[]{:S(2)}) %collective-permute-start.8) | collective-permute-done | bytes 1048608 | tf_op jit(solution)/shard_map/ppermute | solution.py:248
  170.7 5.6 %reduce-scatter.3.cloned.1.call-done = f32[512,256]{1,0:T(8,128)} async-done(((f32[4096,256]{1,0:T(8,128)}), f32[512,256]{1,0:T(8,128)}) %reduce-scatter.3.cloned.1.call-update) | async-done | bytes 524304 | tf_op jit(solution)/shard_map/reduce_scatter | solution.py:258
  181.1 11.7 %back_products.1 = (f32[32,128,256]{2,1,0:T(8,128)}, bf16[32,128,256]{2,1,0:T(8,128)(2,1)}) custom-call(s32[128]{0:T(128)S(1)} %reshape.79.lab_ref, s32[16]{0:T(128)S(1)} %fusion.2.base_ref, s32[64]{0:T(128)S(1)} %fusion.order_ref, bf16[16,1040,128]{2,1,0:T(8,128)(2,1)} %all-to-all-done.rest_0_, bf16[16,128,256]{2,1,0:T(8,128)(2,1)S(1)} %bitcast.35, ...), custom_call_target="tpu_custom_call" | custom-call | flops 1073741824 | bytes 12582912 | tf_op jit(solution)/shard_map/back_products/pallas_call | solution.py:172
  193.6 4.0 %collective-permute-done.10 = bf16[32,128,256]{2,1,0:T(8,128)(2,1)S(1)} collective-permute-done((bf16[32,128,256]{2,1,0:T(8,128)(2,1)}, bf16[32,128,256]{2,1,0:T(8,128)(2,1)S(1)}, u32[]{:S(2)}, u32[]{:S(2)}) %collective-permute-start.10) | collective-permute-done | bytes 2097184 | tf_op jit(solution)/shard_map/ppermute | solution.py:271
  197.6 5.0 %convert_add_fusion = f32[32,128,256]{2,1,0:T(8,128)} fusion(f32[32,128,256]{2,1,0:T(8,128)} %get-tuple-element.48, bf16[32,128,256]{2,1,0:T(8,128)(2,1)S(1)} %collective-permute-done.10), kind=kLoop, calls=%fused_computation.1 | loop fusion | flops 2097152 | bytes 10485760 | tf_op jit(solution)/shard_map/add | solution.py:272
  202.6 17.4 %all-gather.3.cloned.1.call-done = bf16[8192,256]{1,0:T(8,128)(2,1)} async-done(((bf16[512,256]{1,0:T(8,128)(2,1)}), bf16[8192,256]{1,0:T(8,128)(2,1)}) %all-gather.3.cloned.1.call-update) | async-done | bytes 4194320 | tf_op jit(solution)/shard_map/all_gather | solution.py:263
  220.3 9.3 %products.3 = bf16[64,128,256]{2,1,0:T(8,128)(2,1)S(1)} custom-call(s32[128]{0:T(128)S(1)} %reshape.79.lab_ref, s32[16]{0:T(128)S(1)} %iota_multiply_fusion.base_ref, s32[1]{0:T(128)} %constant.85.clone.1.order_ref, bf16[16,1040,128]{2,1,0:T(8,128)(2,1)} %all-to-all-done.rest_0_, bf16[64,128,256]{2,1,0:T(8,128)(2,1)} %bitcast.44), custom_call_target="tpu_custom_call" | custom-call | flops 1073741824 | bytes 12582912 | tf_op jit(solution)/shard_map/products/pallas_call | solution.py:172
  229.6 56.5 %all_to_all.25 = bf16[16,512,256]{2,1,0:T(8,128)(2,1)S(1)} all-to-all(bf16[16,512,256]{2,1,0:T(8,128)(2,1)S(1)} %bitcast.34), channel_id=1, replica_groups=mesh['y'=4,'z'=8,'c'=2,'x'=4] {'y','x'}, dimensions={0} | all-to-all | bytes 8388608 | tf_op jit(solution)/shard_map/all_to_all | solution.py:193
  289.1 17.5 %all_to_all.26 = f32[16,16,256]{2,1,0:T(8,128)S(1)} all-to-all(f32[16,16,256]{2,1,0:T(8,128)S(1)} %bitcast.45), channel_id=1, replica_groups=mesh['y'=4,'z'=8,'c'=2,'x'=4] {'z','c'}, dimensions={0} | all-to-all | bytes 524288 | tf_op jit(solution)/shard_map/all_to_all | solution.py:193
  306.6 11.3 %all_to_all.27 = f32[16,16,256]{2,1,0:T(8,128)S(1)} all-to-all(f32[16,16,256]{2,1,0:T(8,128)S(1)} %broadcast_in_dim.4), channel_id=1, replica_groups=mesh['y'=4,'z'=8,'c'=2,'x'=4] {'y','x'}, dimensions={0} | all-to-all | bytes 524288 | tf_op jit(solution)/shard_map/all_to_all | solution.py:193
  318.6 4.3 %all-to-all-start.4 = ((f32[16,16,256]{2,1,0:T(8,128)}), f32[16,16,256]{2,1,0:T(8,128)S(1)}, u32[]{:S(2)}, u32[]{:S(2)}) async-start(f32[16,16,256]{2,1,0:T(8,128)} %broadcast_in_dim.10), calls=%async_computation.6 | async-start | bytes 524288 | tf_op jit(solution)/shard_map/all_to_all | solution.py:193
  323.9 10.9 %all-to-all-done.4 = f32[16,16,256]{2,1,0:T(8,128)S(1)} async-done(((f32[16,16,256]{2,1,0:T(8,128)}), f32[16,16,256]{2,1,0:T(8,128)S(1)}, u32[]{:S(2)}, u32[]{:S(2)}) %all-to-all-start.4) | async-done | bytes 262176 | tf_op jit(solution)/shard_map/all_to_all | solution.py:193
  (64 shorter events, 27.9 us)
Async XLA Ops:
  7.2 170.4 %copy-start = (bf16[256,256]{1,0:T(8,128)(2,1)S(1)}, bf16[256,256]{1,0:T(8,128)(2,1)}, u32[]{:S(2)}) copy-start(bf16[256,256]{1,0:T(8,128)(2,1)} %param.22) | copy-start | bytes 393220
  15.3 1.0 copy-start.2
  16.4 15.2 %copy-start.1 = (bf16[512,256]{1,0:T(8,128)(2,1)S(1)}, bf16[512,256]{1,0:T(8,128)(2,1)}, u32[]{:S(2)}) copy-start(bf16[512,256]{1,0:T(8,128)(2,1)} %param.13) | copy-start | bytes 786436
  16.4 105.1 %all-to-all-start = ((bf16[16,1040,128]{2,1,0:T(8,128)(2,1)}), bf16[16,1040,128]{2,1,0:T(8,128)(2,1)}, u32[]{:S(2)}, u32[]{:S(2)}) async-start(bf16[16,1040,128]{2,1,0:T(8,128)(2,1)} %get-tuple-element.28), calls=%async_computation | async-start | bytes 8519680 | tf_op jit(solution)/shard_map/all_to_all | solution.py:193
  26.5 149.9 %reduce-scatter.3.cloned.1.call-start = ((), (), s32[]{:S(2)}) async-start(), calls=%async_computation.7 | async-start | bytes 4718592 | tf_op jit(solution)/shard_map/reduce_scatter | solution.py:258
  26.5 26.4 %collective-permute-start = (bf16[4112,128]{1,0:T(8,128)(2,1)}, bf16[4112,128]{1,0:T(8,128)(2,1)S(1)}, u32[]{:S(2)}, u32[]{:S(2)}) collective-permute-start(bf16[4112,128]{1,0:T(8,128)(2,1)} %copy-done.2), channel_id=1, source_target_pairs={{0,64},{64,128},{128,192},{192,0},{1,65},{65,129},{129,193},{193,1... | collective-permute-start | bytes 3158024 | tf_op jit(solution)/shard_map/ppermute | solution.py:242
  27.9 48.7 %collective-permute-start.1 = (bf16[4112,128]{1,0:T(8,128)(2,1)S(1)}, bf16[4112,128]{1,0:T(8,128)(2,1)S(1)}, u32[]{:S(2)}, u32[]{:S(2)}) collective-permute-start(bf16[4112,128]{1,0:T(8,128)(2,1)S(1)} %get-tuple-element.31), channel_id=1, source_target_pairs={{0,128},{64,192},{128,0},{192,64},{1,129},{65,193},{129,1},{193,65... | collective-permute-start | bytes 3158024 | tf_op jit(solution)/shard_map/ppermute | solution.py:242
  30.5 46.0 %collective-permute-start.2 = (bf16[4112,128]{1,0:T(8,128)(2,1)S(1)}, bf16[4112,128]{1,0:T(8,128)(2,1)S(1)}, u32[]{:S(2)}, u32[]{:S(2)}) collective-permute-start(bf16[4112,128]{1,0:T(8,128)(2,1)S(1)} %get-tuple-element.32), channel_id=1, source_target_pairs={{0,192},{64,0},{128,64},{192,128},{1,193},{65,1},{129,65},{193,129... | collective-permute-start | bytes 3158024 | tf_op jit(solution)/shard_map/ppermute | solution.py:242
  31.6 50.7 %collective-permute-start.4 = (bf16[512,256]{1,0:T(8,128)(2,1)S(1)}, bf16[512,256]{1,0:T(8,128)(2,1)S(1)}, u32[]{:S(2)}, u32[]{:S(2)}) collective-permute-start(bf16[512,256]{1,0:T(8,128)(2,1)S(1)} %copy-done.1), channel_id=1, source_target_pairs={{0,128},{64,192},{128,0},{192,64},{1,129},{65,193},{129,1},{193,65... | collective-permute-start | bytes 786440 | tf_op jit(solution)/shard_map/ppermute | solution.py:241
  31.8 55.3 %collective-permute-start.5 = (bf16[512,256]{1,0:T(8,128)(2,1)S(1)}, bf16[512,256]{1,0:T(8,128)(2,1)S(1)}, u32[]{:S(2)}, u32[]{:S(2)}) collective-permute-start(bf16[512,256]{1,0:T(8,128)(2,1)S(1)} %copy-done.1), channel_id=1, source_target_pairs={{0,192},{64,0},{128,64},{192,128},{1,193},{65,1},{129,65},{193,129... | collective-permute-start | bytes 786440 | tf_op jit(solution)/shard_map/ppermute | solution.py:241
  53.0 35.4 %collective-permute-start.3 = (bf16[512,256]{1,0:T(8,128)(2,1)S(1)}, bf16[512,256]{1,0:T(8,128)(2,1)S(1)}, u32[]{:S(2)}, u32[]{:S(2)}) collective-permute-start(bf16[512,256]{1,0:T(8,128)(2,1)S(1)} %copy-done.1), channel_id=1, source_target_pairs={{0,64},{64,128},{128,192},{192,0},{1,65},{65,129},{129,193},{193,1... | collective-permute-start | bytes 786440 | tf_op jit(solution)/shard_map/ppermute | solution.py:241
  97.7 4.5 %collective-permute-start.6 = (bf16[32,128,256]{2,1,0:T(8,128)(2,1)}, bf16[32,128,256]{2,1,0:T(8,128)(2,1)S(1)}, u32[]{:S(2)}, u32[]{:S(2)}) collective-permute-start(bf16[32,128,256]{2,1,0:T(8,128)(2,1)} %get-tuple-element.38), channel_id=1, source_target_pairs={{0,4},{4,0},{1,5},{5,1},{2,6},{6,2},{3,7},{7,3},{8,12},{12,8},{9,1... | collective-permute-start | bytes 6291464 | tf_op jit(solution)/shard_map/ppermute | solution.py:255
  107.2 14.4 %copy-start.5 = (s32[2048]{0:T(1024)S(1)}, s32[2048]{0:T(1024)}, u32[]{:S(2)}) copy-start(s32[2048]{0:T(1024)} %param.24) | copy-start | bytes 24580
  107.2 14.4 %copy-start.3 = (bf16[2048,256]{1,0:T(8,128)(2,1)S(1)}, bf16[2048,256]{1,0:T(8,128)(2,1)}, u32[]{:S(2)}) copy-start(bf16[2048,256]{1,0:T(8,128)(2,1)} %param.25) | copy-start | bytes 3145732
  121.5 5.5 %copy-start.6 = (s32[512]{0:T(512)S(1)}, s32[512]{0:T(512)}, u32[]{:S(2)}) copy-start(s32[512]{0:T(512)} %param.23) | copy-start | bytes 6148
  121.5 98.5 %all-gather.3.cloned.1.call-start = ((), (), s32[]{:S(2)}) async-start(), calls=%async_computation.8 | async-start | bytes 4456448 | tf_op jit(solution)/shard_map/all_gather | solution.py:263
  121.9 25.3 %collective-permute-start.7 = (bf16[2048,256]{1,0:T(8,128)(2,1)S(1)}, bf16[2048,256]{1,0:T(8,128)(2,1)S(1)}, u32[]{:S(2)}, u32[]{:S(2)}) collective-permute-start(bf16[2048,256]{1,0:T(8,128)(2,1)S(1)} %divide_convert_fusion), channel_id=1, source_target_pairs={{0,64},{64,128},{128,192},{192,0},{1,65},{65,129},{129,193},{193,1... | collective-permute-start | bytes 3145736 | tf_op jit(solution)/shard_map/ppermute | solution.py:248
  123.3 47.4 %collective-permute-start.8 = (bf16[2048,256]{1,0:T(8,128)(2,1)S(1)}, bf16[2048,256]{1,0:T(8,128)(2,1)S(1)}, u32[]{:S(2)}, u32[]{:S(2)}) collective-permute-start(bf16[2048,256]{1,0:T(8,128)(2,1)S(1)} %divide_convert_fusion), channel_id=1, source_target_pairs={{0,128},{64,192},{128,0},{192,64},{1,129},{65,193},{129,1},{193,65... | collective-permute-start | bytes 3145736 | tf_op jit(solution)/shard_map/ppermute | solution.py:248
  125.9 44.8 %collective-permute-start.9 = (bf16[2048,256]{1,0:T(8,128)(2,1)S(1)}, bf16[2048,256]{1,0:T(8,128)(2,1)}, u32[]{:S(2)}, u32[]{:S(2)}) collective-permute-start(bf16[2048,256]{1,0:T(8,128)(2,1)S(1)} %divide_convert_fusion), channel_id=1, source_target_pairs={{0,192},{64,0},{128,64},{192,128},{1,193},{65,1},{129,65},{193,129... | collective-permute-start | bytes 3145736 | tf_op jit(solution)/shard_map/ppermute | solution.py:248
  178.7 108.9 %reduce-scatter.5.cloned.1.call-start = ((), (), s32[]{:S(2)}) async-start(), calls=%async_computation.10 | async-start | bytes 4718592 | tf_op jit(solution)/shard_map/reduce_scatter | solution.py:274
  192.9 4.7 %collective-permute-start.10 = (bf16[32,128,256]{2,1,0:T(8,128)(2,1)}, bf16[32,128,256]{2,1,0:T(8,128)(2,1)S(1)}, u32[]{:S(2)}, u32[]{:S(2)}) collective-permute-start(bf16[32,128,256]{2,1,0:T(8,128)(2,1)} %get-tuple-element.49), channel_id=1, source_target_pairs={{0,4},{4,0},{1,5},{5,1},{2,6},{6,2},{3,7},{7,3},{8,12},{12,8},{9,1... | collective-permute-start | bytes 6291464 | tf_op jit(solution)/shard_map/ppermute | solution.py:271
  220.0 102.9 %all-gather.5.cloned.1.call-start = ((), (), s32[]{:S(2)}) async-start(), calls=%async_computation.9 | async-start | bytes 1310720 | tf_op jit(solution)/shard_map/all_gather | solution.py:290
  286.1 1.5 copy-start.4
  318.6 16.2 %all-to-all-start.4 = ((f32[16,16,256]{2,1,0:T(8,128)}), f32[16,16,256]{2,1,0:T(8,128)S(1)}, u32[]{:S(2)}, u32[]{:S(2)}) async-start(f32[16,16,256]{2,1,0:T(8,128)} %broadcast_in_dim.10), calls=%async_computation.6 | async-start | bytes 524288 | tf_op jit(solution)/shard_map/all_to_all | solution.py:193
Sparse Core Ops, SparseCore 0:
  121.6 54.7 reduce-scatter.2
  178.8 41.1 all-gather.2
  222.5 53.5 reduce-scatter.4
  287.7 21.3 all-gather.4
